TPU v7x, 32 devices: a whole 2x2x4 slice. The times are simulated.
32 devices in a mesh: groups: 2 (over y), blk: 16 (over z, x, core).
Axes of the slice: x: 2, y: 2, z: 4, core: 2. Of those that a mesh axis runs over, the one named last changes fastest.
Arguments:
- cell_features: bfloat16 [16384, 768], P(('groups', 'blk')), parts along dimension 0, may hold values from -6 to 6
- cell_geometry_rows: float32 [16384], P(('groups', 'blk')), parts along dimension 0, may hold values from -20 to 20
- anchor_token_features: bfloat16 [256, 768], P(('groups', 'blk')), parts along dimension 0, may hold values from -6 to 6
- anchor_geometry_rows: bfloat16 [256], P(('groups', 'blk')), parts along dimension 0, may hold values from -15 to 15
- live_anchor_count: int32 [32], P(('groups', 'blk')), parts along dimension 0, may hold values from 1 to 8, as said below
- inner_face_first: int32 [49152], P(('groups', 'blk')), parts along dimension 0, may hold values from 0 to 511
- inner_face_second: int32 [49152], P(('groups', 'blk')), parts along dimension 0, may hold values from 0 to 511
- inner_face_weight: float32 [49152], P(('groups', 'blk')), parts along dimension 0, may hold values from 0.05 to 0.4
- upper_face_cell: int32 [8192], P(('groups', 'blk')), parts along dimension 0, may hold values from 0 to 511
- lower_face_cell: int32 [8192], P(('groups', 'blk')), parts along dimension 0, may hold values from 0 to 511
- upper_face_weight: bfloat16 [8192], P(('groups', 'blk')), parts along dimension 0, may hold values from 0.049804688 to 0.3984375
- upper_slot_count: int32 [32], P(('groups', 'blk')), parts along dimension 0, may hold values from 0 to 256, as said below
- query_matrix: bfloat16 [768, 768], replicated, may hold values from -0.21875 to 0.21875
- anchor_keyvalue_matrix: bfloat16 [768, 1536], replicated, may hold values from -0.21875 to 0.21875
- output_matrix: bfloat16 [768, 768], replicated, may hold values from -0.21875 to 0.21875
- cotangent: bfloat16 [16384, 768], P(('groups', 'blk')), parts along dimension 0, may hold values from -6 to 6
Outputs:
- layer_output: bfloat16 [16384, 768], P(('groups', 'blk')), parts along dimension 0
- cell_grads: bfloat16 [16384, 768], P(('groups', 'blk')), parts along dimension 0
- weight_grads: float32 [6144, 768], P(('groups', 'blk')), parts along dimension 0
There are 2 independent parts, one for each index of `groups`. A program takes and returns all parts, laid end to end along the dimension named above; an argument that names none is the same for every part. Nothing has to cross between parts.
Inputs may be any that keep to these rules, and one draw needn't show every extreme that they name: The live anchors of index p of blk are its first live_anchor_count[p] slots; some index has 8. Faces toward the next index of blk use the first upper_slot_count[p] slots; the last index has none; some other index has 256.
All inputs are finite; a program needn't handle non-finite values.
Results may differ from a plain program's by a relative error of at most 0.023.
Values may be sent and summed in bfloat16 or wider, within the bound.
A program may use at most 128 MiB of HBM per device.

v0:
```python
import math

import jax
import jax.numpy as jnp
from jax import lax
from jax.sharding import PartitionSpec as P

MODEL_WIDTH = 768
HEADS = 12


EPS = 1e-06


def passed_along(shard, axis, by):
    count = lax.axis_size(axis)
    pairs = [(i, i + by) for i in range(count) if 0 <= i + by < count]
    return lax.ppermute(shard, axis, pairs)


def contract(left, right, left_dim, right_dim, precision=None):
    return lax.dot_general(
        left,
        right,
        (((left_dim,), (right_dim,)), ((), ())),
        precision=precision,
        preferred_element_type=jnp.float32,
    )


def build_faces(
    inner_face_first,
    inner_face_second,
    inner_face_weight,
    upper_face_cell,
    lower_face_cell,
    upper_live,
    cell_count,
):
    cell_ids = jnp.arange(cell_count, dtype=jnp.int32)
    first_hot = (inner_face_first[:, None] == cell_ids[None, :]).astype(jnp.float32)
    second_hot = (inner_face_second[:, None] == cell_ids[None, :]).astype(jnp.float32)
    difference = second_hot - first_hot
    inner_matrix = -contract(
        difference * inner_face_weight[:, None], difference, 0, 0, lax.Precision.HIGHEST
    )
    upper_map = (upper_face_cell[:, None] == cell_ids[None, :]).astype(jnp.bfloat16)
    lower_map = (lower_face_cell[:, None] == cell_ids[None, :]).astype(jnp.bfloat16)
    return (inner_matrix, upper_map, lower_map, upper_live)


def face_operator(field_rows, face_lists):
    inner_matrix, upper_map, lower_map, upper_live = face_lists
    values = field_rows.astype(jnp.float32)
    result = jnp.dot(
        inner_matrix, values, precision=lax.Precision.HIGHEST, preferred_element_type=jnp.float32
    )
    own_upper = jnp.dot(upper_map, field_rows, preferred_element_type=jnp.float32).astype(
        jnp.bfloat16
    )
    own_lower = jnp.dot(lower_map, field_rows, preferred_element_type=jnp.float32).astype(
        jnp.bfloat16
    )
    peer_rows = passed_along(own_lower, "blk", -1)
    cross_flux = upper_live[:, None] * (
        peer_rows.astype(jnp.float32) - own_upper.astype(jnp.float32)
    )
    result = result + contract(
        upper_map.astype(jnp.float32), cross_flux, 0, 0, lax.Precision.HIGHEST
    )
    returned = passed_along(cross_flux.astype(jnp.bfloat16), "blk", 1).astype(cross_flux.dtype)
    result = result - contract(lower_map.astype(jnp.float32), returned, 0, 0, lax.Precision.HIGHEST)
    return result


def split_heads(keyvals):
    count_rows = keyvals.shape[0]
    paired = keyvals.reshape(count_rows, 2, HEADS, MODEL_WIDTH // HEADS)
    return (paired[:, 0].transpose(1, 0, 2), paired[:, 1].transpose(1, 0, 2))


def per_head_scores(
    single_query_head,
    single_key_head,
    anchor_geometry_code,
    usable_mask,
    cell_geometry_rows,
    attention_score_scale,
):
    attention_scores = (
        contract(single_query_head, single_key_head, 1, 1) * attention_score_scale
        + cell_geometry_rows[:, None] * anchor_geometry_code[None, :]
    )
    return jnp.where(usable_mask[None, :], attention_scores, -jnp.inf)


def shards(
    cell_features,
    cell_geometry_rows,
    anchor_token_features,
    anchor_geometry_rows,
    live_anchor_count,
    inner_face_first,
    inner_face_second,
    inner_face_weight,
    upper_face_cell,
    lower_face_cell,
    upper_face_weight,
    upper_slot_count,
    query_matrix,
    anchor_keyvalue_matrix,
    output_matrix,
    cotangent,
):
    head_dim = MODEL_WIDTH // HEADS
    attention_score_scale = 1.0 / math.sqrt(head_dim)
    cell_count = cell_features.shape[0]
    slot_index = jnp.arange(upper_face_cell.shape[0], dtype=jnp.int32)
    upper_live = jnp.where(
        slot_index < upper_slot_count[0], upper_face_weight.astype(jnp.float32), 0.0
    )
    face_lists = build_faces(
        inner_face_first,
        inner_face_second,
        inner_face_weight,
        upper_face_cell,
        lower_face_cell,
        upper_live,
        cell_count,
    )
    mixed_rows = (
        cell_features.astype(jnp.float32) + face_operator(cell_features, face_lists)
    ).astype(jnp.bfloat16)
    mixed_f = lax.optimization_barrier(mixed_rows).astype(jnp.float32)
    inverse_rms = lax.rsqrt(jnp.mean(mixed_f * mixed_f, axis=1, keepdims=True) + EPS)
    normal_hat = mixed_f * inverse_rms
    normed = normal_hat.astype(jnp.bfloat16)
    query_rows = jnp.dot(normed, query_matrix, preferred_element_type=jnp.float32).astype(
        jnp.bfloat16
    )
    query_heads = query_rows.reshape(cell_count, HEADS, head_dim).transpose(1, 0, 2)
    keyvals = jnp.dot(
        anchor_token_features, anchor_keyvalue_matrix, preferred_element_type=jnp.float32
    ).astype(jnp.bfloat16)
    local_face_slots = jnp.arange(anchor_token_features.shape[0], dtype=jnp.int32)
    side_info = jnp.stack(
        [anchor_geometry_rows, (local_face_slots < live_anchor_count[0]).astype(jnp.bfloat16)],
        axis=1,
    )
    empty_state = (
        jnp.full((HEADS, cell_count), -jnp.inf, jnp.float32),
        jnp.zeros((HEADS, cell_count), jnp.float32),
        jnp.zeros((HEADS, cell_count, head_dim), jnp.float32),
    )
    shard_piece = (
        lax.all_gather(keyvals, "blk", axis=0, tiled=True),
        lax.all_gather(side_info, "blk", axis=0, tiled=True),
    )
    key_heads, value_heads = split_heads(shard_piece[0])
    anchor_geometry_code = shard_piece[1][:, 0].astype(jnp.float32)
    usable_mask = shard_piece[1][:, 1] > 0

    def one_head(operands):
        single_query_head, single_key_head, value_head, peak_head, total_head, accum_head = operands
        attention_scores = per_head_scores(
            single_query_head,
            single_key_head,
            anchor_geometry_code,
            usable_mask,
            cell_geometry_rows,
            attention_score_scale,
        )
        new_peak = jnp.maximum(peak_head, jnp.max(attention_scores, axis=1))
        factor = jnp.exp(peak_head - new_peak)
        exp_scores = jnp.exp(attention_scores - new_peak[:, None])
        new_total = total_head * factor + jnp.sum(exp_scores, axis=1)
        new_accum = accum_head * factor[:, None] + jnp.dot(
            exp_scores.astype(jnp.bfloat16), value_head, preferred_element_type=jnp.float32
        )
        return (new_peak, new_total, new_accum)

    run_peak, run_total, run_accum = lax.map(
        one_head, (query_heads, key_heads, value_heads) + tuple(empty_state)
    )
    all_keyvals, all_side = (
        lax.all_gather(keyvals, "blk", axis=0, tiled=True),
        lax.all_gather(side_info, "blk", axis=0, tiled=True),
    )
    attended_heads = (run_accum / run_total[:, :, None]).astype(jnp.bfloat16)
    log_total = run_peak + jnp.log(run_total)
    attended = attended_heads.transpose(1, 0, 2).reshape(cell_count, MODEL_WIDTH)
    layer_output = (
        mixed_f + jnp.dot(attended, output_matrix, preferred_element_type=jnp.float32)
    ).astype(jnp.bfloat16)
    attended_gradient = contract(cotangent, output_matrix, 1, 1).astype(jnp.bfloat16)
    grad_heads = attended_gradient.reshape(cell_count, HEADS, head_dim).transpose(1, 0, 2)
    row_dot = jnp.sum(grad_heads.astype(jnp.float32) * attended_heads.astype(jnp.float32), axis=2)
    all_keys, all_values = split_heads(all_keyvals)
    every_geometry_code = all_side[:, 0].astype(jnp.float32)
    every_usable_mask = all_side[:, 1] > 0

    def head_grads(operands):
        single_query_head, single_key_head, value_head, grad_head, total_head, dot_head = operands
        attention_scores = per_head_scores(
            single_query_head,
            single_key_head,
            every_geometry_code,
            every_usable_mask,
            cell_geometry_rows,
            attention_score_scale,
        )
        prob_weights = jnp.exp(attention_scores - total_head[:, None])
        prob_low = prob_weights.astype(jnp.bfloat16)
        grad_prob = contract(grad_head, value_head, 1, 1)
        grad_low = (prob_weights * (grad_prob - dot_head[:, None])).astype(jnp.bfloat16)
        grad_query = (
            jnp.dot(grad_low, single_key_head, preferred_element_type=jnp.float32)
            * attention_score_scale
        ).astype(jnp.bfloat16)
        grad_key = contract(grad_low, single_query_head, 0, 0) * attention_score_scale
        grad_value = contract(prob_low, grad_head, 0, 0)
        return (grad_query, grad_key, grad_value)

    grad_q_heads, grad_k_heads, grad_v_heads = lax.map(
        head_grads, (query_heads, all_keys, all_values, grad_heads, log_total, row_dot)
    )
    grad_queries = grad_q_heads.transpose(1, 0, 2).reshape(cell_count, MODEL_WIDTH)
    anchor_total = grad_k_heads.shape[1]
    grad_keyvals = jnp.concatenate(
        [
            grad_k_heads.transpose(1, 0, 2).reshape(anchor_total, MODEL_WIDTH),
            grad_v_heads.transpose(1, 0, 2).reshape(anchor_total, MODEL_WIDTH),
        ],
        axis=1,
    )
    grad_normed = contract(grad_queries, query_matrix, 1, 1)
    grad_mixed = (
        cotangent.astype(jnp.float32)
        + inverse_rms
        * (grad_normed - normal_hat * jnp.mean(grad_normed * normal_hat, axis=1, keepdims=True))
    ).astype(jnp.bfloat16)
    grad_mixed_f = lax.optimization_barrier(grad_mixed).astype(jnp.float32)
    cell_grads = (grad_mixed_f + face_operator(grad_mixed, face_lists)).astype(jnp.bfloat16)
    query_part = contract(grad_queries, normed, 0, 0)
    output_part = contract(cotangent, attended, 0, 0)
    own_grads = lax.psum_scatter(grad_keyvals, "blk", scatter_dimension=0, tiled=True)
    pair_part = contract(
        own_grads, anchor_token_features.astype(jnp.float32), 0, 0, lax.Precision.HIGHEST
    )
    stacked_terms = jnp.concatenate([query_part, pair_part, output_part], axis=0)
    weight_grads = lax.psum_scatter(stacked_terms, "blk", scatter_dimension=0, tiled=True)
    return (layer_output, cell_grads, weight_grads)


def solution(mesh):
    in_specs = (
        P(("groups", "blk"), None),
        P(("groups", "blk")),
        P(("groups", "blk"), None),
        P(("groups", "blk")),
        P(("groups", "blk")),
        P(("groups", "blk")),
        P(("groups", "blk")),
        P(("groups", "blk")),
        P(("groups", "blk")),
        P(("groups", "blk")),
        P(("groups", "blk")),
        P(("groups", "blk")),
        P(),
        P(),
        P(),
        P(("groups", "blk"), None),
    )
    out_specs = (P(("groups", "blk"), None), P(("groups", "blk"), None), P(("groups", "blk"), None))
    return jax.shard_map(shards, mesh=mesh, in_specs=in_specs, out_specs=out_specs, check_vma=False)
```

profile of v0, /device:TPU:0, one launch (start us, length us, event | category | flops | bytes accessed | tf_op | source)
XLA Modules:
  0.0 411.5 jit_solution(16580329373916814216)
XLA Ops:
  7.2 2.5 convolution_convert_fusion.6
  12.9 23.6 %all-gather = bf16[16,8,2]{1,2,0:T(2,128)(2,1)S(1)} all-gather(bf16[1,8,2]{1,2,0:T(2,128)(2,1)S(1)} %maximum_bitcast_fusion), channel_id=1, replica_groups=mesh['groups'=2,'blk'=16] {'blk'}, dimensions={0}, use_global_device_ids=true | all-gather | bytes 544 | tf_op jit(solution)/shard_map/all_gather | solution.py:157
  37.7 20.0 %all_gather.9 = bf16[128,1536]{1,0:T(8,128)(2,1)} all-gather(bf16[8,1536]{1,0:T(8,128)(2,1)S(1)} %convolution_convert_fusion), channel_id=1, replica_groups=mesh['groups'=2,'blk'=16] {'blk'}, dimensions={0}, use_global_device_ids=true | all-gather | bytes 417792 | tf_op jit(solution)/shard_map/all_gather | solution.py:156
  59.8 3.0 convolution_convert_fusion.1
  62.8 7.0 %fusion.66 = f32[512,512]{1,0:T(8,128)S(1)} fusion(s32[1536]{0:T(1024)S(1)} %copy-done.23, s32[1536]{0:T(1024)S(1)} %copy-done.24, f32[1536]{0:T(1024)S(1)} %copy-done.25), kind=kOutput, calls=%fused_computation.91 | convolution fusion | flops 4840751104 | bytes 1067008 | tf_op jit(solution)/shard_map/dot_general | solution.py:22
  70.4 2.6 fusion.89
  73.0 2.5 fusion.87
  75.5 3.1 collective-permute-start.1
  81.1 2.3 copy.41
  85.0 1.7 add_convert_fusion.1
  87.0 1.7 convolution_convert_fusion.2
  88.7 2.3 copy.36
  91.0 2.5 copy.38
  93.6 35.7 %while.28 = (s32[]{:T(128)}, f32[12,512]{1,0:T(8,128)S(1)}, f32[12,512]{1,0:T(8,128)S(1)}, f32[12,512,64]{1,2,0:T(8,128)}, pred[128]{0:T(512)(128)(4,1)S(1)}, /*...) while((s32[]{:T(128)}, f32[12,512]{1,0:T(8,128)S(1)}, ...), condition=%wide.region_4.5_spmd, body=%wide.region_1.4_spmd.sunk | while | flops 17401344 | bytes 1147653 | solution.py:182
  94.9 1.6 fusion.144
  97.9 1.6 fusion.144
  100.9 1.6 fusion.144
  103.9 1.6 fusion.144
  112.8 1.6 fusion.144
  115.7 1.6 fusion.144
  118.7 1.6 fusion.144
  121.7 1.6 fusion.144
  127.6 1.6 fusion.144
  129.9 3.4 multiply_reduce_fusion
  133.3 87.8 %while.29 = (s32[]{:T(128)}, bf16[12,512,64]{1,2,0:T(8,128)(2,1)}, f32[12,128,64]{1,2,0:T(8,128)}, f32[12,128,64]{1,2,0:T(8,128)S(1)}, pred[128]{0:T(512)(128)(4...) while((s32[]{:T(128)}, bf16[12,512,64]{1,2,0:T(8,128)(2,1)}, ...), condition=%wide.region_7.8_spmd, body=%wide.region_6.7_spmd.sunk | while | flops 42606592 | bytes 1822865 | solution.py:224
  137.3 1.7 fusion.158
  144.6 1.7 fusion.158
  151.9 1.7 fusion.158
  159.2 1.7 fusion.158
  166.6 1.7 fusion.158
  173.9 1.7 fusion.158
  181.2 1.7 fusion.158
  188.5 1.7 fusion.158
  195.8 1.7 fusion.158
  203.1 1.7 fusion.158
  210.4 1.7 fusion.158
  217.7 1.7 fusion.158
  221.1 1.9 pad_maximum_fusion.1
  223.0 2.3 copy.46
  225.4 3.6 convolution_bitcast_fusion.1
  229.0 2.3 fusion.75
  231.3 49.1 %reduce-scatter.7.cloned.1.call-done = f32[8,1536]{1,0:T(8,128)} async-done(((f32[128,1536]{1,0:T(8,128)}), f32[8,1536]{1,0:T(8,128)}) %reduce-scatter.7.cloned.1.call-update) | async-done | bytes 49168
  280.5 5.1 %fusion.91 = f32[1536,768]{1,0:T(8,128)} fusion(f32[8,1536]{1,0:T(8,128)} %reduce-scatter.7.cloned.1.call-done, bf16[8,768]{1,0:T(8,128)(2,1)S(1)} %copy-done.16), kind=kOutput, calls=%fused_computation.129 | convolution fusion | flops 113246208 | bytes 4780032 | tf_op jit(solution)/shard_map/dot_general | solution.py:22
  285.6 8.0 %pad_maximum_fusion = f32[3072,768]{1,0:T(8,128)} fusion(f32[768,768]{1,0:T(8,128)} %convolution_bitcast_fusion.1, f32[1536,768]{1,0:T(8,128)} %fusion.91, f32[768,768]{1,0:T(8,128)} %fusion.75), kind=kLoop, calls=%fused_computation.59 | loop fusion | flops 4718592 | bytes 18874368 | tf_op jit(solution)/shard_map/concatenate | solution.py:250
  293.6 2.6 fusion.56
  298.7 1.7 fusion.62
  301.2 7.1 %collective-permute-start.3 = (bf16[256,768]{1,0:T(8,128)(2,1)S(1)}, bf16[256,768]{1,0:T(8,128)(2,1)S(1)}, u32[]{:S(2)}, u32[]{:S(2)}) collective-permute-start(bf16[256,768]{1,0:T(8,128)(2,1)S(1)} %get-tuple-element.236), channel_id=1, source_target_pairs={{0,1},{1,2},{2,3},{3,4},{4,5},{5,6},{6,7},{7,8},{8,9},{9,10},{10,1... | collective-permute-start | bytes 1179656 | tf_op jit(solution)/shard_map/ppermute | solution.py:18
  312.5 92.1 %reduce-scatter.5.cloned.1.call-done = f32[192,768]{1,0:T(8,128)} async-done(((f32[3072,768]{1,0:T(8,128)}), f32[192,768]{1,0:T(8,128)}) %reduce-scatter.5.cloned.1.call-update) | async-done | bytes 589840 | tf_op jit(solution)/shard_map/reduce_scatter | solution.py:251
  (232 shorter events, 105.6 us)
Async XLA Ops:
  7.2 29.5 %copy-start = (bf16[768,1536]{1,0:T(8,128)(2,1)S(1)}, bf16[768,1536]{1,0:T(8,128)(2,1)}, u32[]{:S(2)}) copy-start(bf16[768,1536]{1,0:T(8,128)(2,1)} %param.33) | copy-start | bytes 7077892
  7.2 273.3 %reduce-scatter.7.cloned.1.call-start = ((), (), s32[]{:S(2)}) async-start(), calls=%async_computation.3 | async-start | bytes 835584
  9.7 63.3 %collective-permute-start = (bf16[256,768]{1,0:T(8,128)(2,1)}, bf16[256,768]{1,0:T(8,128)(2,1)}, u32[]{:S(2)}, u32[]{:S(2)}) collective-permute-start(bf16[256,768]{1,0:T(8,128)(2,1)} %convolution_convert_fusion.6), channel_id=1, source_target_pairs={{1,0},{2,1},{3,2},{4,3},{5,4},{6,5},{7,6},{8,7},{9,8},{10,9},{11,1... | collective-permute-start | bytes 1179656 | tf_op jit(solution)/shard_map/ppermute | solution.py:18
  37.7 22.0 %copy-start.20 = (bf16[256]{0:T(256)(128)(2,1)S(1)}, bf16[256]{0:T(256)(128)(2,1)}, u32[]{:S(2)}) copy-start(bf16[256]{0:T(256)(128)(2,1)} %param.30) | copy-start | bytes 1540
  37.7 22.0 %copy-start.7 = (bf16[512,768]{1,0:T(8,128)(2,1)S(1)}, bf16[512,768]{1,0:T(8,128)(2,1)}, u32[]{:S(2)}) copy-start(bf16[512,768]{1,0:T(8,128)(2,1)} %param.35) | copy-start | bytes 2359300
  59.8 3.0 copy-start.23
  59.8 3.0 copy-start.24
  59.8 3.0 copy-start.25
  62.8 7.6 %copy-start.1 = (bf16[512,768]{1,0:T(8,128)(2,1)S(1)}, bf16[512,768]{1,0:T(8,128)(2,1)}, u32[]{:S(2)}) copy-start(bf16[512,768]{1,0:T(8,128)(2,1)} %param.20) | copy-start | bytes 2359300
  69.8 3.2 copy-start.4
  70.4 2.6 copy-start.18
  73.0 6.2 %copy-start.12 = (bf16[12,128,64]{1,2,0:T(8,128)(2,1)S(1)}, bf16[12,128,64]{1,2,0:T(8,128)(2,1)}, u32[]{:S(2)}) copy-start(bf16[12,128,64]{1,2,0:T(8,128)(2,1)} %get-tuple-element.230) | copy-start | bytes 589828
  73.0 7.1 %copy-start.11 = (bf16[12,128,64]{1,2,0:T(8,128)(2,1)S(1)}, bf16[12,128,64]{1,2,0:T(8,128)(2,1)}, u32[]{:S(2)}) copy-start(bf16[12,128,64]{1,2,0:T(8,128)(2,1)} %get-tuple-element.231) | copy-start | bytes 589828
  75.5 7.9 %copy-start.6 = (f32[256,768]{1,0:T(8,128)S(1)}, f32[256,768]{1,0:T(8,128)}, u32[]{:S(2)}) copy-start(f32[256,768]{1,0:T(8,128)} %get-tuple-element.233) | copy-start | bytes 2359300
  75.5 8.9 %collective-permute-start.1 = (bf16[256,768]{1,0:T(8,128)(2,1)}, bf16[256,768]{1,0:T(8,128)(2,1)}, u32[]{:S(2)}, u32[]{:S(2)}) collective-permute-start(bf16[256,768]{1,0:T(8,128)(2,1)} %get-tuple-element.232), channel_id=1, source_target_pairs={{0,1},{1,2},{2,3},{3,4},{4,5},{5,6},{6,7},{7,8},{8,9},{9,10},{10,1... | collective-permute-start | bytes 1179656 | tf_op jit(solution)/shard_map/ppermute | solution.py:18
  83.4 1.1 copy-start.2
  83.4 1.7 copy-start.3
  83.4 1.7 copy-start.19
  84.4 2.5 copy-start.21
  91.0 2.5 copy-start.14
  91.0 2.5 copy-start.17
  91.0 2.5 copy-start.26
  91.0 2.6 copy-start.27
  91.0 2.6 copy-start.28
  129.3 0.6 copy-start.15
  129.9 3.4 copy-start.13
  225.3 179.3 %reduce-scatter.5.cloned.1.call-start = ((), (), s32[]{:S(2)}) async-start(), calls=%async_computation.2 | async-start | bytes 10027008 | tf_op jit(solution)/shard_map/reduce_scatter | solution.py:251
  225.4 3.7 copy-start.10
  229.0 51.5 %copy-start.16 = (bf16[8,768]{1,0:T(8,128)(2,1)S(1)}, bf16[8,768]{1,0:T(8,128)(2,1)}, u32[]{:S(2)}) copy-start(bf16[8,768]{1,0:T(8,128)(2,1)} %param.22) | copy-start | bytes 36868
  293.6 2.6 copy-start.8
  296.2 2.4 copy-start.9
  296.2 2.4 copy-start.22
  297.1 3.6 collective-permute-start.2
  300.4 7.9 %copy-start.5 = (f32[512,512]{1,0:T(8,128)S(1)}, f32[512,512]{1,0:T(8,128)}, u32[]{:S(2)}) copy-start(f32[512,512]{1,0:T(8,128)} %copy-done.4) | copy-start | bytes 3145732
  301.2 9.7 %collective-permute-start.3 = (bf16[256,768]{1,0:T(8,128)(2,1)S(1)}, bf16[256,768]{1,0:T(8,128)(2,1)S(1)}, u32[]{:S(2)}, u32[]{:S(2)}) collective-permute-start(bf16[256,768]{1,0:T(8,128)(2,1)S(1)} %get-tuple-element.236), channel_id=1, source_target_pairs={{0,1},{1,2},{2,3},{3,4},{4,5},{5,6},{6,7},{7,8},{8,9},{9,10},{10,1... | collective-permute-start | bytes 1179656 | tf_op jit(solution)/shard_map/ppermute | solution.py:18
Sparse Core Ops, SparseCore 0:
  225.4 54.9 reduce-scatter.6
  293.7 110.8 reduce-scatter.4
where the time goes:
time: 416 us; the launch traced here: 411 us
  matrix products  155 us (37%)
  waiting for transfers between devices  142 us (34%)
  blocking collectives  43.6 us (10%)
  local copies, waits for them, and re-layouts  24.5 us (6%)
  other arithmetic  17.5 us (4%)
  between operations  15.7 us (4%)
  starting transfers between devices  13.1 us (3%)
    dot_general x70, matrix products, contract(): lax.dot_general(left, right, (((left_dim,), (right_dim,)), ((), ())), pre...  102 us
    reduce_scatter x1, waiting for transfers between devices, shards(): lax.psum_scatter(stacked_terms, 'blk', scatter_dimension=0, tiled=True)  92.1 us
    unnamed x3, waiting for transfers between devices  49.2 us
    all_gather x1, blocking collectives, shards(): lax.all_gather(side_info, 'blk', axis=0, tiled=True)  23.6 us
    all_gather x1, blocking collectives, shards(): lax.all_gather(keyvals, 'blk', axis=0, tiled=True)  20 us
    dot_general x12, matrix products, one_head(): jnp.dot(exp_scores.astype(jnp.bfloat16), value_head, preferred_element_ty...  19.4 us
    dot_general x12, matrix products, head_grads(): jnp.dot(grad_low, single_key_head, preferred_element_type=jnp.float32)  19 us
    ppermute x4, starting transfers between devices, passed_along(): return lax.ppermute(shard, axis, pairs)  13.1 us
  transfers between devices with their start and end apart: 6, of which 3 were waited for; matrix products, arithmetic and copies ran while one was open for 9% of the time, Pallas kernels for 0%

commit v1 on v0

v1 whole, which is shorter than its diff:
```python
import functools
import math

import jax
import jax.numpy as jnp
from jax import lax
from jax.experimental import pallas as pl
from jax.experimental.pallas import tpu as pltpu
from jax.sharding import PartitionSpec as P

MODEL_WIDTH = 768
HEADS = 12
EPS = 1e-06
MIB = 1 << 20


def contract(left, right, left_dim, right_dim, precision=None):
    return lax.dot_general(
        left,
        right,
        (((left_dim,), (right_dim,)), ((), ())),
        precision=precision,
        preferred_element_type=jnp.float32,
    )


def exchanged(shard, bit):
    count = lax.axis_size("blk")
    return lax.ppermute(shard, "blk", [(i, i ^ bit) for i in range(count)])


def passed_along(shard, by):
    count = lax.axis_size("blk")
    return lax.ppermute(
        shard, "blk", [(i, i + by) for i in range(count) if 0 <= i + by < count]
    )


def faces_kernel(first_ref, second_ref, high_ref, low_ref, inner_high_ref, inner_low_ref):
    shape = (inner_high_ref.shape[0], first_ref.shape[1])
    ids = lax.broadcasted_iota(jnp.int32, shape, 0)
    difference = jnp.where(ids == second_ref[...], 1.0, 0.0) - jnp.where(
        ids == first_ref[...], 1.0, 0.0
    )
    low = difference.astype(jnp.bfloat16)
    total = contract((difference * high_ref[...]).astype(jnp.bfloat16), low, 1, 1)
    total = total + contract((difference * low_ref[...]).astype(jnp.bfloat16), low, 1, 1)
    high_part = (-total).astype(jnp.bfloat16)
    inner_high_ref[...] = high_part
    inner_low_ref[...] = (-total - high_part.astype(jnp.float32)).astype(jnp.bfloat16)


def inner_faces(first, second, weight, cell_count):
    high = lax.reduce_precision(weight, 8, 7)
    matrix = jax.ShapeDtypeStruct((cell_count, cell_count), jnp.bfloat16)
    slots = first.shape[0]
    return pl.pallas_call(
        faces_kernel,
        out_shape=(matrix, matrix),
        compiler_params=pltpu.CompilerParams(vmem_limit_bytes=32 * MIB),
        cost_estimate=pl.CostEstimate(
            flops=4 * slots * cell_count * cell_count,
            bytes_accessed=4 * cell_count * cell_count,
            transcendentals=0,
        ),
    )(first[None, :], second[None, :], high[None, :], (weight - high)[None, :])


def face_operator(rows, faces):
    inner_high, inner_low, cross_map, upper_live, lower_live = faces
    slots = upper_live.shape[0]
    own = contract(cross_map, rows, 0, 0)
    own_low = own.astype(jnp.bfloat16)
    peer_lower = passed_along(own_low[slots:], -1)
    peer_upper = passed_along(own_low[:slots], 1)
    inner = contract(inner_high, rows, 1, 0) + contract(inner_low, rows, 1, 0)
    upper_flux = upper_live[:, None] * (peer_lower.astype(jnp.float32) - own[:slots])
    lower_flux = lower_live[:, None] * (peer_upper.astype(jnp.float32) - own[slots:])
    flux = jnp.concatenate([upper_flux, lower_flux], axis=0).astype(jnp.bfloat16)
    return inner + contract(cross_map, flux, 1, 0)


def attention_kernel(
    scale,
    query_ref,
    grad_ref,
    key_ref,
    value_ref,
    cell_code_ref,
    anchor_code_ref,
    dead_ref,
    attended_ref,
    grad_query_ref,
    grad_key_ref,
    grad_value_ref,
):
    anchors = key_ref.shape[0]
    half = key_ref.shape[1] // 2
    left = lax.broadcasted_iota(jnp.int32, key_ref.shape, 1) < half

    def both(ref):
        rows = ref[...]
        none = jnp.zeros_like(rows)
        return jnp.concatenate([jnp.where(left, rows, none), jnp.where(left, none, rows)], axis=0)

    keys, values = both(key_ref), both(value_ref)
    queries, grads = query_ref[...], grad_ref[...]
    scores = contract(queries, keys, 1, 1)
    grad_prob = contract(grads, values, 1, 1)
    bias = cell_code_ref[...] * anchor_code_ref[...] + dead_ref[...]
    lows, grad_lows = [], []
    for head in range(2):
        part = slice(head * anchors, (head + 1) * anchors)
        score = scores[:, part] * scale + bias
        exp_scores = jnp.exp(score - jnp.max(score, axis=1, keepdims=True))
        weights = exp_scores * (1.0 / jnp.sum(exp_scores, axis=1, keepdims=True))
        low = weights.astype(jnp.bfloat16)
        gradient = grad_prob[:, part]
        dots = jnp.sum(low.astype(jnp.float32) * gradient, axis=1, keepdims=True)
        lows.append(low)
        grad_lows.append((weights * (gradient - dots)).astype(jnp.bfloat16))
    low = jnp.concatenate(lows, axis=1)
    grad_low = jnp.concatenate(grad_lows, axis=1)
    attended_ref[...] = contract(low, values, 1, 0).astype(jnp.bfloat16)
    grad_query_ref[...] = (contract(grad_low, keys, 1, 0) * scale).astype(jnp.bfloat16)
    upper = lax.broadcasted_iota(jnp.int32, grad_key_ref.shape, 0) < half
    grad_key = contract(queries, grad_low, 0, 0) * scale
    grad_key_ref[...] = jnp.where(upper, grad_key[:, :anchors], grad_key[:, anchors:])
    grad_value = contract(grads, low, 0, 0)
    grad_value_ref[...] = jnp.where(upper, grad_value[:, :anchors], grad_value[:, anchors:])


def attention(queries, grads, keyvals, cell_code, anchor_code, dead):
    cells = queries.shape[0]
    anchors = keyvals.shape[0]
    pairs = HEADS // 2
    wide = MODEL_WIDTH // pairs
    rows = pl.BlockSpec((cells, wide), lambda i: (0, i))
    keys = pl.BlockSpec((anchors, wide), lambda i: (0, i))
    values = pl.BlockSpec((anchors, wide), lambda i: (0, i + pairs))
    turned = pl.BlockSpec((wide, anchors), lambda i: (i, 0))
    fixed = lambda shape: pl.BlockSpec(shape, lambda i: (0, 0))
    limit = min(56 * MIB, 16 * MIB + 64 * cells * anchors)
    return pl.pallas_call(
        functools.partial(attention_kernel, 1.0 / math.sqrt(MODEL_WIDTH // HEADS)),
        grid=(pairs,),
        in_specs=[rows, rows, keys, values, fixed((cells, 1)), fixed((1, anchors)), fixed((1, anchors))],
        out_specs=[rows, rows, turned, turned],
        out_shape=(
            jax.ShapeDtypeStruct((cells, MODEL_WIDTH), jnp.bfloat16),
            jax.ShapeDtypeStruct((cells, MODEL_WIDTH), jnp.bfloat16),
            jax.ShapeDtypeStruct((MODEL_WIDTH, anchors), jnp.float32),
            jax.ShapeDtypeStruct((MODEL_WIDTH, anchors), jnp.float32),
        ),
        compiler_params=pltpu.CompilerParams(vmem_limit_bytes=limit),
        cost_estimate=pl.CostEstimate(
            flops=24 * cells * anchors * MODEL_WIDTH,
            bytes_accessed=8 * cells * MODEL_WIDTH,
            transcendentals=cells * anchors * HEADS,
        ),
    )(queries, grads, keyvals, keyvals, cell_code[:, None], anchor_code[None, :], dead[None, :])


def gathered(rows):
    me = lax.axis_index("blk")
    bit = 1
    while bit < lax.axis_size("blk"):
        peer = exchanged(rows, bit)
        upper = (me & bit) > 0
        rows = jnp.concatenate(
            [jnp.where(upper, peer, rows), jnp.where(upper, rows, peer)], axis=0
        )
        bit *= 2
    return rows


def halved(blocks, quarter):
    me = lax.axis_index("blk")
    bit = 1
    while bit < quarter:
        shape = blocks.shape
        paired = blocks.reshape(shape[0], shape[1] // 2, 2, shape[2], shape[3])
        upper = (me & bit) > 0
        sent = jnp.where(upper, paired[:, :, 0], paired[:, :, 1]).astype(jnp.bfloat16)
        kept = jnp.where(upper, paired[:, :, 1], paired[:, :, 0])
        blocks = kept + exchanged(sent, bit).astype(jnp.float32)
        bit *= 2
    return blocks[:, 0]


def summed_weight_grads(query_part, pair_left, output_part, tokens):
    count = lax.axis_size("blk")
    me = lax.axis_index("blk")
    quarter = count // 4
    rows = 4 * MODEL_WIDTH // count
    output_block = halved(output_part.reshape(1, quarter, rows, MODEL_WIDTH), quarter)[0]
    pair_blocks = halved(pair_left.reshape(2, quarter, rows, -1), quarter)
    query_block = halved(query_part.reshape(1, quarter, rows, MODEL_WIDTH), quarter)[0]
    place = me // quarter
    odd = place % 2 > 0
    pair_sent = jnp.where(odd, pair_blocks[1], pair_blocks[0]).astype(jnp.bfloat16)
    pair_kept = jnp.where(odd, pair_blocks[0], pair_blocks[1])
    pair = pair_kept + exchanged(pair_sent, quarter).astype(jnp.float32)
    sent = jnp.where(odd, query_block, output_block).astype(jnp.bfloat16)
    kept = jnp.where(odd, output_block, query_block)
    block = kept + exchanged(sent, quarter).astype(jnp.float32)
    inward = [(i, i + 2 * quarter) for i in range(quarter)]
    inward += [(i, i - 2 * quarter) for i in range(3 * quarter, count)]
    outward = [(to, start) for start, to in inward]
    pair = pair + lax.ppermute(pair.astype(jnp.bfloat16), "blk", inward).astype(jnp.float32)
    block = block + lax.ppermute(block.astype(jnp.bfloat16), "blk", outward).astype(jnp.float32)
    product = contract(pair, tokens.astype(jnp.float32), 1, 0, lax.Precision.HIGHEST)
    return jnp.where((place == 0) | (place == 3), block, product)


def shards(
    cell_features,
    cell_geometry_rows,
    anchor_token_features,
    anchor_geometry_rows,
    live_anchor_count,
    inner_face_first,
    inner_face_second,
    inner_face_weight,
    upper_face_cell,
    lower_face_cell,
    upper_face_weight,
    upper_slot_count,
    query_matrix,
    anchor_keyvalue_matrix,
    output_matrix,
    cotangent,
):
    cell_count = cell_features.shape[0]
    own_anchors = anchor_token_features.shape[0]
    slot_index = jnp.arange(upper_face_cell.shape[0], dtype=jnp.int32)
    live_weight = jnp.where(slot_index < upper_slot_count[0], upper_face_weight, 0).astype(
        jnp.bfloat16
    )
    lower_live = passed_along(live_weight, 1).astype(jnp.float32)
    live = jnp.arange(own_anchors, dtype=jnp.int32) < live_anchor_count[0]
    side = jnp.stack([anchor_geometry_rows, live.astype(jnp.bfloat16)], axis=1)
    packed = gathered(
        jnp.concatenate([anchor_token_features, jnp.pad(side, ((0, 0), (0, 126)))], axis=1)
    )
    tokens = packed[:, :MODEL_WIDTH]
    anchor_code = packed[:, MODEL_WIDTH].astype(jnp.float32)
    dead = jnp.where(packed[:, MODEL_WIDTH + 1] > 0, 0.0, -jnp.inf).astype(jnp.float32)

    cell_ids = jnp.arange(cell_count, dtype=jnp.int32)
    cross_cells = jnp.concatenate([upper_face_cell, lower_face_cell])
    cross_map = (cell_ids[:, None] == cross_cells[None, :]).astype(jnp.bfloat16)
    faces = inner_faces(inner_face_first, inner_face_second, inner_face_weight, cell_count) + (
        cross_map,
        live_weight.astype(jnp.float32),
        lower_live,
    )
    mixed_rows = (
        cell_features.astype(jnp.float32) + face_operator(cell_features, faces)
    ).astype(jnp.bfloat16)
    mixed_f = lax.optimization_barrier(mixed_rows).astype(jnp.float32)
    inverse_rms = lax.rsqrt(jnp.mean(mixed_f * mixed_f, axis=1, keepdims=True) + EPS)
    normal_hat = mixed_f * inverse_rms
    normed = normal_hat.astype(jnp.bfloat16)
    queries = contract(normed, query_matrix, 1, 0).astype(jnp.bfloat16)
    keyvals = contract(tokens, anchor_keyvalue_matrix, 1, 0).astype(jnp.bfloat16)
    attended_gradient = contract(cotangent, output_matrix, 1, 1).astype(jnp.bfloat16)
    attended, grad_queries, grad_keys, grad_values = attention(
        queries, attended_gradient, keyvals, cell_geometry_rows, anchor_code, dead
    )
    grad_normed = contract(grad_queries, query_matrix, 1, 1)
    grad_mixed = (
        cotangent.astype(jnp.float32)
        + inverse_rms
        * (grad_normed - normal_hat * jnp.mean(grad_normed * normal_hat, axis=1, keepdims=True))
    ).astype(jnp.bfloat16)
    grad_mixed = lax.optimization_barrier(grad_mixed)
    weight_grads = summed_weight_grads(
        contract(grad_queries, normed, 0, 0),
        jnp.stack([grad_keys, grad_values]),
        contract(cotangent, attended, 0, 0),
        tokens,
    )
    cell_grads = (grad_mixed.astype(jnp.float32) + face_operator(grad_mixed, faces)).astype(
        jnp.bfloat16
    )
    layer_output = (mixed_f + contract(attended, output_matrix, 1, 0)).astype(jnp.bfloat16)
    return (layer_output, cell_grads, weight_grads)


def solution(mesh):
    cells = P(("groups", "blk"))
    in_specs = (cells,) * 12 + (P(), P(), P(), cells)
    return jax.shard_map(
        shards, mesh=mesh, in_specs=in_specs, out_specs=(cells, cells, cells), check_vma=False
    )
```

time: 416 us -> 107 us (0.26)
  matrix products: 155 us -> 20.4 us
  waiting for transfers between devices: 142 us -> 26.7 us
  blocking collectives: 43.6 us -> 0 us
  starting transfers between devices: 13.1 us -> 34.3 us
  local copies, waits for them, and re-layouts: 24.5 us -> 4.51 us
  between operations: 15.7 us -> 2.55 us
  Pallas kernels: 0 us -> 8.03 us
  other arithmetic: 17.5 us -> 10 us
    reduce_scatter x1 -> x0, waiting for transfers between devices: 92.1 us -> none  [shards(): lax.psum_scatter(stacked_terms, 'blk', scatter_dimension=0, tiled=True)]
    dot_general x70 -> x16, matrix products: 102 us -> 20.4 us  [contract(): lax.dot_general(left, right, (((left_dim,), (right_dim,)), ((), ())), pre...]
    dot_general x33 -> x0, matrix products: 52.9 us -> none  [the longest x12 19.4 us: one_head(): jnp.dot(exp_scores.astype(jnp.bfloat16), value_head, preferred_element_ty...]
    unnamed x3 -> x0, waiting for transfers between devices: 49.2 us -> none
    all_gather x2 -> x0, blocking collectives: 43.6 us -> none  [the longest x1 23.6 us: shards(): lax.all_gather(side_info, 'blk', axis=0, tiled=True)]
    ppermute x4 -> x19, waiting for transfers between devices: 0.38 us -> 26.7 us  [the longest x12 20 us: exchanged(): return lax.ppermute(shard, 'blk', [(i, i ^ bit) for i in range(count)])]
    ppermute x4 -> x19, starting transfers between devices: 13.1 us -> 34.3 us  [the longest x12 16 us: exchanged(): return lax.ppermute(shard, 'blk', [(i, i ^ bit) for i in range(count)])]
    dynamic_slice x12 -> x0, local copies, waits for them, and re-layouts: 8.89 us -> none  [shards(): lax.map(one_head, (query_heads, key_heads, value_heads) + tuple(empty_sta...]
  transfers between devices with their start and end apart: 6 -> 19, of which waited for: 3 -> 7; matrix products, arithmetic and copies ran while one was open for 9% -> 21% of each run, Pallas kernels for 0% -> 2%
where the time goes in v1:
time: 107 us
  starting transfers between devices  34.3 us (32%)
  waiting for transfers between devices  26.7 us (25%)
  matrix products  20.4 us (19%)
  other arithmetic  10 us (9%)
  Pallas kernels  8.03 us (8%)
  local copies, waits for them, and re-layouts  4.51 us (4%)
  between operations  2.55 us (2%)
    dot_general x16, matrix products, contract(): lax.dot_general(left, right, (((left_dim,), (right_dim,)), ((), ())), pre...  20.4 us
    ppermute x12, waiting for transfers between devices, exchanged(): return lax.ppermute(shard, 'blk', [(i, i ^ bit) for i in range(count)])  20 us
    ppermute x12, starting transfers between devices, exchanged(): return lax.ppermute(shard, 'blk', [(i, i ^ bit) for i in range(count)])  16 us
    ppermute x5, starting transfers between devices, passed_along(): lax.ppermute(shard, 'blk', [(i, i + by) for i in range(count) if 0 <= i +...  12.3 us
    ppermute x1, waiting for transfers between devices, summed_weight_grads(): lax.ppermute(block.astype(jnp.bfloat16), 'blk', outward).astype(jnp.float32)  6.7 us
    pallas_call x1, Pallas kernels, attention(): pl.pallas_call(functools.partial(attention_kernel, 1.0 / math.sqrt(MODEL_...  5.92 us
    ppermute x1, starting transfers between devices, summed_weight_grads(): lax.ppermute(pair.astype(jnp.bfloat16), 'blk', inward).astype(jnp.float32)  4.71 us
    unnamed x33, local copies, waits for them, and re-layouts  2.62 us
  transfers between devices with their start and end apart: 19, of which 7 were waited for; matrix products, arithmetic and copies ran while one was open for 21% of the time, Pallas kernels for 2%

profile of v1, /device:TPU:0, one launch (start us, length us, event | category | flops | bytes accessed | tf_op | source)
XLA Modules:
  0.0 106.5 jit_solution(15938539046139660212)
XLA Ops:
  1.4 1.2 %fusion.67 = (f32[256]{0:T(256)}, bf16[256]{0:T(256)(128)(2,1)}) fusion(bf16[256]{0:T(256)(128)(2,1)} %param.26, s32[]{:T(128)} %bitcast.172), kind=kLoop, calls=%fused_computation.125 | loop fusion | flops 768 | bytes 2052 | tf_op jit(solution)/shard_map/convert_element_type | solution.py:255
  2.6 2.9 %collective-permute-start.1 = (bf16[256]{0:T(256)(128)(2,1)}, bf16[256]{0:T(256)(128)(2,1)}, u32[]{:S(2)}, u32[]{:S(2)}) collective-permute-start(bf16[256]{0:T(256)(128)(2,1)} %get-tuple-element.21), channel_id=1, source_target_pairs={{0,1},{1,2},{2,3},{3,4},{4,5},{5,6},{6,7},{7,8},{8,9},{9,10},{10,1... | collective-permute-start | bytes 1544 | tf_op jit(solution)/shard_map/ppermute | solution.py:34
  6.2 0.7 pad_maximum_fusion.5
  7.0 0.7 fusion.61
  7.7 2.0 %collective-permute-start.3 = (bf16[8,896]{1,0:T(8,128)(2,1)S(1)}, bf16[8,896]{1,0:T(8,128)(2,1)S(1)}, u32[]{:S(2)}, u32[]{:S(2)}) collective-permute-start(bf16[8,896]{1,0:T(8,128)(2,1)S(1)} %fusion.61), channel_id=1, source_target_pairs={{0,1},{1,0},{2,3},{3,2},{4,5},{5,4},{6,7},{7,6},{8,9},{9,8},{10,11... | collective-permute-start | bytes 43016 | tf_op jit(solution)/shard_map/ppermute | solution.py:29
  9.7 0.7 pad_add_fusion
  10.4 2.9 %fusion.70 = (bf16[512,768]{1,0:T(8,128)(2,1)S(1)}, f32[512,768]{1,0:T(8,128)}) fusion(bf16[512,768]{1,0:T(8,128)(2,1)} %param.16, s32[512]{0:T(512)S(1)} %pad_add_fusion), kind=kOutput, calls=%fused_computation.128 | convolution fusion | flops 403308544 | bytes 3147776 | tf_op jit(solution)/shard_map/dot_general | solution.py:18
  13.4 0.9 fusion.69
  14.3 1.3 %collective-permute-start = (bf16[256,768]{1,0:T(8,128)(2,1)}, bf16[256,768]{1,0:T(8,128)(2,1)}, u32[]{:S(2)}, u32[]{:S(2)}) collective-permute-start(bf16[256,768]{1,0:T(8,128)(2,1)} %get-tuple-element.28), channel_id=1, source_target_pairs={{1,0},{2,1},{3,2},{4,3},{5,4},{6,5},{7,6},{8,7},{9,8},{10,9},{11,1... | collective-permute-start | bytes 1179656 | tf_op jit(solution)/shard_map/ppermute | solution.py:34
  15.6 3.8 %collective-permute-start.2 = (bf16[256,768]{1,0:T(8,128)(2,1)}, bf16[256,768]{1,0:T(8,128)(2,1)}, u32[]{:S(2)}, u32[]{:S(2)}) collective-permute-start(bf16[256,768]{1,0:T(8,128)(2,1)} %get-tuple-element.29), channel_id=1, source_target_pairs={{0,1},{1,2},{2,3},{3,4},{4,5},{5,6},{6,7},{7,8},{8,9},{9,10},{10,1... | collective-permute-start | bytes 1179656 | tf_op jit(solution)/shard_map/ppermute | solution.py:34
  19.5 0.9 collective-permute-start.4
  20.4 2.1 %shard_map.175 = (bf16[512,512]{1,0:T(8,128)(2,1)S(1)}, bf16[512,512]{1,0:T(8,128)(2,1)S(1)}) custom-call(s32[1,1536]{1,0:T(1,128)S(1)} %broadcast_in_dim.37.first_ref, s32[1,1536]{1,0:T(1,128)S(1)} %broadcast_in_dim.38.second_ref, f32[1,1536]{1,0:T(1,128)S(1)} %broadcast_in_dim.39.high_ref, f32[1,1536]{1,0:T(1,128)S(1)} %broadcast_in_dim.40.low_ref), custom_call_target="tpu_custom_call" | custom-call | flops 1610612736 | bytes 1048576 | tf_op jit(solution)/shard_map/pallas_call | solution.py:57
  22.6 1.9 %collective-permute-done.4 = bf16[16,896]{1,0:T(8,128)(2,1)S(1)} collective-permute-done((bf16[16,896]{1,0:T(8,128)(2,1)S(1)}, bf16[16,896]{1,0:T(8,128)(2,1)S(1)}, u32[]{:S(2)}, u32[]{:S(2)}) %collective-permute-start.4) | collective-permute-done | bytes 28704 | tf_op jit(solution)/shard_map/ppermute | solution.py:29
  24.5 5.9 %collective-permute-start.5 = (bf16[32,896]{1,0:T(8,128)(2,1)S(1)}, bf16[32,896]{1,0:T(8,128)(2,1)}, u32[]{:S(2)}, u32[]{:S(2)}) collective-permute-start(bf16[32,896]{1,0:T(8,128)(2,1)S(1)} %pad_maximum_fusion.2), channel_id=1, source_target_pairs={{0,4},{1,5},{2,6},{3,7},{4,0},{5,1},{6,2},{7,3},{8,12},{9,13},{10,... | collective-permute-start | bytes 172040 | tf_op jit(solution)/shard_map/ppermute | solution.py:29
  30.3 2.8 %fusion.72 = f32[512,768]{1,0:T(8,128)} fusion(bf16[512,512]{1,0:T(8,128)(2,1)S(1)} %get-tuple-element.9, bf16[512,768]{1,0:T(8,128)(2,1)} %param.16), kind=kOutput, calls=%fused_computation.130 | convolution fusion | flops 402653184 | bytes 2883584 | tf_op jit(solution)/shard_map/dot_general | solution.py:18
  33.2 0.8 broadcast_select_fusion.3
  34.0 0.7 pad_maximum_fusion.1
  34.7 2.6 %collective-permute-start.6 = (bf16[64,896]{1,0:T(8,128)(2,1)}, bf16[64,896]{1,0:T(8,128)(2,1)}, u32[]{:S(2)}, u32[]{:S(2)}) collective-permute-start(bf16[64,896]{1,0:T(8,128)(2,1)} %pad_maximum_fusion.1), channel_id=1, source_target_pairs={{0,8},{1,9},{2,10},{3,11},{4,12},{5,13},{6,14},{7,15},{8,0},{9,1},... | collective-permute-start | bytes 344072 | tf_op jit(solution)/shard_map/ppermute | solution.py:29
  37.3 3.2 %convolution_convert_fusion.1.grad_ref = bf16[512,768]{1,0:T(8,128)(2,1)} fusion(bf16[512,768]{1,0:T(8,128)(2,1)} %param.31, bf16[768,768]{1,0:T(8,128)(2,1)} %param.30), kind=kOutput, calls=%fused_computation.16 | convolution fusion | flops 604372992 | bytes 2752512 | tf_op jit(solution)/shard_map/dot_general | solution.py:18
  40.5 0.9 copy.37.cell_code_ref
  41.4 0.7 convert_element_type.219
  42.0 1.2 %collective-permute-done.6 = bf16[64,896]{1,0:T(8,128)(2,1)} collective-permute-done((bf16[64,896]{1,0:T(8,128)(2,1)}, bf16[64,896]{1,0:T(8,128)(2,1)}, u32[]{:S(2)}, u32[]{:S(2)}) %collective-permute-start.6) | collective-permute-done | bytes 114720 | tf_op jit(solution)/shard_map/ppermute | solution.py:29
  43.2 0.9 broadcast_select_fusion
  44.9 0.7 copy-done.4
  45.6 1.3 %fusion.23 = (bf16[256,768]{1,0:T(8,128)(2,1)S(1)}, bf16[256,768]{1,0:T(8,128)(2,1)S(1)}) fusion(f32[512,768]{1,0:T(8,128)S(1)} %copy-done.4, bf16[256,768]{1,0:T(8,128)(2,1)} %collective-permute-done, f32[256]{0:T(256)S(1)} %copy-done.9, bf16[256,768]{1,0:T(8,128)(2,1)} %collective-permute-done.2, f32[256]{0:T(256)S(1)} %convert_element_type.219), kind=kLoop, calls=%fused_computation.44 | loop fusion | flops 1572864 | bytes 3147776 | tf_op jit(solution)/shard_map/convert.3
  46.9 0.6 fusion.14
  48.6 0.6 add_convert_fusion.1
  49.8 0.8 convolution_convert_fusion.2.query_ref
  51.1 5.9 %shard_map.176 = (bf16[512,768]{1,0:T(8,128)(2,1)S(1)}, bf16[512,768]{1,0:T(8,128)(2,1)S(1)}, f32[768,128]{1,0:T(8,128)S(1)}, f32[768,128]{1,0:T(8,128)S(1)}) custom-call(bf16[512,768]{1,0:T(8,128)(2,1)S(1)} %convolution_convert_fusion.2.query_ref, bf16[512,768]{1,0:T(8,128)(2,1)S(1)} %copy-done.2, ...), custom_call_target="tpu_custom_call" | custom-call | flops 1207959552 | bytes 3145728 | tf_op jit(solution)/shard_map/pallas_call | solution.py:144
  57.0 1.7 %fusion.9 = bf16[512,768]{1,0:T(8,128)(2,1)} fusion(bf16[512,768]{1,0:T(8,128)(2,1)S(1)} %add_convert_fusion.1, bf16[512,768]{1,0:T(8,128)(2,1)S(1)} %get-tuple-element.11, bf16[768,768]{1,0:T(8,128)(2,1)S(1)} %copy-done.14), kind=kOutput, calls=%fused_computation.13 | convolution fusion | flops 605159424 | bytes 3538944 | tf_op jit(solution)/shard_map/dot_general | solution.py:18
  58.7 0.8 fusion.74
  59.5 0.9 fusion.3
  60.4 0.9 fusion.40
  62.6 0.6 fusion.71
  64.4 4.3 %collective-permute-done.16 = bf16[2,1,192,128]{3,2,0,1:T(8,128)(2,1)S(1)} collective-permute-done((bf16[2,1,192,128]{3,2,0,1:T(8,128)(2,1)S(1)}, bf16[2,1,192,128]{3,2,0,1:T(8,128)(2,1)S(1)}, u32[]{:S(2)}, u32[]{:S(2)}) %collective-permute-start.16) | collective-permute-done | bytes 98336 | tf_op jit(solution)/shard_map/ppermute | solution.py:29
  69.3 1.3 %collective-permute-start.10 = (bf16[1,1,192,768]{3,2,1,0:T(8,128)(2,1)S(1)}, bf16[1,1,192,768]{3,2,1,0:T(8,128)(2,1)S(1)}, u32[]{:S(2)}, u32[]{:S(2)}) collective-permute-start(bf16[1,1,192,768]{3,2,1,0:T(8,128)(2,1)S(1)} %fusion.43), channel_id=1, source_target_pairs={{0,2},{1,3},{2,0},{3,1},{4,6},{5,7},{6,4},{7,5},{8,10},{9,11},{10,... | collective-permute-start | bytes 884744 | tf_op jit(solution)/shard_map/ppermute | solution.py:29
  70.9 0.8 collective-permute-start.12
  71.8 1.3 %collective-permute-start.7 = (bf16[256,768]{1,0:T(8,128)(2,1)S(1)}, bf16[256,768]{1,0:T(8,128)(2,1)S(1)}, u32[]{:S(2)}, u32[]{:S(2)}) collective-permute-start(bf16[256,768]{1,0:T(8,128)(2,1)S(1)} %get-tuple-element.26), channel_id=1, source_target_pairs={{1,0},{2,1},{3,2},{4,3},{5,4},{6,5},{7,6},{8,7},{9,8},{10,9},{11,1... | collective-permute-start | bytes 1179656 | tf_op jit(solution)/shard_map/ppermute | solution.py:34
  73.1 3.1 %collective-permute-start.8 = (bf16[256,768]{1,0:T(8,128)(2,1)S(1)}, bf16[256,768]{1,0:T(8,128)(2,1)S(1)}, u32[]{:S(2)}, u32[]{:S(2)}) collective-permute-start(bf16[256,768]{1,0:T(8,128)(2,1)S(1)} %get-tuple-element.27), channel_id=1, source_target_pairs={{0,1},{1,2},{2,3},{3,4},{4,5},{5,6},{6,7},{7,8},{8,9},{9,10},{10,1... | collective-permute-start | bytes 1179656 | tf_op jit(solution)/shard_map/ppermute | solution.py:34
  76.2 4.7 %collective-permute-start.18 = (bf16[192,128]{1,0:T(8,128)(2,1)S(1)}, bf16[192,128]{1,0:T(8,128)(2,1)S(1)}, u32[]{:S(2)}, u32[]{:S(2)}) collective-permute-start(bf16[192,128]{1,0:T(8,128)(2,1)S(1)} %fusion.62), channel_id=1, source_target_pairs={{0,8},{1,9},{2,10},{3,11},{12,4},{13,5},{14,6},{15,7},{16,24},{17,... | collective-permute-start | bytes 147464 | tf_op jit(solution)/shard_map/ppermute | solution.py:210
  80.9 1.4 %collective-permute-done.10 = bf16[1,1,192,768]{3,2,1,0:T(8,128)(2,1)S(1)} collective-permute-done((bf16[1,1,192,768]{3,2,1,0:T(8,128)(2,1)S(1)}, bf16[1,1,192,768]{3,2,1,0:T(8,128)(2,1)S(1)}, u32[]{:S(2)}, u32[]{:S(2)}) %collective-permute-start.10) | collective-permute-done | bytes 294944 | tf_op jit(solution)/shard_map/ppermute | solution.py:29
  82.3 6.3 %collective-permute-done.12 = bf16[1,1,192,768]{3,2,1,0:T(8,128)(2,1)S(1)} collective-permute-done((bf16[1,1,192,768]{3,2,1,0:T(8,128)(2,1)S(1)}, bf16[1,1,192,768]{3,2,1,0:T(8,128)(2,1)S(1)}, u32[]{:S(2)}, u32[]{:S(2)}) %collective-permute-start.12) | collective-permute-done | bytes 294944 | tf_op jit(solution)/shard_map/ppermute | solution.py:29
  88.8 1.1 %collective-permute-start.13 = (bf16[192,768]{1,0:T(8,128)(2,1)S(1)}, bf16[192,768]{1,0:T(8,128)(2,1)S(1)}, u32[]{:S(2)}, u32[]{:S(2)}) collective-permute-start(bf16[192,768]{1,0:T(8,128)(2,1)S(1)} %get-tuple-element.17), channel_id=1, source_target_pairs={{0,4},{1,5},{2,6},{3,7},{4,0},{5,1},{6,2},{7,3},{8,12},{9,13},{10,... | collective-permute-start | bytes 884744 | tf_op jit(solution)/shard_map/ppermute | solution.py:29
  90.7 4.9 %collective-permute-done.13 = bf16[192,768]{1,0:T(8,128)(2,1)S(1)} collective-permute-done((bf16[192,768]{1,0:T(8,128)(2,1)S(1)}, bf16[192,768]{1,0:T(8,128)(2,1)S(1)}, u32[]{:S(2)}, u32[]{:S(2)}) %collective-permute-start.13) | collective-permute-done | bytes 294944 | tf_op jit(solution)/shard_map/ppermute | solution.py:29
  95.7 1.3 %collective-permute-start.14 = (bf16[192,768]{1,0:T(8,128)(2,1)S(1)}, bf16[192,768]{1,0:T(8,128)(2,1)S(1)}, u32[]{:S(2)}, u32[]{:S(2)}) collective-permute-start(bf16[192,768]{1,0:T(8,128)(2,1)S(1)} %fusion.57), channel_id=1, source_target_pairs={{8,0},{9,1},{10,2},{11,3},{4,12},{5,13},{6,14},{7,15},{24,16},{25,... | collective-permute-start | bytes 884744 | tf_op jit(solution)/shard_map/ppermute | solution.py:211
  97.0 1.5 %add_convert_fusion = bf16[512,768]{1,0:T(8,128)(2,1)} fusion(f32[512,768]{1,0:T(8,128)S(1)} %fusion.12, f32[512,768]{1,0:T(8,128)S(1)} %fusion.73, bf16[512,768]{1,0:T(8,128)(2,1)S(1)} %fusion.7, bf16[512,512]{1,0:T(8,128)(2,1)S(1)} %get-tuple-element.10), kind=kOutput, calls=%fused_computation.14 | convolution fusion | flops 404619264 | bytes 5242880 | tf_op jit(solution)/shard_map/dot_general | solution.py:18
  98.5 6.7 %collective-permute-done.14 = bf16[192,768]{1,0:T(8,128)(2,1)S(1)} collective-permute-done((bf16[192,768]{1,0:T(8,128)(2,1)S(1)}, bf16[192,768]{1,0:T(8,128)(2,1)S(1)}, u32[]{:S(2)}, u32[]{:S(2)}) %collective-permute-start.14) | collective-permute-done | bytes 294944 | tf_op jit(solution)/shard_map/ppermute | solution.py:211
  105.2 1.3 %add_select_fusion = f32[192,768]{1,0:T(8,128)} fusion(bf16[192,768]{1,0:T(8,128)(2,1)S(1)} %collective-permute-done.14, pred[]{:T(512)S(6)} %or.3, bf16[192,128]{1,0:T(8,128)(2,1)S(1)} %collective-permute-done.18, bf16[192,768]{1,0:T(8,128)(2,1)S(1)} %collective-permute-done.13, f32[1,1,192,768]{3,2,1,0:T(8,128)S(1)} %get-tuple-element.18, ...), kind=kOutput, calls=%fused_computation.58 | convolution fusion | flops 227893248 | bytes 2885120 | tf_op jit(solution)/shard_map/dot_general | solution.py:18
  (83 shorter events, 7.4 us)
Async XLA Ops:
  0.6 43.7 %copy-start = (bf16[768,1536]{1,0:T(8,128)(2,1)S(1)}, bf16[768,1536]{1,0:T(8,128)(2,1)}, u32[]{:S(2)}) copy-start(bf16[768,1536]{1,0:T(8,128)(2,1)} %param.29) | copy-start | bytes 7077892
  2.6 38.7 %collective-permute-start.1 = (bf16[256]{0:T(256)(128)(2,1)}, bf16[256]{0:T(256)(128)(2,1)}, u32[]{:S(2)}, u32[]{:S(2)}) collective-permute-start(bf16[256]{0:T(256)(128)(2,1)} %get-tuple-element.21), channel_id=1, source_target_pairs={{0,1},{1,2},{2,3},{3,4},{4,5},{5,6},{6,7},{7,8},{8,9},{9,10},{10,1... | collective-permute-start | bytes 1544 | tf_op jit(solution)/shard_map/ppermute | solution.py:34
  7.7 11.8 %collective-permute-start.3 = (bf16[8,896]{1,0:T(8,128)(2,1)S(1)}, bf16[8,896]{1,0:T(8,128)(2,1)S(1)}, u32[]{:S(2)}, u32[]{:S(2)}) collective-permute-start(bf16[8,896]{1,0:T(8,128)(2,1)S(1)} %fusion.61), channel_id=1, source_target_pairs={{0,1},{1,0},{2,3},{3,2},{4,5},{5,4},{6,7},{7,6},{8,9},{9,8},{10,11... | collective-permute-start | bytes 43016 | tf_op jit(solution)/shard_map/ppermute | solution.py:29
  13.4 6.0 %copy-start.10 = (f32[1536]{0:T(1024)S(1)}, f32[1536]{0:T(1024)}, u32[]{:S(2)}) copy-start(f32[1536]{0:T(1024)} %param.23) | copy-start | bytes 18436
  13.4 6.0 %copy-start.11 = (s32[1536]{0:T(1024)S(1)}, s32[1536]{0:T(1024)}, u32[]{:S(2)}) copy-start(s32[1536]{0:T(1024)} %param.21) | copy-start | bytes 18436
  13.4 6.0 %copy-start.12 = (s32[1536]{0:T(1024)S(1)}, s32[1536]{0:T(1024)}, u32[]{:S(2)}) copy-start(s32[1536]{0:T(1024)} %param.22) | copy-start | bytes 18436
  13.4 6.1 %copy-start.8 = (bf16[8,768]{1,0:T(8,128)(2,1)S(1)}, bf16[8,768]{1,0:T(8,128)(2,1)}, u32[]{:S(2)}) copy-start(bf16[8,768]{1,0:T(8,128)(2,1)} %param.18) | copy-start | bytes 36868
  14.3 30.6 %collective-permute-start = (bf16[256,768]{1,0:T(8,128)(2,1)}, bf16[256,768]{1,0:T(8,128)(2,1)}, u32[]{:S(2)}, u32[]{:S(2)}) collective-permute-start(bf16[256,768]{1,0:T(8,128)(2,1)} %get-tuple-element.28), channel_id=1, source_target_pairs={{1,0},{2,1},{3,2},{4,3},{5,4},{6,5},{7,6},{8,7},{9,8},{10,9},{11,1... | collective-permute-start | bytes 1179656 | tf_op jit(solution)/shard_map/ppermute | solution.py:34
  15.6 29.3 %collective-permute-start.2 = (bf16[256,768]{1,0:T(8,128)(2,1)}, bf16[256,768]{1,0:T(8,128)(2,1)}, u32[]{:S(2)}, u32[]{:S(2)}) collective-permute-start(bf16[256,768]{1,0:T(8,128)(2,1)} %get-tuple-element.29), channel_id=1, source_target_pairs={{0,1},{1,2},{2,3},{3,4},{4,5},{5,6},{6,7},{7,8},{8,9},{9,10},{10,1... | collective-permute-start | bytes 1179656 | tf_op jit(solution)/shard_map/ppermute | solution.py:34
  19.5 4.9 %collective-permute-start.4 = (bf16[16,896]{1,0:T(8,128)(2,1)S(1)}, bf16[16,896]{1,0:T(8,128)(2,1)S(1)}, u32[]{:S(2)}, u32[]{:S(2)}) collective-permute-start(bf16[16,896]{1,0:T(8,128)(2,1)S(1)} %pad_maximum_fusion.4), channel_id=1, source_target_pairs={{0,2},{1,3},{2,0},{3,1},{4,6},{5,7},{6,4},{7,5},{8,10},{9,11},{10,... | collective-permute-start | bytes 86024 | tf_op jit(solution)/shard_map/ppermute | solution.py:29
  24.4 8.7 %copy-start.7 = (bf16[16,896]{1,0:T(8,128)(2,1)}, bf16[16,896]{1,0:T(8,128)(2,1)S(1)}, u32[]{:S(2)}) copy-start(bf16[16,896]{1,0:T(8,128)(2,1)S(1)} %get-tuple-element.35) | copy-start | bytes 86020
  24.5 8.7 %collective-permute-start.5 = (bf16[32,896]{1,0:T(8,128)(2,1)S(1)}, bf16[32,896]{1,0:T(8,128)(2,1)}, u32[]{:S(2)}, u32[]{:S(2)}) collective-permute-start(bf16[32,896]{1,0:T(8,128)(2,1)S(1)} %pad_maximum_fusion.2), channel_id=1, source_target_pairs={{0,4},{1,5},{2,6},{3,7},{4,0},{5,1},{6,2},{7,3},{8,12},{9,13},{10,... | collective-permute-start | bytes 172040 | tf_op jit(solution)/shard_map/ppermute | solution.py:29
  34.7 5.8 %copy-start.13 = (f32[512]{0:T(512)S(1)}, f32[512]{0:T(512)}, u32[]{:S(2)}) copy-start(f32[512]{0:T(512)} %param.17) | copy-start | bytes 6148
  34.7 8.5 %collective-permute-start.6 = (bf16[64,896]{1,0:T(8,128)(2,1)}, bf16[64,896]{1,0:T(8,128)(2,1)}, u32[]{:S(2)}, u32[]{:S(2)}) collective-permute-start(bf16[64,896]{1,0:T(8,128)(2,1)} %pad_maximum_fusion.1), channel_id=1, source_target_pairs={{0,8},{1,9},{2,10},{3,11},{4,12},{5,13},{6,14},{7,15},{8,0},{9,1},... | collective-permute-start | bytes 344072 | tf_op jit(solution)/shard_map/ppermute | solution.py:29
  44.2 1.4 %copy-start.4 = (f32[512,768]{1,0:T(8,128)S(1)}, f32[512,768]{1,0:T(8,128)}, u32[]{:S(2)}) copy-start(f32[512,768]{1,0:T(8,128)} %get-tuple-element.41) | copy-start | bytes 4718596
  44.2 1.4 %copy-start.9 = (f32[256]{0:T(256)S(1)}, f32[256]{0:T(256)}, u32[]{:S(2)}) copy-start(f32[256]{0:T(256)} %get-tuple-element.20) | copy-start | bytes 3076
  46.9 1.1 %copy-start.3 = (bf16[512,768]{1,0:T(8,128)(2,1)S(1)}, bf16[512,768]{1,0:T(8,128)(2,1)}, u32[]{:S(2)}) copy-start(bf16[512,768]{1,0:T(8,128)(2,1)} %param.16) | copy-start | bytes 2359300
  46.9 1.6 %copy-start.5 = (f32[512,768]{1,0:T(8,128)S(1)}, f32[512,768]{1,0:T(8,128)}, u32[]{:S(2)}) copy-start(f32[512,768]{1,0:T(8,128)} %fusion.72) | copy-start | bytes 4718596
  48.6 1.3 %copy-start.15 = (bf16[768,768]{1,0:T(8,128)(2,1)S(1)}, bf16[768,768]{1,0:T(8,128)(2,1)}, u32[]{:S(2)}) copy-start(bf16[768,768]{1,0:T(8,128)(2,1)} %param.28) | copy-start | bytes 3538948
  49.8 0.9 copy-start.1
  49.8 1.2 %copy-start.2 = (bf16[512,768]{1,0:T(8,128)(2,1)S(1)}, bf16[512,768]{1,0:T(8,128)(2,1)}, u32[]{:S(2)}) copy-start(bf16[512,768]{1,0:T(8,128)(2,1)} %convolution_convert_fusion.1.grad_ref) | copy-start | bytes 2359300
  51.1 5.9 %copy-start.14 = (bf16[768,768]{1,0:T(8,128)(2,1)S(1)}, bf16[768,768]{1,0:T(8,128)(2,1)}, u32[]{:S(2)}) copy-start(bf16[768,768]{1,0:T(8,128)(2,1)} %param.30) | copy-start | bytes 3538948
  57.0 1.7 %copy-start.6 = (bf16[512,768]{1,0:T(8,128)(2,1)S(1)}, bf16[512,768]{1,0:T(8,128)(2,1)}, u32[]{:S(2)}) copy-start(bf16[512,768]{1,0:T(8,128)(2,1)} %param.31) | copy-start | bytes 2359300
  61.4 2.4 %collective-permute-start.15 = (bf16[2,2,192,128]{3,2,1,0:T(8,128)(2,1)S(1)}, bf16[2,2,192,128]{3,2,1,0:T(8,128)(2,1)S(1)}, u32[]{:S(2)}, u32[]{:S(2)}) collective-permute-start(bf16[2,2,192,128]{3,2,1,0:T(8,128)(2,1)S(1)} %fusion.47), channel_id=1, source_target_pairs={{0,1},{1,0},{2,3},{3,2},{4,5},{5,4},{6,7},{7,6},{8,9},{9,8},{10,11... | collective-permute-start | bytes 589832 | tf_op jit(solution)/shard_map/ppermute | solution.py:29
  61.6 7.5 %collective-permute-start.9 = (bf16[1,2,192,768]{3,2,1,0:T(8,128)(2,1)S(1)}, bf16[1,2,192,768]{3,2,1,0:T(8,128)(2,1)S(1)}, u32[]{:S(2)}, u32[]{:S(2)}) collective-permute-start(bf16[1,2,192,768]{3,2,1,0:T(8,128)(2,1)S(1)} %fusion.30), channel_id=1, source_target_pairs={{0,1},{1,0},{2,3},{3,2},{4,5},{5,4},{6,7},{7,6},{8,9},{9,8},{10,11... | collective-permute-start | bytes 1769480 | tf_op jit(solution)/shard_map/ppermute | solution.py:29
  63.9 4.8 %collective-permute-start.16 = (bf16[2,1,192,128]{3,2,0,1:T(8,128)(2,1)S(1)}, bf16[2,1,192,128]{3,2,0,1:T(8,128)(2,1)S(1)}, u32[]{:S(2)}, u32[]{:S(2)}) collective-permute-start(bf16[2,1,192,128]{3,2,0,1:T(8,128)(2,1)S(1)} %fusion.50), channel_id=1, source_target_pairs={{0,2},{1,3},{2,0},{3,1},{4,6},{5,7},{6,4},{7,5},{8,10},{9,11},{10,... | collective-permute-start | bytes 294920 | tf_op jit(solution)/shard_map/ppermute | solution.py:29
  64.1 6.5 %collective-permute-start.11 = (bf16[1,2,192,768]{3,2,1,0:T(8,128)(2,1)S(1)}, bf16[1,2,192,768]{3,2,1,0:T(8,128)(2,1)S(1)}, u32[]{:S(2)}, u32[]{:S(2)}) collective-permute-start(bf16[1,2,192,768]{3,2,1,0:T(8,128)(2,1)S(1)} %fusion.31), channel_id=1, source_target_pairs={{0,1},{1,0},{2,3},{3,2},{4,5},{5,4},{6,7},{7,6},{8,9},{9,8},{10,11... | collective-permute-start | bytes 1769480 | tf_op jit(solution)/shard_map/ppermute | solution.py:29
  68.7 7.4 %collective-permute-start.17 = (bf16[192,128]{1,0:T(8,128)(2,1)S(1)}, bf16[192,128]{1,0:T(8,128)(2,1)S(1)}, u32[]{:S(2)}, u32[]{:S(2)}) collective-permute-start(bf16[192,128]{1,0:T(8,128)(2,1)S(1)} %fusion.58), channel_id=1, source_target_pairs={{0,4},{1,5},{2,6},{3,7},{4,0},{5,1},{6,2},{7,3},{8,12},{9,13},{10,... | collective-permute-start | bytes 147464 | tf_op jit(solution)/shard_map/ppermute | solution.py:29
  69.3 13.0 %collective-permute-start.10 = (bf16[1,1,192,768]{3,2,1,0:T(8,128)(2,1)S(1)}, bf16[1,1,192,768]{3,2,1,0:T(8,128)(2,1)S(1)}, u32[]{:S(2)}, u32[]{:S(2)}) collective-permute-start(bf16[1,1,192,768]{3,2,1,0:T(8,128)(2,1)S(1)} %fusion.43), channel_id=1, source_target_pairs={{0,2},{1,3},{2,0},{3,1},{4,6},{5,7},{6,4},{7,5},{8,10},{9,11},{10,... | collective-permute-start | bytes 884744 | tf_op jit(solution)/shard_map/ppermute | solution.py:29
  70.9 17.7 %collective-permute-start.12 = (bf16[1,1,192,768]{3,2,1,0:T(8,128)(2,1)S(1)}, bf16[1,1,192,768]{3,2,1,0:T(8,128)(2,1)S(1)}, u32[]{:S(2)}, u32[]{:S(2)}) collective-permute-start(bf16[1,1,192,768]{3,2,1,0:T(8,128)(2,1)S(1)} %fusion.44), channel_id=1, source_target_pairs={{0,2},{1,3},{2,0},{3,1},{4,6},{5,7},{6,4},{7,5},{8,10},{9,11},{10,... | collective-permute-start | bytes 884744 | tf_op jit(solution)/shard_map/ppermute | solution.py:29
  71.8 18.1 %collective-permute-start.7 = (bf16[256,768]{1,0:T(8,128)(2,1)S(1)}, bf16[256,768]{1,0:T(8,128)(2,1)S(1)}, u32[]{:S(2)}, u32[]{:S(2)}) collective-permute-start(bf16[256,768]{1,0:T(8,128)(2,1)S(1)} %get-tuple-element.26), channel_id=1, source_target_pairs={{1,0},{2,1},{3,2},{4,3},{5,4},{6,5},{7,6},{8,7},{9,8},{10,9},{11,1... | collective-permute-start | bytes 1179656 | tf_op jit(solution)/shard_map/ppermute | solution.py:34
  73.1 16.8 %collective-permute-start.8 = (bf16[256,768]{1,0:T(8,128)(2,1)S(1)}, bf16[256,768]{1,0:T(8,128)(2,1)S(1)}, u32[]{:S(2)}, u32[]{:S(2)}) collective-permute-start(bf16[256,768]{1,0:T(8,128)(2,1)S(1)} %get-tuple-element.27), channel_id=1, source_target_pairs={{0,1},{1,2},{2,3},{3,4},{4,5},{5,6},{6,7},{7,8},{8,9},{9,10},{10,1... | collective-permute-start | bytes 1179656 | tf_op jit(solution)/shard_map/ppermute | solution.py:34
  76.2 22.4 %collective-permute-start.18 = (bf16[192,128]{1,0:T(8,128)(2,1)S(1)}, bf16[192,128]{1,0:T(8,128)(2,1)S(1)}, u32[]{:S(2)}, u32[]{:S(2)}) collective-permute-start(bf16[192,128]{1,0:T(8,128)(2,1)S(1)} %fusion.62), channel_id=1, source_target_pairs={{0,8},{1,9},{2,10},{3,11},{12,4},{13,5},{14,6},{15,7},{16,24},{17,... | collective-permute-start | bytes 147464 | tf_op jit(solution)/shard_map/ppermute | solution.py:210
  88.8 6.8 %collective-permute-start.13 = (bf16[192,768]{1,0:T(8,128)(2,1)S(1)}, bf16[192,768]{1,0:T(8,128)(2,1)S(1)}, u32[]{:S(2)}, u32[]{:S(2)}) collective-permute-start(bf16[192,768]{1,0:T(8,128)(2,1)S(1)} %get-tuple-element.17), channel_id=1, source_target_pairs={{0,4},{1,5},{2,6},{3,7},{4,0},{5,1},{6,2},{7,3},{8,12},{9,13},{10,... | collective-permute-start | bytes 884744 | tf_op jit(solution)/shard_map/ppermute | solution.py:29
  95.7 9.5 %collective-permute-start.14 = (bf16[192,768]{1,0:T(8,128)(2,1)S(1)}, bf16[192,768]{1,0:T(8,128)(2,1)S(1)}, u32[]{:S(2)}, u32[]{:S(2)}) collective-permute-start(bf16[192,768]{1,0:T(8,128)(2,1)S(1)} %fusion.57), channel_id=1, source_target_pairs={{8,0},{9,1},{10,2},{11,3},{4,12},{5,13},{6,14},{7,15},{24,16},{25,... | collective-permute-start | bytes 884744 | tf_op jit(solution)/shard_map/ppermute | solution.py:211

commit v2 on v1

--- a/solution.py
+++ b/solution.py
@@ -12,6 +12,7 @@
 HEADS = 12
 EPS = 1e-06
 MIB = 1 << 20
+MESH = pl.DeviceIdType.MESH
 
 
 def contract(left, right, left_dim, right_dim, precision=None):
@@ -36,8 +37,104 @@
     )
 
 
-def faces_kernel(first_ref, second_ref, high_ref, low_ref, inner_high_ref, inner_low_ref):
-    shape = (inner_high_ref.shape[0], first_ref.shape[1])
+def front_kernel(
+    count,
+    cells_ref,
+    first_ref,
+    second_ref,
+    high_ref,
+    low_ref,
+    cross_ref,
+    live_ref,
+    pack_ref,
+    mixed_ref,
+    normed_ref,
+    inverse_ref,
+    inner_high_ref,
+    inner_low_ref,
+    cross_map_ref,
+    weighted_map_ref,
+    gathered_ref,
+    own,
+    peer,
+    lower_live,
+    landed,
+    pack_send,
+    pack_recv,
+    face_send,
+    face_recv,
+):
+    me = lax.axis_index("blk")
+    slots = live_ref.shape[1]
+    cell_count = cells_ref.shape[0]
+    barrier = pltpu.get_barrier_semaphore()
+
+    def greet(step, carry):
+        pl.semaphore_signal(
+            barrier, inc=1, device_id={"blk": lax.rem(me + step, count)}, device_id_type=MESH
+        )
+        return carry
+
+    lax.fori_loop(1, count, greet, 0)
+    ids = lax.broadcasted_iota(jnp.int32, (cell_count, 2 * slots), 0)
+    cross_map = jnp.where(ids == cross_ref[...], 1.0, 0.0)
+    cross_map_ref[...] = cross_map.astype(jnp.bfloat16)
+    rows = cells_ref[...]
+    chosen = contract(cross_map_ref[...], rows, 0, 0)
+    own[0] = chosen[:slots].astype(jnp.bfloat16)
+    own[1] = chosen[slots:].astype(jnp.bfloat16)
+    pl.semaphore_wait(barrier, count - 1)
+
+    def sent(source, target, place, by):
+        return pltpu.make_async_remote_copy(
+            src_ref=source,
+            dst_ref=target,
+            send_sem=face_send.at[place],
+            recv_sem=face_recv.at[place],
+            device_id={"blk": lax.rem(me + by + count, count)},
+            device_id_type=MESH,
+        )
+
+    down = sent(own.at[1], peer.at[0], 0, -1)
+    up = sent(own.at[0], peer.at[1], 1, 1)
+    weights = sent(live_ref, lower_live, 2, 1)
+
+    @pl.when(me > 0)
+    def _():
+        down.start()
+
+    @pl.when(me < count - 1)
+    def _():
+        up.start()
+        weights.start()
+
+    def pack_copy(step, place):
+        return pltpu.make_async_remote_copy(
+            src_ref=pack_ref,
+            dst_ref=landed.at[place],
+            send_sem=pack_send.at[step],
+            recv_sem=pack_recv.at[place],
+            device_id={"blk": lax.rem(me + step, count)},
+            device_id_type=MESH,
+        )
+
+    def send_pack(step, carry):
+        pack_copy(step, me).start()
+        return carry
+
+    lax.fori_loop(1, count, send_pack, 0)
+    landed[me] = pack_ref[...]
+
+    @pl.when(me == 0)
+    def _():
+        peer[1] = jnp.zeros(peer.shape[1:], peer.dtype)
+        lower_live[...] = jnp.zeros_like(lower_live)
+
+    @pl.when(me == count - 1)
+    def _():
+        peer[0] = jnp.zeros(peer.shape[1:], peer.dtype)
+
+    shape = (cell_count, first_ref.shape[1])
     ids = lax.broadcasted_iota(jnp.int32, shape, 0)
     difference = jnp.where(ids == second_ref[...], 1.0, 0.0) - jnp.where(
         ids == first_ref[...], 1.0, 0.0
@@ -48,36 +145,108 @@
     high_part = (-total).astype(jnp.bfloat16)
     inner_high_ref[...] = high_part
     inner_low_ref[...] = (-total - high_part.astype(jnp.float32)).astype(jnp.bfloat16)
-
-
-def inner_faces(first, second, weight, cell_count):
+    inner = contract(inner_high_ref[...], rows, 1, 0) + contract(inner_low_ref[...], rows, 1, 0)
+
+    @pl.when(me < count - 1)
+    def _():
+        down.wait_recv()
+        up.wait_send()
+        weights.wait_send()
+
+    @pl.when(me > 0)
+    def _():
+        up.wait_recv()
+        weights.wait_recv()
+        down.wait_send()
+
+    live = jnp.concatenate([live_ref[...][:1], lower_live[...][:1]], axis=1)
+    weighted_map_ref[...] = (cross_map_ref[...].astype(jnp.float32) * live).astype(jnp.bfloat16)
+    flux = jnp.concatenate(
+        [
+            (peer[0].astype(jnp.float32) - own[0].astype(jnp.float32)).astype(jnp.bfloat16),
+            (peer[1].astype(jnp.float32) - own[1].astype(jnp.float32)).astype(jnp.bfloat16),
+        ],
+        axis=0,
+    )
+    mixed = (
+        rows.astype(jnp.float32) + inner + contract(weighted_map_ref[...], flux, 1, 0)
+    ).astype(jnp.bfloat16)
+    mixed_ref[...] = mixed
+    mixed = mixed.astype(jnp.float32)
+    inverse = lax.rsqrt(jnp.mean(mixed * mixed, axis=1, keepdims=True) + EPS)
+    inverse_ref[...] = inverse
+    normed_ref[...] = (mixed * inverse).astype(jnp.bfloat16)
+
+    def take_pack(step, carry):
+        pack_copy(step, lax.rem(me + count - step, count)).wait_recv()
+        pack_copy(step, me).wait_send()
+        return carry
+
+    lax.fori_loop(1, count, take_pack, 0)
+    gathered_ref[...] = landed[...]
+
+
+def front(cells, first, second, weight, cross_cells, live, pack):
+    count = lax.axis_size("blk")
+    cell_count = cells.shape[0]
+    slots = live.shape[0]
     high = lax.reduce_precision(weight, 8, 7)
-    matrix = jax.ShapeDtypeStruct((cell_count, cell_count), jnp.bfloat16)
-    slots = first.shape[0]
+    low_type = lambda *shape: jax.ShapeDtypeStruct(shape, jnp.bfloat16)
     return pl.pallas_call(
-        faces_kernel,
-        out_shape=(matrix, matrix),
-        compiler_params=pltpu.CompilerParams(vmem_limit_bytes=32 * MIB),
+        functools.partial(front_kernel, count),
+        in_specs=[pl.BlockSpec(memory_space=pltpu.VMEM)] * 8,
+        out_specs=[pl.BlockSpec(memory_space=pltpu.VMEM)] * 8,
+        out_shape=(
+            low_type(*cells.shape),
+            low_type(*cells.shape),
+            jax.ShapeDtypeStruct((cell_count, 1), jnp.float32),
+            low_type(cell_count, cell_count),
+            low_type(cell_count, cell_count),
+            low_type(cell_count, 2 * slots),
+            low_type(cell_count, 2 * slots),
+            low_type(count, *pack.shape),
+        ),
+        scratch_shapes=[
+            pltpu.VMEM((2, slots, cells.shape[1]), jnp.bfloat16),
+            pltpu.VMEM((2, slots, cells.shape[1]), jnp.bfloat16),
+            pltpu.VMEM((8, slots), jnp.float32),
+            pltpu.VMEM((count, *pack.shape), jnp.bfloat16),
+            pltpu.SemaphoreType.DMA((count,)),
+            pltpu.SemaphoreType.DMA((count,)),
+            pltpu.SemaphoreType.DMA((3,)),
+            pltpu.SemaphoreType.DMA((3,)),
+        ],
+        compiler_params=pltpu.CompilerParams(
+            collective_id=0, has_side_effects=True, vmem_limit_bytes=40 * MIB
+        ),
         cost_estimate=pl.CostEstimate(
-            flops=4 * slots * cell_count * cell_count,
-            bytes_accessed=4 * cell_count * cell_count,
+            flops=8 * first.shape[0] * cell_count * cell_count,
+            bytes_accessed=8 * cell_count * cell_count,
             transcendentals=0,
         ),
-    )(first[None, :], second[None, :], high[None, :], (weight - high)[None, :])
+    )(
+        cells,
+        first[None, :],
+        second[None, :],
+        high[None, :],
+        (weight - high)[None, :],
+        cross_cells[None, :],
+        jnp.broadcast_to(live[None, :], (8, slots)),
+        pack,
+    )
 
 
 def face_operator(rows, faces):
-    inner_high, inner_low, cross_map, upper_live, lower_live = faces
-    slots = upper_live.shape[0]
+    inner_high, inner_low, cross_map, weighted_map = faces
+    slots = cross_map.shape[1] // 2
     own = contract(cross_map, rows, 0, 0)
     own_low = own.astype(jnp.bfloat16)
     peer_lower = passed_along(own_low[slots:], -1)
     peer_upper = passed_along(own_low[:slots], 1)
     inner = contract(inner_high, rows, 1, 0) + contract(inner_low, rows, 1, 0)
-    upper_flux = upper_live[:, None] * (peer_lower.astype(jnp.float32) - own[:slots])
-    lower_flux = lower_live[:, None] * (peer_upper.astype(jnp.float32) - own[slots:])
-    flux = jnp.concatenate([upper_flux, lower_flux], axis=0).astype(jnp.bfloat16)
-    return inner + contract(cross_map, flux, 1, 0)
+    peers = jnp.concatenate([peer_lower, peer_upper], axis=0)
+    flux = (peers.astype(jnp.float32) - own).astype(jnp.bfloat16)
+    return inner + contract(weighted_map, flux, 1, 0)
 
 
 def attention_kernel(
@@ -161,19 +330,6 @@
     )(queries, grads, keyvals, keyvals, cell_code[:, None], anchor_code[None, :], dead[None, :])
 
 
-def gathered(rows):
-    me = lax.axis_index("blk")
-    bit = 1
-    while bit < lax.axis_size("blk"):
-        peer = exchanged(rows, bit)
-        upper = (me & bit) > 0
-        rows = jnp.concatenate(
-            [jnp.where(upper, peer, rows), jnp.where(upper, rows, peer)], axis=0
-        )
-        bit *= 2
-    return rows
-
-
 def halved(blocks, quarter):
     me = lax.axis_index("blk")
     bit = 1
@@ -231,37 +387,37 @@
     output_matrix,
     cotangent,
 ):
-    cell_count = cell_features.shape[0]
     own_anchors = anchor_token_features.shape[0]
     slot_index = jnp.arange(upper_face_cell.shape[0], dtype=jnp.int32)
-    live_weight = jnp.where(slot_index < upper_slot_count[0], upper_face_weight, 0).astype(
-        jnp.bfloat16
-    )
-    lower_live = passed_along(live_weight, 1).astype(jnp.float32)
+    live_weight = jnp.where(
+        slot_index < upper_slot_count[0], upper_face_weight.astype(jnp.float32), 0.0
+    )
     live = jnp.arange(own_anchors, dtype=jnp.int32) < live_anchor_count[0]
-    side = jnp.stack([anchor_geometry_rows, live.astype(jnp.bfloat16)], axis=1)
-    packed = gathered(
-        jnp.concatenate([anchor_token_features, jnp.pad(side, ((0, 0), (0, 126)))], axis=1)
-    )
-    tokens = packed[:, :MODEL_WIDTH]
-    anchor_code = packed[:, MODEL_WIDTH].astype(jnp.float32)
-    dead = jnp.where(packed[:, MODEL_WIDTH + 1] > 0, 0.0, -jnp.inf).astype(jnp.float32)
-
-    cell_ids = jnp.arange(cell_count, dtype=jnp.int32)
-    cross_cells = jnp.concatenate([upper_face_cell, lower_face_cell])
-    cross_map = (cell_ids[:, None] == cross_cells[None, :]).astype(jnp.bfloat16)
-    faces = inner_faces(inner_face_first, inner_face_second, inner_face_weight, cell_count) + (
-        cross_map,
-        live_weight.astype(jnp.float32),
-        lower_live,
-    )
-    mixed_rows = (
-        cell_features.astype(jnp.float32) + face_operator(cell_features, faces)
-    ).astype(jnp.bfloat16)
-    mixed_f = lax.optimization_barrier(mixed_rows).astype(jnp.float32)
-    inverse_rms = lax.rsqrt(jnp.mean(mixed_f * mixed_f, axis=1, keepdims=True) + EPS)
+    side = jnp.concatenate([anchor_geometry_rows, live.astype(jnp.bfloat16)])
+    half_width = MODEL_WIDTH // 2
+    pack = jnp.concatenate(
+        [
+            anchor_token_features.reshape(2 * own_anchors, half_width),
+            jnp.broadcast_to(side[:, None], (2 * own_anchors, 128)),
+        ],
+        axis=1,
+    )
+    mixed_rows, normed, inverse_rms, inner_high, inner_low, cross_map, weighted_map, packed = front(
+        cell_features,
+        inner_face_first,
+        inner_face_second,
+        inner_face_weight,
+        jnp.concatenate([upper_face_cell, lower_face_cell]),
+        live_weight,
+        pack,
+    )
+    faces = (inner_high, inner_low, cross_map, weighted_map)
+    tokens = packed[:, :, :half_width].reshape(-1, MODEL_WIDTH)
+    anchor_code = packed[:, :own_anchors, half_width].reshape(-1).astype(jnp.float32)
+    dead = jnp.where(packed[:, own_anchors:, half_width] > 0, 0.0, -jnp.inf)
+    dead = dead.reshape(-1).astype(jnp.float32)
+    mixed_f = mixed_rows.astype(jnp.float32)
     normal_hat = mixed_f * inverse_rms
-    normed = normal_hat.astype(jnp.bfloat16)
     queries = contract(normed, query_matrix, 1, 0).astype(jnp.bfloat16)
     keyvals = contract(tokens, anchor_keyvalue_matrix, 1, 0).astype(jnp.bfloat16)
     attended_gradient = contract(cotangent, output_matrix, 1, 1).astype(jnp.bfloat16)

time: 107 us -> 116 us (1.084)
  starting transfers between devices: 34.3 us -> 18.2 us
  Pallas kernels: 8.03 us -> 22.4 us
  local copies, waits for them, and re-layouts: 4.51 us -> 14.7 us
  waiting for transfers between devices: 26.7 us -> 19.6 us
  other arithmetic: 10 us -> 16.4 us
    pallas_call x1, Pallas kernels: 2.11 us -> 16.5 us  [front(): pl.pallas_call(functools.partial(front_kernel, count), in_specs=[pl.Block...]
    ppermute x12 -> x8, starting transfers between devices: 16 us -> 8.7 us  [exchanged(): return lax.ppermute(shard, 'blk', [(i, i ^ bit) for i in range(count)])]
    ppermute x5 -> x2, starting transfers between devices: 12.3 us -> 5.21 us  [passed_along(): lax.ppermute(shard, 'blk', [(i, i + by) for i in range(count) if 0 <= i +...]
    unnamed x33 -> x70, local copies, waits for them, and re-layouts: 2.62 us -> 9.71 us
    ppermute x12 -> x8, waiting for transfers between devices: 20 us -> 13.6 us  [exchanged(): return lax.ppermute(shard, 'blk', [(i, i ^ bit) for i in range(count)])]
    reshape x3, other arithmetic: 0.41 us -> 4.25 us  [halved(): paired = blocks.reshape(shape[0], shape[1] // 2, 2, shape[2], shape[3])]
    convert_element_type x6, other arithmetic: 0.39 us -> 2.82 us  [halved(): jnp.where(upper, paired[:, :, 0], paired[:, :, 1]).astype(jnp.bfloat16)]
    another operation x3 -> x0, other arithmetic: 2.22 us -> none
  transfers between devices with their start and end apart: 19 -> 12, of which waited for: 7 -> 4; matrix products, arithmetic and copies ran while one was open for 21% -> 25% of each run, Pallas kernels for 2% -> 0%
where the time goes in v2:
time: 116 us; the launch traced here: 115 us
  Pallas kernels  22.4 us (19%)
  matrix products  21.4 us (18%)
  waiting for transfers between devices  19.6 us (17%)
  starting transfers between devices  18.2 us (16%)
  other arithmetic  16.4 us (14%)
  local copies, waits for them, and re-layouts  14.7 us (13%)
  between operations  2.52 us (2%)
    dot_general x12, matrix products, contract(): lax.dot_general(left, right, (((left_dim,), (right_dim,)), ((), ())), pre...  21.4 us
    pallas_call x1, Pallas kernels, front(): pl.pallas_call(functools.partial(front_kernel, count), in_specs=[pl.Block...  16.5 us
    ppermute x8, waiting for transfers between devices, exchanged(): return lax.ppermute(shard, 'blk', [(i, i ^ bit) for i in range(count)])  13.6 us
    unnamed x70, local copies, waits for them, and re-layouts  9.71 us
    ppermute x8, starting transfers between devices, exchanged(): return lax.ppermute(shard, 'blk', [(i, i ^ bit) for i in range(count)])  8.7 us
    ppermute x1, waiting for transfers between devices, summed_weight_grads(): lax.ppermute(block.astype(jnp.bfloat16), 'blk', outward).astype(jnp.float32)  5.96 us
    pallas_call x1, Pallas kernels, attention(): pl.pallas_call(functools.partial(attention_kernel, 1.0 / math.sqrt(MODEL_...  5.89 us
    ppermute x2, starting transfers between devices, passed_along(): lax.ppermute(shard, 'blk', [(i, i + by) for i in range(count) if 0 <= i +...  5.21 us
  transfers between devices with their start and end apart: 12, of which 4 were waited for; matrix products, arithmetic and copies ran while one was open for 25% of the time, Pallas kernels for 0%

profile of v2, /device:TPU:0, one launch (start us, length us, event | category | flops | bytes accessed | tf_op | source)
XLA Modules:
  0.0 115.2 jit_solution(9471117361396505395)
XLA Ops:
  4.9 0.7 pad_maximum_fusion.2
  7.1 1.1 copy-done.18
  8.3 16.5 %shard_map.175 = (bf16[512,768]{1,0:T(8,128)(2,1)S(1)}, bf16[512,768]{1,0:T(8,128)(2,1)S(1)}, f32[512,1]{1,0:T(8,128)S(1)}, bf16[512,512]{1,0:T(8,128)(2,1)S(1)}...) custom-call(bf16[512,768]{1,0:T(8,128)(2,1)S(1)} %copy-done.18, ...), custom_call_target="tpu_custom_call" | custom-call | flops 3221225472 | bytes 2097152 | tf_op jit(solution)/shard_map/pallas_call | solution.py:195
  24.8 0.9 copy-done.4
  25.7 0.8 copy-done.8
  26.5 0.8 copy-done.10
  27.3 0.8 copy-done.12
  28.1 0.8 copy-done.14
  29.6 0.8 select_reduce_fusion
  30.5 0.9 copy.35.cell_code_ref
  31.4 0.8 select_n.237.dead_ref
  32.3 2.3 %convolution_convert_fusion.1.grad_ref = bf16[512,768]{1,0:T(8,128)(2,1)S(1)} fusion(bf16[512,768]{1,0:T(8,128)(2,1)} %param.31, bf16[768,768]{1,0:T(8,128)(2,1)} %param.30), kind=kOutput, calls=%fused_computation.13 | convolution fusion | flops 604372992 | bytes 2752512 | tf_op jit(solution)/shard_map/dot_general | solution.py:19
  35.2 0.8 copy-done.33
  35.9 0.8 convolution_convert_fusion.2.query_ref
  36.9 5.9 %shard_map.176 = (bf16[512,768]{1,0:T(8,128)(2,1)S(1)}, bf16[512,768]{1,0:T(8,128)(2,1)S(1)}, f32[768,128]{1,0:T(8,128)S(1)}, f32[768,128]{1,0:T(8,128)S(1)}) custom-call(bf16[512,768]{1,0:T(8,128)(2,1)S(1)} %convolution_convert_fusion.2.query_ref, bf16[512,768]{1,0:T(8,128)(2,1)S(1)} %convolution_convert_fusion.1.grad_ref, ...), custom_call_target="tpu_custom_call" | custom-call | flops 1207959552 | bytes 3145728 | tf_op jit(solution)/shard_map/pallas_call | solution.py:313
  42.8 0.8 fusion.22
  43.7 2.5 %collective-permute-start.8 = (bf16[2,2,192,128]{3,2,1,0:T(8,128)(2,1)}, bf16[2,2,192,128]{3,2,1,0:T(8,128)(2,1)}, u32[]{:S(2)}, u32[]{:S(2)}) collective-permute-start(bf16[2,2,192,128]{3,2,1,0:T(8,128)(2,1)} %fusion.22), channel_id=1, source_target_pairs={{0,1},{1,0},{2,3},{3,2},{4,5},{5,4},{6,7},{7,6},{8,9},{9,8},{10,11... | collective-permute-start | bytes 589832 | tf_op jit(solution)/shard_map/ppermute | solution.py:30
  46.2 0.8 fusion.40
  47.1 0.9 fusion.13
  48.7 0.8 fusion.41
  49.6 1.4 %copy-done.19 = f32[768,768]{1,0:T(8,128)} copy-done((f32[768,768]{1,0:T(8,128)}, f32[768,768]{1,0:T(8,128)S(1)}, u32[]{:S(2)}) %copy-start.19) | copy-done | bytes 2359320
  51.0 0.9 fusion.14
  51.9 1.1 reduce.2
  53.0 2.7 %fusion.2 = (f32[512]{0:T(512)S(1)}, f32[512,768]{1,0:T(8,128)S(1)}) fusion(bf16[512,768]{1,0:T(8,128)(2,1)} %copy-done.4, f32[512]{0:T(512)S(1)} %reduce.2, bf16[512,768]{1,0:T(8,128)(2,1)} %copy-done.1, bf16[768,768]{1,0:T(8,128)(2,1)} %param.28), kind=kOutput, calls=%fused_computation.5 | convolution fusion | flops 605552128 | bytes 4329472 | tf_op jit(solution)/shard_map/dot_general | solution.py:19
  56.9 1.8 %fusion.37 = (bf16[512,768]{1,0:T(8,128)(2,1)S(1)}, f32[512,768]{1,0:T(8,128)}) fusion(bf16[512,512]{1,0:T(8,128)(2,1)S(1)} %copy-done.9, bf16[512,768]{1,0:T(8,128)(2,1)S(1)} %fusion.6), kind=kOutput, calls=%fused_computation.76 | convolution fusion | flops 403046400 | bytes 3670016 | tf_op jit(solution)/shard_map/dot_general | solution.py:19
  58.7 0.9 fusion.36
  59.6 1.3 %collective-permute-start = (bf16[256,768]{1,0:T(8,128)(2,1)}, bf16[256,768]{1,0:T(8,128)(2,1)}, u32[]{:S(2)}, u32[]{:S(2)}) collective-permute-start(bf16[256,768]{1,0:T(8,128)(2,1)} %get-tuple-element.32), channel_id=1, source_target_pairs={{1,0},{2,1},{3,2},{4,3},{5,4},{6,5},{7,6},{8,7},{9,8},{10,9},{11,1... | collective-permute-start | bytes 1179656 | tf_op jit(solution)/shard_map/ppermute | solution.py:35
  60.9 3.9 %collective-permute-start.1 = (bf16[256,768]{1,0:T(8,128)(2,1)}, bf16[256,768]{1,0:T(8,128)(2,1)}, u32[]{:S(2)}, u32[]{:S(2)}) collective-permute-start(bf16[256,768]{1,0:T(8,128)(2,1)} %get-tuple-element.33), channel_id=1, source_target_pairs={{0,1},{1,2},{2,3},{3,4},{4,5},{5,6},{6,7},{7,8},{8,9},{9,10},{10,1... | collective-permute-start | bytes 1179656 | tf_op jit(solution)/shard_map/ppermute | solution.py:35
  64.8 1.7 %fusion.7 = bf16[512,768]{1,0:T(8,128)(2,1)} fusion(bf16[512,768]{1,0:T(8,128)(2,1)S(1)} %copy-done.5, bf16[512,768]{1,0:T(8,128)(2,1)S(1)} %get-tuple-element.18, bf16[768,768]{1,0:T(8,128)(2,1)S(1)} %copy-done.34), kind=kOutput, calls=%fused_computation.10 | convolution fusion | flops 605159424 | bytes 3538944 | tf_op jit(solution)/shard_map/dot_general | solution.py:19
  66.5 1.7 %fusion.39 = f32[512,768]{1,0:T(8,128)} fusion(bf16[512,512]{1,0:T(8,128)(2,1)S(1)} %copy-done.13, bf16[512,768]{1,0:T(8,128)(2,1)S(1)} %fusion.6), kind=kOutput, calls=%fused_computation.78 | convolution fusion | flops 402653184 | bytes 2883584 | tf_op jit(solution)/shard_map/dot_general | solution.py:19
  68.3 1.0 fusion.18
  69.3 2.4 %collective-permute-start.9 = (bf16[2,1,192,128]{3,2,0,1:T(8,128)(2,1)S(1)}, bf16[2,1,192,128]{3,2,0,1:T(8,128)(2,1)S(1)}, u32[]{:S(2)}, u32[]{:S(2)}) collective-permute-start(bf16[2,1,192,128]{3,2,0,1:T(8,128)(2,1)S(1)} %fusion.25), channel_id=1, source_target_pairs={{0,2},{1,3},{2,0},{3,1},{4,6},{5,7},{6,4},{7,5},{8,10},{9,11},{10,... | collective-permute-start | bytes 294920 | tf_op jit(solution)/shard_map/ppermute | solution.py:30
  71.7 2.0 %fusion.9 = f32[1,1,2,192,768]{4,3,2,1,0:T(8,128)S(1)} fusion(bf16[1,2,192,768]{3,2,1,0:T(8,128)(2,1)} %collective-permute-done.2, f32[1,2,2,192,768]{4,3,2,1,0:T(8,128)} %bitcast.180, pred[]{:T(512)S(6)} %gt.31), kind=kLoop, calls=%fused_computation.22 | loop fusion | flops 884736 | bytes 4128769 | tf_op jit(solution)/shard_map/reshape | solution.py:338
  74.0 1.3 %fusion.8 = f32[1,1,2,192,768]{4,3,2,1,0:T(8,128)S(1)} fusion(bf16[1,2,192,768]{3,2,1,0:T(8,128)(2,1)} %collective-permute-done.4, f32[1,2,2,192,768]{4,3,2,1,0:T(8,128)S(1)} %bitcast.178, pred[]{:T(512)S(6)} %gt.31), kind=kLoop, calls=%fused_computation.20 | loop fusion | flops 884736 | bytes 4128769 | tf_op jit(solution)/shard_map/reshape | solution.py:338
  75.3 1.9 %collective-permute-start.5 = (bf16[1,1,192,768]{3,2,1,0:T(8,128)(2,1)S(1)}, bf16[1,1,192,768]{3,2,1,0:T(8,128)(2,1)S(1)}, u32[]{:S(2)}, u32[]{:S(2)}) collective-permute-start(bf16[1,1,192,768]{3,2,1,0:T(8,128)(2,1)S(1)} %fusion.20), channel_id=1, source_target_pairs={{0,2},{1,3},{2,0},{3,1},{4,6},{5,7},{6,4},{7,5},{8,10},{9,11},{10,... | collective-permute-start | bytes 884744 | tf_op jit(solution)/shard_map/ppermute | solution.py:30
  78.7 4.1 %collective-permute-done.3 = bf16[1,1,192,768]{3,2,1,0:T(8,128)(2,1)S(1)} collective-permute-done((bf16[1,1,192,768]{3,2,1,0:T(8,128)(2,1)S(1)}, bf16[1,1,192,768]{3,2,1,0:T(8,128)(2,1)S(1)}, u32[]{:S(2)}, u32[]{:S(2)}) %collective-permute-start.3) | collective-permute-done | bytes 294944 | tf_op jit(solution)/shard_map/ppermute | solution.py:30
  82.8 6.3 %collective-permute-done.5 = bf16[1,1,192,768]{3,2,1,0:T(8,128)(2,1)S(1)} collective-permute-done((bf16[1,1,192,768]{3,2,1,0:T(8,128)(2,1)S(1)}, bf16[1,1,192,768]{3,2,1,0:T(8,128)(2,1)S(1)}, u32[]{:S(2)}, u32[]{:S(2)}) %collective-permute-start.5) | collective-permute-done | bytes 294944 | tf_op jit(solution)/shard_map/ppermute | solution.py:30
  89.1 1.1 fusion.21
  90.3 0.9 collective-permute-start.6
  91.2 1.7 %fusion.38 = f32[512,768]{1,0:T(8,128)} fusion(bf16[512,512]{1,0:T(8,128)(2,1)S(1)} %copy-done.11, bf16[512,768]{1,0:T(8,128)(2,1)S(1)} %copy-done.23), kind=kOutput, calls=%fused_computation.77 | convolution fusion | flops 402653184 | bytes 2883584 | tf_op jit(solution)/shard_map/dot_general | solution.py:19
  92.9 1.1 fusion.34
  94.0 3.0 %collective-permute-start.11 = (bf16[192,128]{1,0:T(8,128)(2,1)S(1)}, bf16[192,128]{1,0:T(8,128)(2,1)S(1)}, u32[]{:S(2)}, u32[]{:S(2)}) collective-permute-start(bf16[192,128]{1,0:T(8,128)(2,1)S(1)} %fusion.34), channel_id=1, source_target_pairs={{0,8},{1,9},{2,10},{3,11},{12,4},{13,5},{14,6},{15,7},{16,24},{17,... | collective-permute-start | bytes 147464 | tf_op jit(solution)/shard_map/ppermute | solution.py:366
  97.0 3.2 %collective-permute-done.6 = bf16[192,768]{1,0:T(8,128)(2,1)} collective-permute-done((bf16[192,768]{1,0:T(8,128)(2,1)}, bf16[192,768]{1,0:T(8,128)(2,1)}, u32[]{:S(2)}, u32[]{:S(2)}) %collective-permute-start.6) | collective-permute-done | bytes 294944 | tf_op jit(solution)/shard_map/ppermute | solution.py:30
  100.2 1.2 %fusion.32 = bf16[192,768]{1,0:T(8,128)(2,1)S(1)} fusion(bf16[192,768]{1,0:T(8,128)(2,1)} %collective-permute-done.6, f32[1,1,192,768]{3,2,1,0:T(8,128)S(1)} %get-tuple-element.30, f32[1,1,192,768]{3,2,1,0:T(8,128)} %get-tuple-element.31, pred[]{:T(512)S(6)} %gt.29), kind=kLoop, calls=%fused_computation.62 | loop fusion | flops 589824 | bytes 1769473 | tf_op jit(solution)/shard_map/convert_element_type | solution.py:367
  101.4 1.3 %collective-permute-start.7 = (bf16[192,768]{1,0:T(8,128)(2,1)S(1)}, bf16[192,768]{1,0:T(8,128)(2,1)S(1)}, u32[]{:S(2)}, u32[]{:S(2)}) collective-permute-start(bf16[192,768]{1,0:T(8,128)(2,1)S(1)} %fusion.32), channel_id=1, source_target_pairs={{8,0},{9,1},{10,2},{11,3},{4,12},{5,13},{6,14},{7,15},{24,16},{25,... | collective-permute-start | bytes 884744 | tf_op jit(solution)/shard_map/ppermute | solution.py:367
  102.8 4.2 %add_convert_fusion = bf16[512,768]{1,0:T(8,128)(2,1)} fusion(f32[512,768]{1,0:T(8,128)} %fusion.38, f32[512,768]{1,0:T(8,128)} %fusion.39, bf16[512,768]{1,0:T(8,128)(2,1)S(1)} %copy-done.24, bf16[512,512]{1,0:T(8,128)(2,1)S(1)} %copy-done.15, f32[512,768]{1,0:T(8,128)} %get-tuple-element.39, bf16[256,768]{1,0:T(8,128)(2,1)} %collective-permute-done.1, ...), kind=kOutput, calls=%fused_computation.11 | convolution fusion | flops 406978560 | bytes 7602176 | tf_op jit(solution)/shard_map/dot_general | solution.py:19
  107.0 6.0 %collective-permute-done.7 = bf16[192,768]{1,0:T(8,128)(2,1)S(1)} collective-permute-done((bf16[192,768]{1,0:T(8,128)(2,1)S(1)}, bf16[192,768]{1,0:T(8,128)(2,1)S(1)}, u32[]{:S(2)}, u32[]{:S(2)}) %collective-permute-start.7) | collective-permute-done | bytes 294944 | tf_op jit(solution)/shard_map/ppermute | solution.py:367
  113.0 2.2 %add_select_fusion = f32[192,768]{1,0:T(8,128)} fusion(bf16[192,768]{1,0:T(8,128)(2,1)S(1)} %collective-permute-done.7, pred[]{:T(512)S(6)} %or.3, bf16[128,768]{1,0:T(8,128)(2,1)S(1)} %copy-done.31, bf16[192,128]{1,0:T(8,128)(2,1)S(1)} %collective-permute-done.11, bf16[192,768]{1,0:T(8,128)(2,1)} %collective-permute-done.6, ...), kind=kOutput, calls=%fused_computation.35 | convolution fusion | flops 227500032 | bytes 2852352 | tf_op jit(solution)/shard_map/dot_general | solution.py:19
  (97 shorter events, 9.6 us)
Async XLA Ops:
  0.6 34.0 %copy-start = (bf16[768,1536]{1,0:T(8,128)(2,1)S(1)}, bf16[768,1536]{1,0:T(8,128)(2,1)}, u32[]{:S(2)}) copy-start(bf16[768,1536]{1,0:T(8,128)(2,1)} %param.29) | copy-start | bytes 7077892
  7.1 1.1 copy-start.18
  8.3 22.2 %copy-start.32 = (f32[512]{0:T(512)S(1)}, f32[512]{0:T(512)}, u32[]{:S(2)}) copy-start(f32[512]{0:T(512)} %param.17) | copy-start | bytes 6148
  24.8 0.9 copy-start.4
  25.7 0.8 copy-start.8
  26.5 0.8 copy-start.10
  27.3 0.8 copy-start.12
  28.1 0.8 copy-start.14
  28.9 0.7 copy-start.16
  29.6 5.6 %copy-start.6 = (bf16[512,768]{1,0:T(8,128)(2,1)}, bf16[512,768]{1,0:T(8,128)(2,1)S(1)}, u32[]{:S(2)}) copy-start(bf16[512,768]{1,0:T(8,128)(2,1)S(1)} %get-tuple-element.16) | copy-start | bytes 2359300
  31.4 3.2 %copy-start.30 = (bf16[128,768]{1,0:T(8,128)(2,1)}, bf16[128,768]{1,0:T(8,128)(2,1)S(1)}, u32[]{:S(2)}) copy-start(bf16[128,768]{1,0:T(8,128)(2,1)S(1)} %reshape.326) | copy-start | bytes 589828
  34.7 1.3 %copy-start.33 = (bf16[768,768]{1,0:T(8,128)(2,1)S(1)}, bf16[768,768]{1,0:T(8,128)(2,1)}, u32[]{:S(2)}) copy-start(bf16[768,768]{1,0:T(8,128)(2,1)} %param.28) | copy-start | bytes 3538948
  35.9 0.9 copy-start.17
  36.9 9.3 %copy-start.26 = (bf16[512,768]{1,0:T(8,128)(2,1)S(1)}, bf16[512,768]{1,0:T(8,128)(2,1)}, u32[]{:S(2)}) copy-start(bf16[512,768]{1,0:T(8,128)(2,1)} %param.31) | copy-start | bytes 2359300
  42.8 4.2 %copy-start.2 = (f32[768,128]{1,0:T(8,128)}, f32[768,128]{1,0:T(8,128)S(1)}, u32[]{:S(2)}) copy-start(f32[768,128]{1,0:T(8,128)S(1)} %get-tuple-element.26) | copy-start | bytes 1179652
  42.8 5.9 %copy-start.1 = (bf16[512,768]{1,0:T(8,128)(2,1)}, bf16[512,768]{1,0:T(8,128)(2,1)S(1)}, u32[]{:S(2)}) copy-start(bf16[512,768]{1,0:T(8,128)(2,1)S(1)} %get-tuple-element.20) | copy-start | bytes 2359300
  43.7 24.6 %collective-permute-start.8 = (bf16[2,2,192,128]{3,2,1,0:T(8,128)(2,1)}, bf16[2,2,192,128]{3,2,1,0:T(8,128)(2,1)}, u32[]{:S(2)}, u32[]{:S(2)}) collective-permute-start(bf16[2,2,192,128]{3,2,1,0:T(8,128)(2,1)} %fusion.22), channel_id=1, source_target_pairs={{0,1},{1,0},{2,3},{3,2},{4,5},{5,4},{6,7},{7,6},{8,9},{9,8},{10,11... | collective-permute-start | bytes 589832 | tf_op jit(solution)/shard_map/ppermute | solution.py:30
  47.0 1.6 %copy-start.21 = (f32[768,768]{0,1:T(8,128)}, f32[768,768]{0,1:T(8,128)S(1)}, u32[]{:S(2)}) copy-start(f32[768,768]{0,1:T(8,128)S(1)} %fusion.40) | copy-start | bytes 7077892
  47.0 1.7 %copy-start.7 = (bf16[512,768]{1,0:T(8,128)(2,1)S(1)}, bf16[512,768]{1,0:T(8,128)(2,1)}, u32[]{:S(2)}) copy-start(bf16[512,768]{1,0:T(8,128)(2,1)} %copy-done.6) | copy-start | bytes 2359300
  48.0 23.7 %collective-permute-start.2 = (bf16[1,2,192,768]{3,2,1,0:T(8,128)(2,1)}, bf16[1,2,192,768]{3,2,1,0:T(8,128)(2,1)}, u32[]{:S(2)}, u32[]{:S(2)}) collective-permute-start(bf16[1,2,192,768]{3,2,1,0:T(8,128)(2,1)} %fusion.13), channel_id=1, source_target_pairs={{0,1},{1,0},{2,3},{3,2},{4,5},{5,4},{6,7},{7,6},{8,9},{9,8},{10,11... | collective-permute-start | bytes 1769480 | tf_op jit(solution)/shard_map/ppermute | solution.py:30
  49.6 1.4 %copy-start.19 = (f32[768,768]{1,0:T(8,128)}, f32[768,768]{1,0:T(8,128)S(1)}, u32[]{:S(2)}) copy-start(f32[768,768]{1,0:T(8,128)S(1)} %fusion.41) | copy-start | bytes 7077892
  51.9 22.0 %collective-permute-start.4 = (bf16[1,2,192,768]{3,2,1,0:T(8,128)(2,1)}, bf16[1,2,192,768]{3,2,1,0:T(8,128)(2,1)}, u32[]{:S(2)}, u32[]{:S(2)}) collective-permute-start(bf16[1,2,192,768]{3,2,1,0:T(8,128)(2,1)} %fusion.14), channel_id=1, source_target_pairs={{0,1},{1,0},{2,3},{3,2},{4,5},{5,4},{6,7},{7,6},{8,9},{9,8},{10,11... | collective-permute-start | bytes 1769480 | tf_op jit(solution)/shard_map/ppermute | solution.py:30
  53.0 2.8 %copy-start.5 = (bf16[512,768]{1,0:T(8,128)(2,1)S(1)}, bf16[512,768]{1,0:T(8,128)(2,1)}, u32[]{:S(2)}) copy-start(bf16[512,768]{1,0:T(8,128)(2,1)} %copy-done.4) | copy-start | bytes 2359300
  53.0 2.8 %copy-start.27 = (bf16[512,768]{1,0:T(8,128)(2,1)S(1)}, bf16[512,768]{1,0:T(8,128)(2,1)}, u32[]{:S(2)}) copy-start(bf16[512,768]{1,0:T(8,128)(2,1)} %param.31) | copy-start | bytes 2359300
  55.8 1.0 copy-start.9
  56.3 10.2 %copy-start.22 = (bf16[512,768]{1,0:T(8,128)(2,1)}, bf16[512,768]{1,0:T(8,128)(2,1)S(1)}, u32[]{:S(2)}) copy-start(bf16[512,768]{1,0:T(8,128)(2,1)S(1)} %fusion.6) | copy-start | bytes 2359300
  58.7 6.2 %copy-start.34 = (bf16[768,768]{1,0:T(8,128)(2,1)S(1)}, bf16[768,768]{1,0:T(8,128)(2,1)}, u32[]{:S(2)}) copy-start(bf16[768,768]{1,0:T(8,128)(2,1)} %param.30) | copy-start | bytes 3538948
  59.6 43.1 %collective-permute-start = (bf16[256,768]{1,0:T(8,128)(2,1)}, bf16[256,768]{1,0:T(8,128)(2,1)}, u32[]{:S(2)}, u32[]{:S(2)}) collective-permute-start(bf16[256,768]{1,0:T(8,128)(2,1)} %get-tuple-element.32), channel_id=1, source_target_pairs={{1,0},{2,1},{3,2},{4,3},{5,4},{6,5},{7,6},{8,7},{9,8},{10,9},{11,1... | collective-permute-start | bytes 1179656 | tf_op jit(solution)/shard_map/ppermute | solution.py:35
  60.9 5.6 %copy-start.13 = (bf16[512,512]{1,0:T(8,128)(2,1)S(1)}, bf16[512,512]{1,0:T(8,128)(2,1)}, u32[]{:S(2)}) copy-start(bf16[512,512]{1,0:T(8,128)(2,1)} %copy-done.12) | copy-start | bytes 1572868
  60.9 41.8 %collective-permute-start.1 = (bf16[256,768]{1,0:T(8,128)(2,1)}, bf16[256,768]{1,0:T(8,128)(2,1)}, u32[]{:S(2)}, u32[]{:S(2)}) collective-permute-start(bf16[256,768]{1,0:T(8,128)(2,1)} %get-tuple-element.33), channel_id=1, source_target_pairs={{0,1},{1,2},{2,3},{3,4},{4,5},{5,6},{6,7},{7,8},{8,9},{9,10},{10,1... | collective-permute-start | bytes 1179656 | tf_op jit(solution)/shard_map/ppermute | solution.py:35
  66.5 1.8 %copy-start.3 = (f32[768,128]{1,0:T(8,128)S(1)}, f32[768,128]{1,0:T(8,128)}, u32[]{:S(2)}) copy-start(f32[768,128]{1,0:T(8,128)} %copy-done.2) | copy-start | bytes 1179652
  69.3 4.7 %copy-start.20 = (f32[768,768]{1,0:T(8,128)S(1)}, f32[768,768]{1,0:T(8,128)}, u32[]{:S(2)}) copy-start(f32[768,768]{1,0:T(8,128)} %copy-done.19) | copy-start | bytes 7077892
  69.3 7.9 %collective-permute-start.9 = (bf16[2,1,192,128]{3,2,0,1:T(8,128)(2,1)S(1)}, bf16[2,1,192,128]{3,2,0,1:T(8,128)(2,1)S(1)}, u32[]{:S(2)}, u32[]{:S(2)}) collective-permute-start(bf16[2,1,192,128]{3,2,0,1:T(8,128)(2,1)S(1)} %fusion.25), channel_id=1, source_target_pairs={{0,2},{1,3},{2,0},{3,1},{4,6},{5,7},{6,4},{7,5},{8,10},{9,11},{10,... | collective-permute-start | bytes 294920 | tf_op jit(solution)/shard_map/ppermute | solution.py:30
  73.7 9.1 %collective-permute-start.3 = (bf16[1,1,192,768]{3,2,1,0:T(8,128)(2,1)S(1)}, bf16[1,1,192,768]{3,2,1,0:T(8,128)(2,1)S(1)}, u32[]{:S(2)}, u32[]{:S(2)}) collective-permute-start(bf16[1,1,192,768]{3,2,1,0:T(8,128)(2,1)S(1)} %fusion.19), channel_id=1, source_target_pairs={{0,2},{1,3},{2,0},{3,1},{4,6},{5,7},{6,4},{7,5},{8,10},{9,11},{10,... | collective-permute-start | bytes 884744 | tf_op jit(solution)/shard_map/ppermute | solution.py:30
  75.3 13.8 %collective-permute-start.5 = (bf16[1,1,192,768]{3,2,1,0:T(8,128)(2,1)S(1)}, bf16[1,1,192,768]{3,2,1,0:T(8,128)(2,1)S(1)}, u32[]{:S(2)}, u32[]{:S(2)}) collective-permute-start(bf16[1,1,192,768]{3,2,1,0:T(8,128)(2,1)S(1)} %fusion.20), channel_id=1, source_target_pairs={{0,2},{1,3},{2,0},{3,1},{4,6},{5,7},{6,4},{7,5},{8,10},{9,11},{10,... | collective-permute-start | bytes 884744 | tf_op jit(solution)/shard_map/ppermute | solution.py:30
  77.3 5.5 %copy-start.28 = (f32[2,1,192,128]{3,2,0,1:T(8,128)}, f32[2,1,192,128]{3,2,0,1:T(8,128)S(1)}, u32[]{:S(2)}) copy-start(f32[2,1,192,128]{3,2,0,1:T(8,128)S(1)} %fusion.24) | copy-start | bytes 589828
  78.0 13.2 %copy-start.11 = (bf16[512,512]{1,0:T(8,128)(2,1)S(1)}, bf16[512,512]{1,0:T(8,128)(2,1)}, u32[]{:S(2)}) copy-start(bf16[512,512]{1,0:T(8,128)(2,1)} %copy-done.10) | copy-start | bytes 1572868
  78.0 13.2 %copy-start.23 = (bf16[512,768]{1,0:T(8,128)(2,1)S(1)}, bf16[512,768]{1,0:T(8,128)(2,1)}, u32[]{:S(2)}) copy-start(bf16[512,768]{1,0:T(8,128)(2,1)} %copy-done.22) | copy-start | bytes 2359300
  78.0 14.9 %collective-permute-start.10 = (bf16[192,128]{1,0:T(8,128)(2,1)}, bf16[192,128]{1,0:T(8,128)(2,1)S(1)}, u32[]{:S(2)}, u32[]{:S(2)}) collective-permute-start(bf16[192,128]{1,0:T(8,128)(2,1)} %fusion.33), channel_id=1, source_target_pairs={{0,4},{1,5},{2,6},{3,7},{4,0},{5,1},{6,2},{7,3},{8,12},{9,13},{10,... | collective-permute-start | bytes 147464 | tf_op jit(solution)/shard_map/ppermute | solution.py:30
  90.3 9.9 %collective-permute-start.6 = (bf16[192,768]{1,0:T(8,128)(2,1)}, bf16[192,768]{1,0:T(8,128)(2,1)}, u32[]{:S(2)}, u32[]{:S(2)}) collective-permute-start(bf16[192,768]{1,0:T(8,128)(2,1)} %get-tuple-element.29), channel_id=1, source_target_pairs={{0,4},{1,5},{2,6},{3,7},{4,0},{5,1},{6,2},{7,3},{8,12},{9,13},{10,... | collective-permute-start | bytes 884744 | tf_op jit(solution)/shard_map/ppermute | solution.py:30
  92.9 9.8 %copy-start.15 = (bf16[512,512]{1,0:T(8,128)(2,1)S(1)}, bf16[512,512]{1,0:T(8,128)(2,1)}, u32[]{:S(2)}) copy-start(bf16[512,512]{1,0:T(8,128)(2,1)} %copy-done.14) | copy-start | bytes 1572868
  92.9 9.8 %copy-start.24 = (bf16[512,768]{1,0:T(8,128)(2,1)S(1)}, bf16[512,768]{1,0:T(8,128)(2,1)}, u32[]{:S(2)}) copy-start(bf16[512,768]{1,0:T(8,128)(2,1)} %copy-done.22) | copy-start | bytes 2359300
  94.0 13.0 %collective-permute-start.11 = (bf16[192,128]{1,0:T(8,128)(2,1)S(1)}, bf16[192,128]{1,0:T(8,128)(2,1)S(1)}, u32[]{:S(2)}, u32[]{:S(2)}) collective-permute-start(bf16[192,128]{1,0:T(8,128)(2,1)S(1)} %fusion.34), channel_id=1, source_target_pairs={{0,8},{1,9},{2,10},{3,11},{12,4},{13,5},{14,6},{15,7},{16,24},{17,... | collective-permute-start | bytes 147464 | tf_op jit(solution)/shard_map/ppermute | solution.py:366
  101.4 11.5 %collective-permute-start.7 = (bf16[192,768]{1,0:T(8,128)(2,1)S(1)}, bf16[192,768]{1,0:T(8,128)(2,1)S(1)}, u32[]{:S(2)}, u32[]{:S(2)}) collective-permute-start(bf16[192,768]{1,0:T(8,128)(2,1)S(1)} %fusion.32), channel_id=1, source_target_pairs={{8,0},{9,1},{10,2},{11,3},{4,12},{5,13},{6,14},{7,15},{24,16},{25,... | collective-permute-start | bytes 884744 | tf_op jit(solution)/shard_map/ppermute | solution.py:367
  102.8 10.2 %copy-start.25 = (f32[1,1,192,768]{3,2,1,0:T(8,128)S(1)}, f32[1,1,192,768]{3,2,1,0:T(8,128)}, u32[]{:S(2)}) copy-start(f32[1,1,192,768]{3,2,1,0:T(8,128)} %get-tuple-element.31) | copy-start | bytes 1769476
  102.8 10.2 %copy-start.29 = (f32[2,1,192,128]{3,2,0,1:T(8,128)S(1)}, f32[2,1,192,128]{3,2,0,1:T(8,128)}, u32[]{:S(2)}) copy-start(f32[2,1,192,128]{3,2,0,1:T(8,128)} %copy-done.28) | copy-start | bytes 589828
  102.8 10.2 %copy-start.31 = (bf16[128,768]{1,0:T(8,128)(2,1)S(1)}, bf16[128,768]{1,0:T(8,128)(2,1)}, u32[]{:S(2)}) copy-start(bf16[128,768]{1,0:T(8,128)(2,1)} %copy-done.30) | copy-start | bytes 589828

commit v3 on v2

--- a/solution.py
+++ b/solution.py
@@ -40,12 +40,8 @@
 def front_kernel(
     count,
     cells_ref,
-    first_ref,
-    second_ref,
-    high_ref,
-    low_ref,
+    inner_ref,
     cross_ref,
-    live_ref,
     pack_ref,
     mixed_ref,
     normed_ref,
@@ -65,7 +61,8 @@
     face_recv,
 ):
     me = lax.axis_index("blk")
-    slots = live_ref.shape[1]
+    slots = cross_ref.shape[1] // 2
+    live_ref = cross_ref.at[:, pl.ds(0, slots)]
     cell_count = cells_ref.shape[0]
     barrier = pltpu.get_barrier_semaphore()
 
@@ -77,7 +74,7 @@
 
     lax.fori_loop(1, count, greet, 0)
     ids = lax.broadcasted_iota(jnp.int32, (cell_count, 2 * slots), 0)
-    cross_map = jnp.where(ids == cross_ref[...], 1.0, 0.0)
+    cross_map = jnp.where(ids == cross_ref[...][:1].astype(jnp.int32), 1.0, 0.0)
     cross_map_ref[...] = cross_map.astype(jnp.bfloat16)
     rows = cells_ref[...]
     chosen = contract(cross_map_ref[...], rows, 0, 0)
@@ -134,14 +131,16 @@
     def _():
         peer[0] = jnp.zeros(peer.shape[1:], peer.dtype)
 
-    shape = (cell_count, first_ref.shape[1])
-    ids = lax.broadcasted_iota(jnp.int32, shape, 0)
-    difference = jnp.where(ids == second_ref[...], 1.0, 0.0) - jnp.where(
-        ids == first_ref[...], 1.0, 0.0
-    )
+    inner_rows = inner_ref[...]
+    first, second = inner_rows[:1].astype(jnp.int32), inner_rows[1:2].astype(jnp.int32)
+    weight = inner_rows[2:3]
+    weight_high = weight.astype(jnp.bfloat16).astype(jnp.float32)
+    weight_low = weight - weight_high
+    ids = lax.broadcasted_iota(jnp.int32, (cell_count, inner_ref.shape[1]), 0)
+    difference = jnp.where(ids == second, 1.0, 0.0) - jnp.where(ids == first, 1.0, 0.0)
     low = difference.astype(jnp.bfloat16)
-    total = contract((difference * high_ref[...]).astype(jnp.bfloat16), low, 1, 1)
-    total = total + contract((difference * low_ref[...]).astype(jnp.bfloat16), low, 1, 1)
+    total = contract((difference * weight_high).astype(jnp.bfloat16), low, 1, 1)
+    total = total + contract((difference * weight_low).astype(jnp.bfloat16), low, 1, 1)
     high_part = (-total).astype(jnp.bfloat16)
     inner_high_ref[...] = high_part
     inner_low_ref[...] = (-total - high_part.astype(jnp.float32)).astype(jnp.bfloat16)
@@ -159,7 +158,9 @@
         weights.wait_recv()
         down.wait_send()
 
-    live = jnp.concatenate([live_ref[...][:1], lower_live[...][:1]], axis=1)
+    live = jnp.concatenate(
+        [cross_ref[...][1:2, :slots], lower_live[...][1:2]], axis=1
+    )
     weighted_map_ref[...] = (cross_map_ref[...].astype(jnp.float32) * live).astype(jnp.bfloat16)
     flux = jnp.concatenate(
         [
@@ -190,11 +191,27 @@
     count = lax.axis_size("blk")
     cell_count = cells.shape[0]
     slots = live.shape[0]
-    high = lax.reduce_precision(weight, 8, 7)
+    inner_table = jnp.concatenate(
+        [
+            first.astype(jnp.float32)[None, :],
+            second.astype(jnp.float32)[None, :],
+            weight[None, :],
+            jnp.zeros((5, first.shape[0]), jnp.float32),
+        ],
+        axis=0,
+    )
+    cross_table = jnp.concatenate(
+        [
+            cross_cells.astype(jnp.float32)[None, :],
+            jnp.pad(live, (0, slots))[None, :],
+            jnp.zeros((6, 2 * slots), jnp.float32),
+        ],
+        axis=0,
+    )
     low_type = lambda *shape: jax.ShapeDtypeStruct(shape, jnp.bfloat16)
     return pl.pallas_call(
         functools.partial(front_kernel, count),
-        in_specs=[pl.BlockSpec(memory_space=pltpu.VMEM)] * 8,
+        in_specs=[pl.BlockSpec(memory_space=pltpu.VMEM)] * 4,
         out_specs=[pl.BlockSpec(memory_space=pltpu.VMEM)] * 8,
         out_shape=(
             low_type(*cells.shape),
@@ -217,7 +234,7 @@
             pltpu.SemaphoreType.DMA((3,)),
         ],
         compiler_params=pltpu.CompilerParams(
-            collective_id=0, has_side_effects=True, vmem_limit_bytes=40 * MIB
+            collective_id=0, has_side_effects=True, vmem_limit_bytes=20 * MIB
         ),
         cost_estimate=pl.CostEstimate(
             flops=8 * first.shape[0] * cell_count * cell_count,
@@ -226,27 +243,10 @@
         ),
     )(
         cells,
-        first[None, :],
-        second[None, :],
-        high[None, :],
-        (weight - high)[None, :],
-        cross_cells[None, :],
-        jnp.broadcast_to(live[None, :], (8, slots)),
+        inner_table,
+        cross_table,
         pack,
     )
-
-
-def face_operator(rows, faces):
-    inner_high, inner_low, cross_map, weighted_map = faces
-    slots = cross_map.shape[1] // 2
-    own = contract(cross_map, rows, 0, 0)
-    own_low = own.astype(jnp.bfloat16)
-    peer_lower = passed_along(own_low[slots:], -1)
-    peer_upper = passed_along(own_low[:slots], 1)
-    inner = contract(inner_high, rows, 1, 0) + contract(inner_low, rows, 1, 0)
-    peers = jnp.concatenate([peer_lower, peer_upper], axis=0)
-    flux = (peers.astype(jnp.float32) - own).astype(jnp.bfloat16)
-    return inner + contract(weighted_map, flux, 1, 0)
 
 
 def attention_kernel(
@@ -309,7 +309,7 @@
     values = pl.BlockSpec((anchors, wide), lambda i: (0, i + pairs))
     turned = pl.BlockSpec((wide, anchors), lambda i: (i, 0))
     fixed = lambda shape: pl.BlockSpec(shape, lambda i: (0, 0))
-    limit = min(56 * MIB, 16 * MIB + 64 * cells * anchors)
+    limit = min(56 * MIB, 8 * MIB + 64 * cells * anchors)
     return pl.pallas_call(
         functools.partial(attention_kernel, 1.0 / math.sqrt(MODEL_WIDTH // HEADS)),
         grid=(pairs,),
@@ -330,43 +330,257 @@
     )(queries, grads, keyvals, keyvals, cell_code[:, None], anchor_code[None, :], dead[None, :])
 
 
-def halved(blocks, quarter):
-    me = lax.axis_index("blk")
-    bit = 1
-    while bit < quarter:
-        shape = blocks.shape
-        paired = blocks.reshape(shape[0], shape[1] // 2, 2, shape[2], shape[3])
-        upper = (me & bit) > 0
-        sent = jnp.where(upper, paired[:, :, 0], paired[:, :, 1]).astype(jnp.bfloat16)
-        kept = jnp.where(upper, paired[:, :, 1], paired[:, :, 0])
-        blocks = kept + exchanged(sent, bit).astype(jnp.float32)
-        bit *= 2
-    return blocks[:, 0]
-
-
-def summed_weight_grads(query_part, pair_left, output_part, tokens):
-    count = lax.axis_size("blk")
+def tail_kernel(
+    count,
+    cotangent_ref,
+    attended_ref,
+    grad_query_ref,
+    normed_ref,
+    mixed_ref,
+    inverse_ref,
+    query_matrix_ref,
+    inner_high_ref,
+    inner_low_ref,
+    cross_map_ref,
+    weighted_map_ref,
+    grad_key_ref,
+    grad_value_ref,
+    tokens_ref,
+    cell_grads_ref,
+    weight_grads_ref,
+    query_sum,
+    output_sum,
+    key_sum,
+    value_sum,
+    own,
+    peer,
+    face_send,
+    face_recv,
+    sum_send,
+    sum_recv,
+    *buffers,
+):
     me = lax.axis_index("blk")
     quarter = count // 4
     rows = 4 * MODEL_WIDTH // count
-    output_block = halved(output_part.reshape(1, quarter, rows, MODEL_WIDTH), quarter)[0]
-    pair_blocks = halved(pair_left.reshape(2, quarter, rows, -1), quarter)
-    query_block = halved(query_part.reshape(1, quarter, rows, MODEL_WIDTH), quarter)[0]
-    place = me // quarter
-    odd = place % 2 > 0
-    pair_sent = jnp.where(odd, pair_blocks[1], pair_blocks[0]).astype(jnp.bfloat16)
-    pair_kept = jnp.where(odd, pair_blocks[0], pair_blocks[1])
-    pair = pair_kept + exchanged(pair_sent, quarter).astype(jnp.float32)
-    sent = jnp.where(odd, query_block, output_block).astype(jnp.bfloat16)
-    kept = jnp.where(odd, output_block, query_block)
-    block = kept + exchanged(sent, quarter).astype(jnp.float32)
-    inward = [(i, i + 2 * quarter) for i in range(quarter)]
-    inward += [(i, i - 2 * quarter) for i in range(3 * quarter, count)]
-    outward = [(to, start) for start, to in inward]
-    pair = pair + lax.ppermute(pair.astype(jnp.bfloat16), "blk", inward).astype(jnp.float32)
-    block = block + lax.ppermute(block.astype(jnp.bfloat16), "blk", outward).astype(jnp.float32)
-    product = contract(pair, tokens.astype(jnp.float32), 1, 0, lax.Precision.HIGHEST)
-    return jnp.where((place == 0) | (place == 3), block, product)
+    slots = own.shape[1]
+    stages = quarter.bit_length() - 1
+    place = lax.div(me, quarter)
+    barrier = pltpu.get_barrier_semaphore()
+
+    def greet(step, carry):
+        pl.semaphore_signal(
+            barrier, inc=1, device_id={"blk": lax.rem(me + step, count)}, device_id_type=MESH
+        )
+        return carry
+
+    lax.fori_loop(1, count, greet, 0)
+
+    def upper_bit(bit):
+        return lax.rem(lax.div(me, bit), 2)
+
+    def copy(source, target, place_in_sems, bit):
+        return pltpu.make_async_remote_copy(
+            src_ref=source,
+            dst_ref=target,
+            send_sem=sum_send.at[place_in_sems],
+            recv_sem=sum_recv.at[place_in_sems],
+            device_id={"blk": me + bit - 2 * bit * upper_bit(bit)},
+            device_id_type=MESH,
+        )
+
+    def send(stage, kind, total):
+        half = quarter >> (stage + 1)
+        bit = 1 << stage
+        upper = upper_bit(bit)
+        out, into = buffers[8 * stage + 2 * kind], buffers[8 * stage + 2 * kind + 1]
+        for i in range(half):
+            out[i] = total[2 * i + 1 - upper].astype(jnp.bfloat16)
+            total[i] = total[2 * i + upper]
+        moved = copy(out, into, 4 * stage + kind, bit)
+        moved.start()
+
+        def take():
+            moved.wait()
+            for i in range(half):
+                total[i] = total[i] + into[i].astype(jnp.float32)
+
+        return take
+
+    totals = (output_sum, query_sum, key_sum, value_sum)
+    shape = (quarter, rows, MODEL_WIDTH)
+    output_sum[...] = contract(cotangent_ref[...], attended_ref[...], 0, 0).reshape(shape)
+    key_sum[...] = grad_key_ref[...].reshape(key_sum.shape)
+    value_sum[...] = grad_value_ref[...].reshape(value_sum.shape)
+    pl.semaphore_wait(barrier, count - 1)
+    waits = [send(0, 0, output_sum)]
+    query_sum[...] = contract(grad_query_ref[...], normed_ref[...], 0, 0).reshape(shape)
+    waits += [send(0, kind, totals[kind]) for kind in range(1, 4)]
+
+    grad_normed = contract(grad_query_ref[...], query_matrix_ref[...], 1, 1)
+    inverse = inverse_ref[...]
+    normal_hat = mixed_ref[...].astype(jnp.float32) * inverse
+    grad_mixed = (
+        cotangent_ref[...].astype(jnp.float32)
+        + inverse
+        * (grad_normed - normal_hat * jnp.mean(grad_normed * normal_hat, axis=1, keepdims=True))
+    ).astype(jnp.bfloat16)
+    cell_grads_ref[...] = grad_mixed
+    chosen = contract(cross_map_ref[...], grad_mixed, 0, 0)
+    own[0] = chosen[:slots].astype(jnp.bfloat16)
+    own[1] = chosen[slots:].astype(jnp.bfloat16)
+
+    def sent(source, target, number, by):
+        return pltpu.make_async_remote_copy(
+            src_ref=source,
+            dst_ref=target,
+            send_sem=face_send.at[number],
+            recv_sem=face_recv.at[number],
+            device_id={"blk": lax.rem(me + by + count, count)},
+            device_id_type=MESH,
+        )
+
+    down = sent(own.at[1], peer.at[0], 0, -1)
+    up = sent(own.at[0], peer.at[1], 1, 1)
+
+    for stage in range(1, stages):
+        following = []
+        for kind in range(4):
+            waits[kind]()
+            following.append(send(stage, kind, totals[kind]))
+        waits = following
+
+    @pl.when(me > 0)
+    def _():
+        down.start()
+
+    @pl.when(me < count - 1)
+    def _():
+        up.start()
+
+    @pl.when(me == 0)
+    def _():
+        peer[1] = jnp.zeros(peer.shape[1:], peer.dtype)
+
+    @pl.when(me == count - 1)
+    def _():
+        peer[0] = jnp.zeros(peer.shape[1:], peer.dtype)
+
+    result = (
+        cell_grads_ref[...].astype(jnp.float32)
+        + contract(inner_high_ref[...], cell_grads_ref[...], 1, 0)
+        + contract(inner_low_ref[...], cell_grads_ref[...], 1, 0)
+    )
+    for take in waits:
+        take()
+    wide_out, wide_in, pair_out, pair_in, last_out, last_in, last_pair_out, last_pair_in = buffers[
+        8 * stages :
+    ]
+    odd = lax.rem(place, 2) > 0
+    wide_out[...] = jnp.where(odd, query_sum[0], output_sum[0]).astype(jnp.bfloat16)
+    pair_out[...] = jnp.where(odd, value_sum[0], key_sum[0]).astype(jnp.bfloat16)
+    wide = copy(wide_out, wide_in, 4 * stages, quarter)
+    pair = copy(pair_out, pair_in, 4 * stages + 1, quarter)
+    wide.start()
+    pair.start()
+    wide_kept = jnp.where(odd, output_sum[0], query_sum[0])
+    pair_kept = jnp.where(odd, key_sum[0], value_sum[0])
+
+    @pl.when(me < count - 1)
+    def _():
+        down.wait_recv()
+        up.wait_send()
+
+    @pl.when(me > 0)
+    def _():
+        up.wait_recv()
+        down.wait_send()
+
+    flux = jnp.concatenate(
+        [
+            (peer[0].astype(jnp.float32) - own[0].astype(jnp.float32)).astype(jnp.bfloat16),
+            (peer[1].astype(jnp.float32) - own[1].astype(jnp.float32)).astype(jnp.bfloat16),
+        ],
+        axis=0,
+    )
+    wide.wait()
+    pair.wait()
+    query_sum[0] = wide_kept + wide_in[...].astype(jnp.float32)
+    key_sum[0] = pair_kept + pair_in[...].astype(jnp.float32)
+    last = copy(last_out, last_in, 4 * stages + 2, 2 * quarter)
+    last_pair = copy(last_pair_out, last_pair_in, 4 * stages + 3, 2 * quarter)
+    outer = lax.rem(place + 1, 4) < 2
+    inside = lax.rem(place + 1, 4) >= 2
+
+    @pl.when(inside)
+    def _():
+        last_out[...] = query_sum[0].astype(jnp.bfloat16)
+        last.start()
+
+    @pl.when(outer)
+    def _():
+        last_pair_out[...] = key_sum[0].astype(jnp.bfloat16)
+        last_pair.start()
+
+    cell_grads_ref[...] = (result + contract(weighted_map_ref[...], flux, 1, 0)).astype(jnp.bfloat16)
+
+    @pl.when(inside)
+    def _():
+        last_pair.wait_recv()
+        total = key_sum[0] + last_pair_in[...].astype(jnp.float32)
+        weight_grads_ref[...] = contract(
+            total, tokens_ref[...].astype(jnp.float32), 1, 0, lax.Precision.HIGHEST
+        )
+        last.wait_send()
+
+    @pl.when(outer)
+    def _():
+        last.wait_recv()
+        weight_grads_ref[...] = query_sum[0] + last_in[...].astype(jnp.float32)
+        last_pair.wait_send()
+
+
+def tail(*operands):
+    count = lax.axis_size("blk")
+    cells = operands[0].shape
+    anchors = operands[-1].shape[0]
+    slots = operands[9].shape[1] // 2
+    quarter = count // 4
+    rows = 4 * MODEL_WIDTH // count
+    stages = quarter.bit_length() - 1
+    low = lambda *shape: pltpu.VMEM(shape, jnp.bfloat16)
+    full = lambda *shape: pltpu.VMEM(shape, jnp.float32)
+    buffers = []
+    for stage in range(stages):
+        half = quarter >> (stage + 1)
+        buffers += [low(half, rows, MODEL_WIDTH)] * 4 + [low(half, rows, anchors)] * 4
+    buffers += ([low(rows, MODEL_WIDTH)] * 2 + [low(rows, anchors)] * 2) * 2
+    vmem = pl.BlockSpec(memory_space=pltpu.VMEM)
+    return pl.pallas_call(
+        functools.partial(tail_kernel, count),
+        in_specs=[vmem] * len(operands),
+        out_specs=[vmem] * 2,
+        out_shape=(
+            jax.ShapeDtypeStruct(cells, jnp.bfloat16),
+            jax.ShapeDtypeStruct((rows, MODEL_WIDTH), jnp.float32),
+        ),
+        scratch_shapes=[
+            full(quarter, rows, MODEL_WIDTH),
+            full(quarter, rows, MODEL_WIDTH),
+            full(quarter, rows, anchors),
+            full(quarter, rows, anchors),
+            low(2, slots, MODEL_WIDTH),
+            low(2, slots, MODEL_WIDTH),
+            pltpu.SemaphoreType.DMA((2,)),
+            pltpu.SemaphoreType.DMA((2,)),
+            pltpu.SemaphoreType.DMA((4 * stages + 4,)),
+            pltpu.SemaphoreType.DMA((4 * stages + 4,)),
+        ]
+        + buffers,
+        compiler_params=pltpu.CompilerParams(
+            collective_id=1, has_side_effects=True, vmem_limit_bytes=48 * MIB
+        ),
+    )(*operands)
 
 
 def shards(
@@ -411,36 +625,35 @@
         live_weight,
         pack,
     )
-    faces = (inner_high, inner_low, cross_map, weighted_map)
     tokens = packed[:, :, :half_width].reshape(-1, MODEL_WIDTH)
     anchor_code = packed[:, :own_anchors, half_width].reshape(-1).astype(jnp.float32)
     dead = jnp.where(packed[:, own_anchors:, half_width] > 0, 0.0, -jnp.inf)
     dead = dead.reshape(-1).astype(jnp.float32)
-    mixed_f = mixed_rows.astype(jnp.float32)
-    normal_hat = mixed_f * inverse_rms
     queries = contract(normed, query_matrix, 1, 0).astype(jnp.bfloat16)
     keyvals = contract(tokens, anchor_keyvalue_matrix, 1, 0).astype(jnp.bfloat16)
     attended_gradient = contract(cotangent, output_matrix, 1, 1).astype(jnp.bfloat16)
     attended, grad_queries, grad_keys, grad_values = attention(
         queries, attended_gradient, keyvals, cell_geometry_rows, anchor_code, dead
     )
-    grad_normed = contract(grad_queries, query_matrix, 1, 1)
-    grad_mixed = (
-        cotangent.astype(jnp.float32)
-        + inverse_rms
-        * (grad_normed - normal_hat * jnp.mean(grad_normed * normal_hat, axis=1, keepdims=True))
+    cell_grads, weight_grads = tail(
+        cotangent,
+        attended,
+        grad_queries,
+        normed,
+        mixed_rows,
+        inverse_rms,
+        query_matrix,
+        inner_high,
+        inner_low,
+        cross_map,
+        weighted_map,
+        grad_keys,
+        grad_values,
+        tokens,
+    )
+    layer_output = (
+        mixed_rows.astype(jnp.float32) + contract(attended, output_matrix, 1, 0)
     ).astype(jnp.bfloat16)
-    grad_mixed = lax.optimization_barrier(grad_mixed)
-    weight_grads = summed_weight_grads(
-        contract(grad_queries, normed, 0, 0),
-        jnp.stack([grad_keys, grad_values]),
-        contract(cotangent, attended, 0, 0),
-        tokens,
-    )
-    cell_grads = (grad_mixed.astype(jnp.float32) + face_operator(grad_mixed, faces)).astype(
-        jnp.bfloat16
-    )
-    layer_output = (mixed_f + contract(attended, output_matrix, 1, 0)).astype(jnp.bfloat16)
     return (layer_output, cell_grads, weight_grads)
 
 

time: 116 us -> 99.3 us (0.86)
  Pallas kernels: 22.4 us -> 73.6 us
  waiting for transfers between devices: 19.6 us -> 0 us
  starting transfers between devices: 18.2 us -> 0 us
  matrix products: 21.4 us -> 6.19 us
  other arithmetic: 16.4 us -> 3.75 us
  local copies, waits for them, and re-layouts: 14.7 us -> 12.9 us
    pallas_call x0 -> x1, Pallas kernels: none -> 51.1 us  [tail(): pl.pallas_call(functools.partial(tail_kernel, count), in_specs=[vmem] * l...]
    ppermute x12 -> x0, waiting for transfers between devices: 19.6 us -> none  [the longest x8 13.6 us: exchanged(): return lax.ppermute(shard, 'blk', [(i, i ^ bit) for i in range(count)])]
    ppermute x12 -> x0, starting transfers between devices: 18.2 us -> none  [the longest x8 8.7 us: exchanged(): return lax.ppermute(shard, 'blk', [(i, i ^ bit) for i in range(count)])]
    dot_general x12 -> x4, matrix products: 21.4 us -> 6.19 us  [contract(): lax.dot_general(left, right, (((left_dim,), (right_dim,)), ((), ())), pre...]
    convert_element_type x11 -> x3, other arithmetic: 7.4 us -> 2.1 us  [the longest x1 0.7 us: front(): cross_cells.astype(jnp.float32)[None, :]]
    reshape x3 -> x0, other arithmetic: 4.25 us -> none  [halved(): paired = blocks.reshape(shape[0], shape[1] // 2, 2, shape[2], shape[3])]
    unnamed x70 -> x48, local copies, waits for them, and re-layouts: 9.71 us -> 9.49 us
  transfers between devices with their start and end apart: 12 -> 0, of which waited for: 4 -> 0; matrix products, arithmetic and copies ran while one was open for 25% -> 0% of each run, Pallas kernels for 0% -> 0%
where the time goes in v3:
time: 99.3 us; the launch traced here: 98.8 us
  Pallas kernels  73.6 us (74%)
  local copies, waits for them, and re-layouts  12.9 us (13%)
  matrix products  6.19 us (6%)
  other arithmetic  3.75 us (4%)
  between operations  2.31 us (2%)
    pallas_call x1, Pallas kernels, tail(): pl.pallas_call(functools.partial(tail_kernel, count), in_specs=[vmem] * l...  51.1 us
    pallas_call x1, Pallas kernels, front(): pl.pallas_call(functools.partial(front_kernel, count), in_specs=[pl.Block...  16.6 us
    unnamed x48, local copies, waits for them, and re-layouts  9.49 us
    dot_general x4, matrix products, contract(): lax.dot_general(left, right, (((left_dim,), (right_dim,)), ((), ())), pre...  6.19 us
    pallas_call x1, Pallas kernels, attention(): pl.pallas_call(functools.partial(attention_kernel, 1.0 / math.sqrt(MODEL_...  5.91 us

profile of v3, /device:TPU:0, one launch (start us, length us, event | category | flops | bytes accessed | tf_op | source)
XLA Modules:
  0.0 98.8 jit_solution(13054764938894719069)
XLA Ops:
  0.6 0.0 copy-start
  2.1 0.7 pad_maximum_fusion.1
  2.8 0.7 compare_select_fusion
  3.5 0.1 pad.11.clone
  3.6 0.1 pad.17.clone
  3.7 0.7 add_convert_fusion.1
  4.4 0.1 broadcast_in_dim.48
  4.4 0.7 broadcast_in_dim.43
  5.1 0.7 convert_element_type.52
  5.8 0.7 convert_element_type.53
  6.5 0.1 maximum_maximum_fusion.1.cross_ref
  6.6 0.7 reshape.72
  7.3 0.1 maximum_maximum_fusion.inner_ref
  7.4 1.5 %copy.19.cell_code_ref = f32[512,1]{1,0:T(8,128)} copy(f32[512,1]{0,1:T(1,128)} %bitcast.17) | data formatting | bytes 4096 | tf_op jit(solution)/shard_map/broadcast_in_dim | solution.py:330
  8.9 3.3 %convolution_convert_fusion.1.grad_ref = bf16[512,768]{1,0:T(8,128)(2,1)} fusion(bf16[512,768]{1,0:T(8,128)(2,1)} %cotangent_ref.1, bf16[768,768]{1,0:T(8,128)(2,1)} %param.30), kind=kOutput, calls=%fused_computation.2 | convolution fusion | flops 604372992 | bytes 2752512 | tf_op jit(solution)/shard_map/dot_general | solution.py:19
  12.2 16.6 %shard_map.175 = (bf16[512,768]{1,0:T(8,128)(2,1)S(1)}, bf16[512,768]{1,0:T(8,128)(2,1)S(1)}, f32[512,1]{1,0:T(8,128)S(1)}, bf16[512,512]{1,0:T(8,128)(2,1)S(1)}...) custom-call(bf16[512,768]{1,0:T(8,128)(2,1)S(1)} %copy-done.19, ...), custom_call_target="tpu_custom_call" | custom-call | flops 3221225472 | bytes 2097152 | tf_op jit(solution)/shard_map/pallas_call | solution.py:212
  28.8 0.0 copy-start.2
  28.8 0.9 copy-done.2
  29.7 0.8 copy-done.8
  30.5 0.8 copy-done.10
  31.3 0.8 copy-done.12
  32.1 0.8 copy-done.14
  32.9 0.7 copy-done.16
  33.6 0.1 select_reduce_fusion
  33.7 0.1 reshape.73.tokens_ref
  33.8 0.1 select_n.20.dead_ref
  33.9 0.1 reshape.74.anchor_code_ref
  34.0 0.0 copy-start.21
  34.0 0.5 convolution_convert_fusion.key_ref.value_ref
  34.5 0.0 copy-done.4
  34.5 0.8 copy-done.21
  35.3 0.8 convolution_convert_fusion.2.query_ref
  36.1 0.2 copy-done.18
  36.2 0.3 copy-done.20
  36.5 5.9 %shard_map.176 = (bf16[512,768]{1,0:T(8,128)(2,1)S(1)}, bf16[512,768]{1,0:T(8,128)(2,1)S(1)}, f32[768,128]{1,0:T(8,128)S(1)}, f32[768,128]{1,0:T(8,128)S(1)}) custom-call(bf16[512,768]{1,0:T(8,128)(2,1)S(1)} %convolution_convert_fusion.2.query_ref, bf16[512,768]{1,0:T(8,128)(2,1)S(1)} %copy-done.20, ...), custom_call_target="tpu_custom_call" | custom-call | flops 1207959552 | bytes 3145728 | tf_op jit(solution)/shard_map/pallas_call | solution.py:313
  42.4 0.0 copy-start.5
  42.4 0.9 copy-done.5
  43.3 0.9 copy-done.7
  44.2 0.0 copy-done.9
  44.3 0.0 copy-start.3
  44.3 0.0 copy-start.6
  44.3 0.0 copy-start.22
  44.3 51.1 %shard_map.177 = (bf16[512,768]{1,0:T(8,128)(2,1)S(1)}, f32[192,768]{1,0:T(8,128)S(1)}) custom-call(bf16[512,768]{1,0:T(8,128)(2,1)S(1)} %copy-done.1, bf16[512,768]{1,0:T(8,128)(2,1)} %copy-done.5, bf16[512,768]{1,0:T(8,128)(2,1)} %copy-done.7, bf16[512,768]{1,0:T(8,128)(2,1)} %copy-done.4, bf16[512,768]{1,0:T(8,128)(2,1)} %copy-done.2, ...), custom_call_target="tpu_custom_call" | custom-call | tf_op jit(solution)/shard_map/pallas_call | solution.py:559
  95.4 0.0 copy-done.3
  95.4 0.0 copy-done.6
  95.5 1.7 %add_convert_fusion = bf16[512,768]{1,0:T(8,128)(2,1)} fusion(bf16[512,768]{1,0:T(8,128)(2,1)S(1)} %copy-done.3, bf16[512,768]{1,0:T(8,128)(2,1)S(1)} %copy-done.6, bf16[768,768]{1,0:T(8,128)(2,1)S(1)} %copy-done.22), kind=kOutput, calls=%fused_computation.1 | convolution fusion | flops 605159424 | bytes 3538944 | tf_op jit(solution)/shard_map/dot_general | solution.py:19
  97.1 0.9 copy.24
  98.0 0.8 copy.25
  (32 shorter events, 0.1 us)
Async XLA Ops:
  0.6 33.4 %copy-start = (bf16[768,1536]{1,0:T(8,128)(2,1)S(1)}, bf16[768,1536]{1,0:T(8,128)(2,1)}, u32[]{:S(2)}) copy-start(bf16[768,1536]{1,0:T(8,128)(2,1)} %param.29) | copy-start | bytes 7077892
  8.9 3.3 %copy-start.19 = (bf16[512,768]{1,0:T(8,128)(2,1)S(1)}, bf16[512,768]{1,0:T(8,128)(2,1)}, u32[]{:S(2)}) copy-start(bf16[512,768]{1,0:T(8,128)(2,1)} %cells_ref.1) | copy-start | bytes 2359300
  28.8 0.9 copy-start.2
  29.7 0.8 copy-start.8
  30.5 0.8 copy-start.10
  31.3 0.8 copy-start.12
  32.1 0.8 copy-start.14
  32.9 0.7 copy-start.16
  33.6 0.9 copy-start.4
  34.0 1.3 %copy-start.21 = (bf16[768,768]{1,0:T(8,128)(2,1)S(1)}, bf16[768,768]{1,0:T(8,128)(2,1)}, u32[]{:S(2)}) copy-start(bf16[768,768]{1,0:T(8,128)(2,1)} %query_matrix_ref.1) | copy-start | bytes 3538948
  35.3 0.9 copy-start.18
  35.3 1.2 %copy-start.20 = (bf16[512,768]{1,0:T(8,128)(2,1)S(1)}, bf16[512,768]{1,0:T(8,128)(2,1)}, u32[]{:S(2)}) copy-start(bf16[512,768]{1,0:T(8,128)(2,1)} %convolution_convert_fusion.1.grad_ref) | copy-start | bytes 2359300
  36.5 7.7 %copy-start.1 = (bf16[512,768]{1,0:T(8,128)(2,1)S(1)}, bf16[512,768]{1,0:T(8,128)(2,1)}, u32[]{:S(2)}) copy-start(bf16[512,768]{1,0:T(8,128)(2,1)} %cotangent_ref.1) | copy-start | bytes 2359300
  36.5 7.7 %copy-start.9 = (bf16[512,512]{1,0:T(8,128)(2,1)S(1)}, bf16[512,512]{1,0:T(8,128)(2,1)}, u32[]{:S(2)}) copy-start(bf16[512,512]{1,0:T(8,128)(2,1)} %copy-done.8) | copy-start | bytes 1572868
  36.5 7.7 %copy-start.11 = (bf16[512,512]{1,0:T(8,128)(2,1)S(1)}, bf16[512,512]{1,0:T(8,128)(2,1)}, u32[]{:S(2)}) copy-start(bf16[512,512]{1,0:T(8,128)(2,1)} %copy-done.10) | copy-start | bytes 1572868
  36.5 7.7 %copy-start.13 = (bf16[512,512]{1,0:T(8,128)(2,1)S(1)}, bf16[512,512]{1,0:T(8,128)(2,1)}, u32[]{:S(2)}) copy-start(bf16[512,512]{1,0:T(8,128)(2,1)} %copy-done.12) | copy-start | bytes 1572868
  36.5 7.7 %copy-start.15 = (bf16[512,512]{1,0:T(8,128)(2,1)S(1)}, bf16[512,512]{1,0:T(8,128)(2,1)}, u32[]{:S(2)}) copy-start(bf16[512,512]{1,0:T(8,128)(2,1)} %copy-done.14) | copy-start | bytes 1572868
  36.5 7.7 %copy-start.17 = (f32[512,1]{1,0:T(8,128)S(1)}, f32[512,1]{1,0:T(8,128)}, u32[]{:S(2)}) copy-start(f32[512,1]{1,0:T(8,128)} %copy-done.16) | copy-start | bytes 6148
  42.4 0.9 copy-start.5
  43.3 0.9 copy-start.7
  44.3 51.2 %copy-start.3 = (bf16[512,768]{1,0:T(8,128)(2,1)S(1)}, bf16[512,768]{1,0:T(8,128)(2,1)}, u32[]{:S(2)}) copy-start(bf16[512,768]{1,0:T(8,128)(2,1)} %copy-done.2) | copy-start | bytes 2359300
  44.3 51.2 %copy-start.6 = (bf16[512,768]{1,0:T(8,128)(2,1)S(1)}, bf16[512,768]{1,0:T(8,128)(2,1)}, u32[]{:S(2)}) copy-start(bf16[512,768]{1,0:T(8,128)(2,1)} %copy-done.5) | copy-start | bytes 2359300
  44.3 51.2 %copy-start.22 = (bf16[768,768]{1,0:T(8,128)(2,1)S(1)}, bf16[768,768]{1,0:T(8,128)(2,1)}, u32[]{:S(2)}) copy-start(bf16[768,768]{1,0:T(8,128)(2,1)} %param.30) | copy-start | bytes 3538948

commit v4 on v3

--- a/solution.py
+++ b/solution.py
@@ -43,6 +43,9 @@
     inner_ref,
     cross_ref,
     pack_ref,
+    cotangent_ref,
+    query_matrix_ref,
+    output_matrix_ref,
     mixed_ref,
     normed_ref,
     inverse_ref,
@@ -51,6 +54,8 @@
     cross_map_ref,
     weighted_map_ref,
     gathered_ref,
+    queries_ref,
+    grads_ref,
     own,
     peer,
     lower_live,
@@ -61,8 +66,8 @@
     face_recv,
 ):
     me = lax.axis_index("blk")
-    slots = cross_ref.shape[1] // 2
-    live_ref = cross_ref.at[:, pl.ds(0, slots)]
+    slots = cross_ref.shape[1]
+    live_ref = cross_ref
     cell_count = cells_ref.shape[0]
     barrier = pltpu.get_barrier_semaphore()
 
@@ -74,7 +79,12 @@
 
     lax.fori_loop(1, count, greet, 0)
     ids = lax.broadcasted_iota(jnp.int32, (cell_count, 2 * slots), 0)
-    cross_map = jnp.where(ids == cross_ref[...][:1].astype(jnp.int32), 1.0, 0.0)
+    cross_map = jnp.where(
+        ids
+        == jnp.concatenate([cross_ref[...][:1], cross_ref[...][1:2]], axis=1).astype(jnp.int32),
+        1.0,
+        0.0,
+    )
     cross_map_ref[...] = cross_map.astype(jnp.bfloat16)
     rows = cells_ref[...]
     chosen = contract(cross_map_ref[...], rows, 0, 0)
@@ -145,6 +155,7 @@
     inner_high_ref[...] = high_part
     inner_low_ref[...] = (-total - high_part.astype(jnp.float32)).astype(jnp.bfloat16)
     inner = contract(inner_high_ref[...], rows, 1, 0) + contract(inner_low_ref[...], rows, 1, 0)
+    grads_ref[...] = contract(cotangent_ref[...], output_matrix_ref[...], 1, 1).astype(jnp.bfloat16)
 
     @pl.when(me < count - 1)
     def _():
@@ -159,7 +170,7 @@
         down.wait_send()
 
     live = jnp.concatenate(
-        [cross_ref[...][1:2, :slots], lower_live[...][1:2]], axis=1
+        [cross_ref[...][2:3], lower_live[...][2:3]], axis=1
     )
     weighted_map_ref[...] = (cross_map_ref[...].astype(jnp.float32) * live).astype(jnp.bfloat16)
     flux = jnp.concatenate(
@@ -177,6 +188,7 @@
     inverse = lax.rsqrt(jnp.mean(mixed * mixed, axis=1, keepdims=True) + EPS)
     inverse_ref[...] = inverse
     normed_ref[...] = (mixed * inverse).astype(jnp.bfloat16)
+    queries_ref[...] = contract(normed_ref[...], query_matrix_ref[...], 1, 0).astype(jnp.bfloat16)
 
     def take_pack(step, carry):
         pack_copy(step, lax.rem(me + count - step, count)).wait_recv()
@@ -187,32 +199,25 @@
     gathered_ref[...] = landed[...]
 
 
-def front(cells, first, second, weight, cross_cells, live, pack):
+def front(
+    cells, first, second, weight, upper_cells, lower_cells, live, pack, cotangent, query_matrix, output_matrix
+):
     count = lax.axis_size("blk")
     cell_count = cells.shape[0]
     slots = live.shape[0]
-    inner_table = jnp.concatenate(
-        [
-            first.astype(jnp.float32)[None, :],
-            second.astype(jnp.float32)[None, :],
-            weight[None, :],
-            jnp.zeros((5, first.shape[0]), jnp.float32),
-        ],
-        axis=0,
-    )
-    cross_table = jnp.concatenate(
-        [
-            cross_cells.astype(jnp.float32)[None, :],
-            jnp.pad(live, (0, slots))[None, :],
-            jnp.zeros((6, 2 * slots), jnp.float32),
-        ],
-        axis=0,
-    )
+    line = lax.broadcasted_iota(jnp.int32, (8, 1), 0)
+    table = lambda one, two, three: jnp.where(
+        line == 0,
+        one.astype(jnp.float32)[None, :],
+        jnp.where(line == 1, two.astype(jnp.float32)[None, :], three[None, :]),
+    )
+    inner_table = table(first, second, weight)
+    cross_table = table(upper_cells, lower_cells, live)
     low_type = lambda *shape: jax.ShapeDtypeStruct(shape, jnp.bfloat16)
     return pl.pallas_call(
         functools.partial(front_kernel, count),
-        in_specs=[pl.BlockSpec(memory_space=pltpu.VMEM)] * 4,
-        out_specs=[pl.BlockSpec(memory_space=pltpu.VMEM)] * 8,
+        in_specs=[pl.BlockSpec(memory_space=pltpu.VMEM)] * 7,
+        out_specs=[pl.BlockSpec(memory_space=pltpu.VMEM)] * 10,
         out_shape=(
             low_type(*cells.shape),
             low_type(*cells.shape),
@@ -222,6 +227,8 @@
             low_type(cell_count, 2 * slots),
             low_type(cell_count, 2 * slots),
             low_type(count, *pack.shape),
+            low_type(*cells.shape),
+            low_type(*cells.shape),
         ),
         scratch_shapes=[
             pltpu.VMEM((2, slots, cells.shape[1]), jnp.bfloat16),
@@ -234,7 +241,7 @@
             pltpu.SemaphoreType.DMA((3,)),
         ],
         compiler_params=pltpu.CompilerParams(
-            collective_id=0, has_side_effects=True, vmem_limit_bytes=20 * MIB
+            collective_id=0, has_side_effects=True, vmem_limit_bytes=(20 if count <= 32 else 28) * MIB
         ),
         cost_estimate=pl.CostEstimate(
             flops=8 * first.shape[0] * cell_count * cell_count,
@@ -246,6 +253,9 @@
         inner_table,
         cross_table,
         pack,
+        cotangent,
+        query_matrix,
+        output_matrix,
     )
 
 
@@ -345,7 +355,9 @@
     weighted_map_ref,
     grad_key_ref,
     grad_value_ref,
+    output_matrix_ref,
     tokens_ref,
+    layer_output_ref,
     cell_grads_ref,
     weight_grads_ref,
     query_sum,
@@ -418,6 +430,13 @@
     waits += [send(0, kind, totals[kind]) for kind in range(1, 4)]
 
     grad_normed = contract(grad_query_ref[...], query_matrix_ref[...], 1, 1)
+    for stage in range(1, stages):
+        following = []
+        for kind in range(4):
+            waits[kind]()
+            following.append(send(stage, kind, totals[kind]))
+        waits = following
+
     inverse = inverse_ref[...]
     normal_hat = mixed_ref[...].astype(jnp.float32) * inverse
     grad_mixed = (
@@ -443,13 +462,6 @@
     down = sent(own.at[1], peer.at[0], 0, -1)
     up = sent(own.at[0], peer.at[1], 1, 1)
 
-    for stage in range(1, stages):
-        following = []
-        for kind in range(4):
-            waits[kind]()
-            following.append(send(stage, kind, totals[kind]))
-        waits = following
-
     @pl.when(me > 0)
     def _():
         down.start()
@@ -471,6 +483,10 @@
         + contract(inner_high_ref[...], cell_grads_ref[...], 1, 0)
         + contract(inner_low_ref[...], cell_grads_ref[...], 1, 0)
     )
+    layer_output_ref[...] = (
+        mixed_ref[...].astype(jnp.float32)
+        + contract(attended_ref[...], output_matrix_ref[...], 1, 0)
+    ).astype(jnp.bfloat16)
     for take in waits:
         take()
     wide_out, wide_in, pair_out, pair_in, last_out, last_in, last_pair_out, last_pair_in = buffers[
@@ -559,8 +575,9 @@
     return pl.pallas_call(
         functools.partial(tail_kernel, count),
         in_specs=[vmem] * len(operands),
-        out_specs=[vmem] * 2,
+        out_specs=[vmem] * 3,
         out_shape=(
+            jax.ShapeDtypeStruct(cells, jnp.bfloat16),
             jax.ShapeDtypeStruct(cells, jnp.bfloat16),
             jax.ShapeDtypeStruct((rows, MODEL_WIDTH), jnp.float32),
         ),
@@ -578,7 +595,7 @@
         ]
         + buffers,
         compiler_params=pltpu.CompilerParams(
-            collective_id=1, has_side_effects=True, vmem_limit_bytes=48 * MIB
+            collective_id=1, has_side_effects=True, vmem_limit_bytes=(24 if count <= 32 else 44) * MIB
         ),
     )(*operands)
 
@@ -616,26 +633,39 @@
         ],
         axis=1,
     )
-    mixed_rows, normed, inverse_rms, inner_high, inner_low, cross_map, weighted_map, packed = front(
+    (
+        mixed_rows,
+        normed,
+        inverse_rms,
+        inner_high,
+        inner_low,
+        cross_map,
+        weighted_map,
+        packed,
+        queries,
+        attended_gradient,
+    ) = front(
         cell_features,
         inner_face_first,
         inner_face_second,
         inner_face_weight,
-        jnp.concatenate([upper_face_cell, lower_face_cell]),
+        upper_face_cell,
+        lower_face_cell,
         live_weight,
         pack,
+        cotangent,
+        query_matrix,
+        output_matrix,
     )
     tokens = packed[:, :, :half_width].reshape(-1, MODEL_WIDTH)
     anchor_code = packed[:, :own_anchors, half_width].reshape(-1).astype(jnp.float32)
     dead = jnp.where(packed[:, own_anchors:, half_width] > 0, 0.0, -jnp.inf)
     dead = dead.reshape(-1).astype(jnp.float32)
-    queries = contract(normed, query_matrix, 1, 0).astype(jnp.bfloat16)
     keyvals = contract(tokens, anchor_keyvalue_matrix, 1, 0).astype(jnp.bfloat16)
-    attended_gradient = contract(cotangent, output_matrix, 1, 1).astype(jnp.bfloat16)
     attended, grad_queries, grad_keys, grad_values = attention(
         queries, attended_gradient, keyvals, cell_geometry_rows, anchor_code, dead
     )
-    cell_grads, weight_grads = tail(
+    layer_output, cell_grads, weight_grads = tail(
         cotangent,
         attended,
         grad_queries,
@@ -649,11 +679,9 @@
         weighted_map,
         grad_keys,
         grad_values,
+        output_matrix,
         tokens,
     )
-    layer_output = (
-        mixed_rows.astype(jnp.float32) + contract(attended, output_matrix, 1, 0)
-    ).astype(jnp.bfloat16)
     return (layer_output, cell_grads, weight_grads)
 
 

time: 99.3 us -> 98.1 us (0.988)
  matrix products: 6.19 us -> 0.48 us
  local copies, waits for them, and re-layouts: 12.9 us -> 18.4 us
  Pallas kernels: 73.6 us -> 71.2 us
  other arithmetic: 3.75 us -> 5.12 us
    unnamed x48 -> x53, local copies, waits for them, and re-layouts: 9.49 us -> 15.8 us
    dot_general x4 -> x1, matrix products: 6.19 us -> 0.48 us  [contract(): lax.dot_general(left, right, (((left_dim,), (right_dim,)), ((), ())), pre...]
    pallas_call x1, Pallas kernels: 51.1 us -> 48.8 us  [tail(): pl.pallas_call(functools.partial(tail_kernel, count), in_specs=[vmem] * l...]
    convert_element_type x3 -> x4, other arithmetic: 2.1 us -> 2.76 us  [the longest x2 1.38 us: front(): one.astype(jnp.float32)[None, :]]
where the time goes in v4:
time: 98.1 us; the launch traced here: 97.5 us
  Pallas kernels  71.2 us (73%)
  local copies, waits for them, and re-layouts  18.4 us (19%)
  other arithmetic  5.12 us (5%)
  between operations  2.32 us (2%)
    pallas_call x1, Pallas kernels, tail(): pl.pallas_call(functools.partial(tail_kernel, count), in_specs=[vmem] * l...  48.8 us
    pallas_call x1, Pallas kernels, front(): pl.pallas_call(functools.partial(front_kernel, count), in_specs=[pl.Block...  16.5 us
    unnamed x53, local copies, waits for them, and re-layouts  15.8 us
    pallas_call x1, Pallas kernels, attention(): pl.pallas_call(functools.partial(attention_kernel, 1.0 / math.sqrt(MODEL_...  5.91 us

profile of v4, /device:TPU:0, one launch (start us, length us, event | category | flops | bytes accessed | tf_op | source)
XLA Modules:
  0.0 97.5 jit_solution(14553483849319727191)
XLA Ops:
  0.6 0.0 copy-start
  2.1 0.7 pad_maximum_fusion.1
  2.8 0.7 compare_select_fusion
  3.5 0.7 convert_element_type.36
  4.2 0.7 convert_element_type.37
  4.9 0.1 broadcast_in_dim.119
  4.9 0.1 select_select_fusion.1.cross_ref
  5.0 0.7 convert_element_type.34
  5.7 0.7 convert_element_type.35
  6.4 0.7 reshape.59
  7.1 0.8 select_select_fusion.inner_ref
  7.9 1.5 %copy.19.cell_code_ref = f32[512,1]{1,0:T(8,128)} copy(f32[512,1]{0,1:T(1,128)} %bitcast.7) | data formatting | bytes 4096 | tf_op jit(solution)/shard_map/broadcast_in_dim | solution.py:340
  9.4 1.3 %copy-done.1 = bf16[768,768]{1,0:T(8,128)(2,1)S(1)} copy-done((bf16[768,768]{1,0:T(8,128)(2,1)S(1)}, bf16[768,768]{1,0:T(8,128)(2,1)}, u32[]{:S(2)}) %copy-start.1) | copy-done | bytes 1179672
  10.7 1.3 %copy-done.3 = bf16[768,768]{1,0:T(8,128)(2,1)S(1)} copy-done((bf16[768,768]{1,0:T(8,128)(2,1)S(1)}, bf16[768,768]{1,0:T(8,128)(2,1)}, u32[]{:S(2)}) %copy-start.3) | copy-done | bytes 1179672
  12.0 1.1 %copy-done.5 = bf16[512,768]{1,0:T(8,128)(2,1)S(1)} copy-done((bf16[512,768]{1,0:T(8,128)(2,1)S(1)}, bf16[512,768]{1,0:T(8,128)(2,1)}, u32[]{:S(2)}) %copy-start.5) | copy-done | bytes 786456
  13.1 1.1 %copy-done.20 = bf16[512,768]{1,0:T(8,128)(2,1)S(1)} copy-done((bf16[512,768]{1,0:T(8,128)(2,1)S(1)}, bf16[512,768]{1,0:T(8,128)(2,1)}, u32[]{:S(2)}) %copy-start.20) | copy-done | bytes 786456
  14.3 16.5 %shard_map.175 = (bf16[512,768]{1,0:T(8,128)(2,1)S(1)}, bf16[512,768]{1,0:T(8,128)(2,1)S(1)}, f32[512,1]{1,0:T(8,128)S(1)}, bf16[512,512]{1,0:T(8,128)(2,1)S(1)}...) custom-call(bf16[512,768]{1,0:T(8,128)(2,1)S(1)} %copy-done.20, ...), custom_call_target="tpu_custom_call" | custom-call | flops 3221225472 | bytes 2097152 | tf_op jit(solution)/shard_map/pallas_call | solution.py:217
  30.8 0.0 copy-start.7
  30.8 0.9 copy-done.7
  31.7 0.8 copy-done.9
  32.5 0.8 copy-done.11
  33.3 0.8 copy-done.13
  34.1 0.8 copy-done.15
  34.9 0.7 copy-done.17
  35.6 0.9 copy-done.21
  36.5 0.9 copy-done.23
  37.4 0.1 select_reduce_fusion
  37.5 0.1 reshape.60.tokens_ref
  37.6 0.1 select_n.40.dead_ref
  37.7 0.1 reshape.61.anchor_code_ref
  37.8 0.0 copy-done
  37.8 0.0 copy-start.19
  37.8 0.0 copy-start.22
  37.8 0.0 copy-start.12
  37.8 0.0 copy-start.14
  37.8 0.0 copy-start.16
  37.8 0.0 copy-start.18
  37.8 0.5 convolution_convert_fusion.key_ref.value_ref
  38.3 0.4 copy-done.19
  38.7 0.3 copy-done.22
  39.0 1.1 %copy-done.24 = bf16[512,768]{1,0:T(8,128)(2,1)S(1)} copy-done((bf16[512,768]{1,0:T(8,128)(2,1)S(1)}, bf16[512,768]{1,0:T(8,128)(2,1)}, u32[]{:S(2)}) %copy-start.24) | copy-done | bytes 786456
  40.1 0.0 copy-start.10
  40.2 5.9 %shard_map.176 = (bf16[512,768]{1,0:T(8,128)(2,1)S(1)}, bf16[512,768]{1,0:T(8,128)(2,1)S(1)}, f32[768,128]{1,0:T(8,128)S(1)}, f32[768,128]{1,0:T(8,128)S(1)}) custom-call(bf16[512,768]{1,0:T(8,128)(2,1)S(1)} %copy-done.22, bf16[512,768]{1,0:T(8,128)(2,1)S(1)} %copy-done.24, bf16[128,1536]{1,0:T(8,128)(2,1)S(1)} %convolution_convert_fusion.key_ref.value_ref, ...), custom_call_target="tpu_custom_call" | custom-call | flops 1207959552 | bytes 3145728 | tf_op jit(solution)/shard_map/pallas_call | solution.py:323
  46.1 0.0 copy-done.12
  46.2 48.8 %shard_map.177 = (bf16[512,768]{1,0:T(8,128)(2,1)S(1)}, bf16[512,768]{1,0:T(8,128)(2,1)S(1)}, f32[192,768]{1,0:T(8,128)S(1)}) custom-call(bf16[512,768]{1,0:T(8,128)(2,1)S(1)} %copy-done.6, bf16[512,768]{1,0:T(8,128)(2,1)S(1)} %get-tuple-element.20.attended_ref, bf16[512,768]{1,0:T(8,128)(2,1)S(1)} %get-tuple-element.21.grad_query_ref, ...), custom_call_target="tpu_custom_call" | custom-call | tf_op jit(solution)/shard_map/pallas_call | solution.py:575
  95.0 0.9 copy.25
  95.8 0.9 copy.26
  96.7 0.8 copy.27
  (28 shorter events, 0.1 us)
Async XLA Ops:
  0.6 37.1 %copy-start = (bf16[768,1536]{1,0:T(8,128)(2,1)S(1)}, bf16[768,1536]{1,0:T(8,128)(2,1)}, u32[]{:S(2)}) copy-start(bf16[768,1536]{1,0:T(8,128)(2,1)} %param.29) | copy-start | bytes 7077892
  9.4 1.3 %copy-start.1 = (bf16[768,768]{1,0:T(8,128)(2,1)S(1)}, bf16[768,768]{1,0:T(8,128)(2,1)}, u32[]{:S(2)}) copy-start(bf16[768,768]{1,0:T(8,128)(2,1)} %query_matrix_ref.3) | copy-start | bytes 3538948
  10.7 1.3 %copy-start.3 = (bf16[768,768]{1,0:T(8,128)(2,1)S(1)}, bf16[768,768]{1,0:T(8,128)(2,1)}, u32[]{:S(2)}) copy-start(bf16[768,768]{1,0:T(8,128)(2,1)} %output_matrix_ref.3) | copy-start | bytes 3538948
  12.0 1.1 %copy-start.5 = (bf16[512,768]{1,0:T(8,128)(2,1)S(1)}, bf16[512,768]{1,0:T(8,128)(2,1)}, u32[]{:S(2)}) copy-start(bf16[512,768]{1,0:T(8,128)(2,1)} %cotangent_ref.3) | copy-start | bytes 2359300
  13.1 1.1 %copy-start.20 = (bf16[512,768]{1,0:T(8,128)(2,1)S(1)}, bf16[512,768]{1,0:T(8,128)(2,1)}, u32[]{:S(2)}) copy-start(bf16[512,768]{1,0:T(8,128)(2,1)} %cells_ref.1) | copy-start | bytes 2359300
  30.8 0.9 copy-start.7
  31.7 0.8 copy-start.9
  32.5 0.8 copy-start.11
  33.3 0.8 copy-start.13
  34.1 0.8 copy-start.15
  34.9 0.7 copy-start.17
  35.6 0.9 copy-start.21
  36.5 0.9 copy-start.23
  37.8 1.0 copy-start.19
  37.8 1.2 %copy-start.22 = (bf16[512,768]{1,0:T(8,128)(2,1)S(1)}, bf16[512,768]{1,0:T(8,128)(2,1)}, u32[]{:S(2)}) copy-start(bf16[512,768]{1,0:T(8,128)(2,1)} %copy-done.21) | copy-start | bytes 2359300
  37.8 8.3 %copy-start.12 = (bf16[512,512]{1,0:T(8,128)(2,1)S(1)}, bf16[512,512]{1,0:T(8,128)(2,1)}, u32[]{:S(2)}) copy-start(bf16[512,512]{1,0:T(8,128)(2,1)} %copy-done.11) | copy-start | bytes 1572868
  37.8 8.3 %copy-start.14 = (bf16[512,512]{1,0:T(8,128)(2,1)S(1)}, bf16[512,512]{1,0:T(8,128)(2,1)}, u32[]{:S(2)}) copy-start(bf16[512,512]{1,0:T(8,128)(2,1)} %copy-done.13) | copy-start | bytes 1572868
  37.8 8.3 %copy-start.16 = (bf16[512,512]{1,0:T(8,128)(2,1)S(1)}, bf16[512,512]{1,0:T(8,128)(2,1)}, u32[]{:S(2)}) copy-start(bf16[512,512]{1,0:T(8,128)(2,1)} %copy-done.15) | copy-start | bytes 1572868
  37.8 8.3 %copy-start.18 = (f32[512,1]{1,0:T(8,128)S(1)}, f32[512,1]{1,0:T(8,128)}, u32[]{:S(2)}) copy-start(f32[512,1]{1,0:T(8,128)} %copy-done.17) | copy-start | bytes 6148
  39.0 1.1 %copy-start.24 = (bf16[512,768]{1,0:T(8,128)(2,1)S(1)}, bf16[512,768]{1,0:T(8,128)(2,1)}, u32[]{:S(2)}) copy-start(bf16[512,768]{1,0:T(8,128)(2,1)} %copy-done.23) | copy-start | bytes 2359300
  40.1 6.0 %copy-start.2 = (bf16[768,768]{1,0:T(8,128)(2,1)S(1)}, bf16[768,768]{1,0:T(8,128)(2,1)}, u32[]{:S(2)}) copy-start(bf16[768,768]{1,0:T(8,128)(2,1)} %query_matrix_ref.3) | copy-start | bytes 3538948
  40.1 6.0 %copy-start.4 = (bf16[768,768]{1,0:T(8,128)(2,1)S(1)}, bf16[768,768]{1,0:T(8,128)(2,1)}, u32[]{:S(2)}) copy-start(bf16[768,768]{1,0:T(8,128)(2,1)} %output_matrix_ref.3) | copy-start | bytes 3538948
  40.1 6.0 %copy-start.6 = (bf16[512,768]{1,0:T(8,128)(2,1)S(1)}, bf16[512,768]{1,0:T(8,128)(2,1)}, u32[]{:S(2)}) copy-start(bf16[512,768]{1,0:T(8,128)(2,1)} %cotangent_ref.3) | copy-start | bytes 2359300
  40.1 6.0 %copy-start.8 = (bf16[512,768]{1,0:T(8,128)(2,1)S(1)}, bf16[512,768]{1,0:T(8,128)(2,1)}, u32[]{:S(2)}) copy-start(bf16[512,768]{1,0:T(8,128)(2,1)} %copy-done.7) | copy-start | bytes 2359300
  40.1 6.0 %copy-start.10 = (bf16[512,512]{1,0:T(8,128)(2,1)S(1)}, bf16[512,512]{1,0:T(8,128)(2,1)}, u32[]{:S(2)}) copy-start(bf16[512,512]{1,0:T(8,128)(2,1)} %copy-done.9) | copy-start | bytes 1572868

commit v5 on v4

--- a/solution.py
+++ b/solution.py
@@ -41,7 +41,9 @@
     count,
     cells_ref,
     inner_ref,
+    weight_ref,
     cross_ref,
+    live_ref,
     pack_ref,
     cotangent_ref,
     query_matrix_ref,
@@ -67,7 +69,6 @@
 ):
     me = lax.axis_index("blk")
     slots = cross_ref.shape[1]
-    live_ref = cross_ref
     cell_count = cells_ref.shape[0]
     barrier = pltpu.get_barrier_semaphore()
 
@@ -81,7 +82,7 @@
     ids = lax.broadcasted_iota(jnp.int32, (cell_count, 2 * slots), 0)
     cross_map = jnp.where(
         ids
-        == jnp.concatenate([cross_ref[...][:1], cross_ref[...][1:2]], axis=1).astype(jnp.int32),
+        == jnp.concatenate([cross_ref[...][:1], cross_ref[...][1:2]], axis=1),
         1.0,
         0.0,
     )
@@ -142,8 +143,8 @@
         peer[0] = jnp.zeros(peer.shape[1:], peer.dtype)
 
     inner_rows = inner_ref[...]
-    first, second = inner_rows[:1].astype(jnp.int32), inner_rows[1:2].astype(jnp.int32)
-    weight = inner_rows[2:3]
+    first, second = inner_rows[:1], inner_rows[1:2]
+    weight = weight_ref[...]
     weight_high = weight.astype(jnp.bfloat16).astype(jnp.float32)
     weight_low = weight - weight_high
     ids = lax.broadcasted_iota(jnp.int32, (cell_count, inner_ref.shape[1]), 0)
@@ -170,7 +171,7 @@
         down.wait_send()
 
     live = jnp.concatenate(
-        [cross_ref[...][2:3], lower_live[...][2:3]], axis=1
+        [live_ref[...][:1], lower_live[...][:1]], axis=1
     )
     weighted_map_ref[...] = (cross_map_ref[...].astype(jnp.float32) * live).astype(jnp.bfloat16)
     flux = jnp.concatenate(
@@ -206,17 +207,14 @@
     cell_count = cells.shape[0]
     slots = live.shape[0]
     line = lax.broadcasted_iota(jnp.int32, (8, 1), 0)
-    table = lambda one, two, three: jnp.where(
-        line == 0,
-        one.astype(jnp.float32)[None, :],
-        jnp.where(line == 1, two.astype(jnp.float32)[None, :], three[None, :]),
-    )
-    inner_table = table(first, second, weight)
-    cross_table = table(upper_cells, lower_cells, live)
+    table = lambda one, two: jnp.where(line == 0, one[None, :], two[None, :])
+    inner_table = table(first, second)
+    cross_table = table(upper_cells, lower_cells)
+    live_table = jnp.broadcast_to(live[None, :], (8, slots))
     low_type = lambda *shape: jax.ShapeDtypeStruct(shape, jnp.bfloat16)
     return pl.pallas_call(
         functools.partial(front_kernel, count),
-        in_specs=[pl.BlockSpec(memory_space=pltpu.VMEM)] * 7,
+        in_specs=[pl.BlockSpec(memory_space=pltpu.VMEM)] * 9,
         out_specs=[pl.BlockSpec(memory_space=pltpu.VMEM)] * 10,
         out_shape=(
             low_type(*cells.shape),
@@ -251,7 +249,9 @@
     )(
         cells,
         inner_table,
+        weight[None, :],
         cross_table,
+        live_table,
         pack,
         cotangent,
         query_matrix,

time: 98.1 us -> 96.8 us (0.987)
  other arithmetic: 5.12 us -> 3.07 us
    convert_element_type x4 -> x0, other arithmetic: 2.76 us -> none  [the longest x2 1.38 us: front(): one.astype(jnp.float32)[None, :]]
where the time goes in v5:
time: 96.8 us; the launch traced here: 96.2 us
  Pallas kernels  71.3 us (74%)
  local copies, waits for them, and re-layouts  19.1 us (20%)
  other arithmetic  3.07 us (3%)
  between operations  2.32 us (2%)
    pallas_call x1, Pallas kernels, tail(): pl.pallas_call(functools.partial(tail_kernel, count), in_specs=[vmem] * l...  48.8 us
    pallas_call x1, Pallas kernels, front(): pl.pallas_call(functools.partial(front_kernel, count), in_specs=[pl.Block...  16.5 us
    unnamed x53, local copies, waits for them, and re-layouts  15.8 us
    pallas_call x1, Pallas kernels, attention(): pl.pallas_call(functools.partial(attention_kernel, 1.0 / math.sqrt(MODEL_...  5.91 us

profile of v5, /device:TPU:0, one launch (start us, length us, event | category | flops | bytes accessed | tf_op | source)
XLA Modules:
  0.0 96.2 jit_solution(173175032977332599)
XLA Ops:
  0.6 0.0 copy-start
  2.1 0.7 pad_maximum_fusion.1
  2.8 0.7 compare_select_fusion
  3.5 0.1 broadcast_in_dim.92
  3.6 0.7 broadcast_in_dim.86.weight_ref
  4.3 0.8 broadcast_select_fusion.1.cross_ref
  5.0 0.7 reshape.53
  5.8 0.8 broadcast_select_fusion.inner_ref
  6.6 1.5 %copy.19.cell_code_ref = f32[512,1]{1,0:T(8,128)} copy(f32[512,1]{0,1:T(1,128)} %bitcast.7) | data formatting | bytes 4096 | tf_op jit(solution)/shard_map/broadcast_in_dim | solution.py:340
  8.1 1.3 %copy-done.1 = bf16[768,768]{1,0:T(8,128)(2,1)S(1)} copy-done((bf16[768,768]{1,0:T(8,128)(2,1)S(1)}, bf16[768,768]{1,0:T(8,128)(2,1)}, u32[]{:S(2)}) %copy-start.1) | copy-done | bytes 1179672
  9.4 1.3 %copy-done.3 = bf16[768,768]{1,0:T(8,128)(2,1)S(1)} copy-done((bf16[768,768]{1,0:T(8,128)(2,1)S(1)}, bf16[768,768]{1,0:T(8,128)(2,1)}, u32[]{:S(2)}) %copy-start.3) | copy-done | bytes 1179672
  10.6 1.1 %copy-done.5 = bf16[512,768]{1,0:T(8,128)(2,1)S(1)} copy-done((bf16[512,768]{1,0:T(8,128)(2,1)S(1)}, bf16[512,768]{1,0:T(8,128)(2,1)}, u32[]{:S(2)}) %copy-start.5) | copy-done | bytes 786456
  11.8 1.1 %copy-done.20 = bf16[512,768]{1,0:T(8,128)(2,1)S(1)} copy-done((bf16[512,768]{1,0:T(8,128)(2,1)S(1)}, bf16[512,768]{1,0:T(8,128)(2,1)}, u32[]{:S(2)}) %copy-start.20) | copy-done | bytes 786456
  12.9 16.5 %shard_map.175 = (bf16[512,768]{1,0:T(8,128)(2,1)S(1)}, bf16[512,768]{1,0:T(8,128)(2,1)S(1)}, f32[512,1]{1,0:T(8,128)S(1)}, bf16[512,512]{1,0:T(8,128)(2,1)S(1)}...) custom-call(bf16[512,768]{1,0:T(8,128)(2,1)S(1)} %copy-done.20, ...), custom_call_target="tpu_custom_call" | custom-call | flops 3221225472 | bytes 2097152 | tf_op jit(solution)/shard_map/pallas_call | solution.py:215
  29.5 0.0 copy-start.7
  29.5 0.9 copy-done.7
  30.4 0.8 copy-done.9
  31.1 0.8 copy-done.11
  32.0 0.8 copy-done.13
  32.8 0.8 copy-done.15
  33.6 0.7 copy-done.17
  34.3 0.9 copy-done.21
  35.2 0.9 copy-done.23
  36.0 0.1 select_reduce_fusion
  36.2 0.1 reshape.54.tokens_ref
  36.3 0.1 select_n.30.dead_ref
  36.3 0.1 reshape.55.anchor_code_ref
  36.4 0.0 copy-done
  36.5 0.0 copy-start.22
  36.5 0.5 convolution_convert_fusion.key_ref.value_ref
  37.0 0.4 copy-done.19
  37.4 0.3 copy-done.22
  37.7 1.1 %copy-done.24 = bf16[512,768]{1,0:T(8,128)(2,1)S(1)} copy-done((bf16[512,768]{1,0:T(8,128)(2,1)S(1)}, bf16[512,768]{1,0:T(8,128)(2,1)}, u32[]{:S(2)}) %copy-start.24) | copy-done | bytes 786456
  38.8 0.0 copy-start.10
  38.8 5.9 %shard_map.176 = (bf16[512,768]{1,0:T(8,128)(2,1)S(1)}, bf16[512,768]{1,0:T(8,128)(2,1)S(1)}, f32[768,128]{1,0:T(8,128)S(1)}, f32[768,128]{1,0:T(8,128)S(1)}) custom-call(bf16[512,768]{1,0:T(8,128)(2,1)S(1)} %copy-done.22, bf16[512,768]{1,0:T(8,128)(2,1)S(1)} %copy-done.24, bf16[128,1536]{1,0:T(8,128)(2,1)S(1)} %convolution_convert_fusion.key_ref.value_ref, ...), custom_call_target="tpu_custom_call" | custom-call | flops 1207959552 | bytes 3145728 | tf_op jit(solution)/shard_map/pallas_call | solution.py:323
  44.7 0.0 copy-done.12
  44.7 0.0 copy-done.14
  44.8 0.0 copy-done.16
  44.8 0.0 copy-done.18
  44.8 0.0 copy-done.2
  44.8 0.0 copy-done.4
  44.8 0.0 copy-done.6
  44.8 0.0 copy-done.8
  44.8 0.0 copy-done.10
  44.8 48.8 %shard_map.177 = (bf16[512,768]{1,0:T(8,128)(2,1)S(1)}, bf16[512,768]{1,0:T(8,128)(2,1)S(1)}, f32[192,768]{1,0:T(8,128)S(1)}) custom-call(bf16[512,768]{1,0:T(8,128)(2,1)S(1)} %copy-done.6, bf16[512,768]{1,0:T(8,128)(2,1)S(1)} %get-tuple-element.20.attended_ref, bf16[512,768]{1,0:T(8,128)(2,1)S(1)} %get-tuple-element.21.grad_query_ref, ...), custom_call_target="tpu_custom_call" | custom-call | tf_op jit(solution)/shard_map/pallas_call | solution.py:575
  93.6 0.9 copy.25
  94.5 0.9 copy.26
  95.4 0.8 copy.27
  (26 shorter events, 0.1 us)
Async XLA Ops:
  0.6 35.8 %copy-start = (bf16[768,1536]{1,0:T(8,128)(2,1)S(1)}, bf16[768,1536]{1,0:T(8,128)(2,1)}, u32[]{:S(2)}) copy-start(bf16[768,1536]{1,0:T(8,128)(2,1)} %param.29) | copy-start | bytes 7077892
  8.1 1.3 %copy-start.1 = (bf16[768,768]{1,0:T(8,128)(2,1)S(1)}, bf16[768,768]{1,0:T(8,128)(2,1)}, u32[]{:S(2)}) copy-start(bf16[768,768]{1,0:T(8,128)(2,1)} %query_matrix_ref.3) | copy-start | bytes 3538948
  9.4 1.3 %copy-start.3 = (bf16[768,768]{1,0:T(8,128)(2,1)S(1)}, bf16[768,768]{1,0:T(8,128)(2,1)}, u32[]{:S(2)}) copy-start(bf16[768,768]{1,0:T(8,128)(2,1)} %output_matrix_ref.3) | copy-start | bytes 3538948
  10.6 1.1 %copy-start.5 = (bf16[512,768]{1,0:T(8,128)(2,1)S(1)}, bf16[512,768]{1,0:T(8,128)(2,1)}, u32[]{:S(2)}) copy-start(bf16[512,768]{1,0:T(8,128)(2,1)} %cotangent_ref.3) | copy-start | bytes 2359300
  11.8 1.1 %copy-start.20 = (bf16[512,768]{1,0:T(8,128)(2,1)S(1)}, bf16[512,768]{1,0:T(8,128)(2,1)}, u32[]{:S(2)}) copy-start(bf16[512,768]{1,0:T(8,128)(2,1)} %cells_ref.1) | copy-start | bytes 2359300
  29.5 0.9 copy-start.7
  30.4 0.8 copy-start.9
  31.1 0.8 copy-start.11
  32.0 0.8 copy-start.13
  32.8 0.8 copy-start.15
  33.6 0.7 copy-start.17
  34.3 0.9 copy-start.21
  35.2 0.9 copy-start.23
  36.4 1.0 copy-start.19
  36.5 1.2 %copy-start.22 = (bf16[512,768]{1,0:T(8,128)(2,1)S(1)}, bf16[512,768]{1,0:T(8,128)(2,1)}, u32[]{:S(2)}) copy-start(bf16[512,768]{1,0:T(8,128)(2,1)} %copy-done.21) | copy-start | bytes 2359300
  36.5 8.3 %copy-start.12 = (bf16[512,512]{1,0:T(8,128)(2,1)S(1)}, bf16[512,512]{1,0:T(8,128)(2,1)}, u32[]{:S(2)}) copy-start(bf16[512,512]{1,0:T(8,128)(2,1)} %copy-done.11) | copy-start | bytes 1572868
  36.5 8.3 %copy-start.14 = (bf16[512,512]{1,0:T(8,128)(2,1)S(1)}, bf16[512,512]{1,0:T(8,128)(2,1)}, u32[]{:S(2)}) copy-start(bf16[512,512]{1,0:T(8,128)(2,1)} %copy-done.13) | copy-start | bytes 1572868
  36.5 8.3 %copy-start.16 = (bf16[512,512]{1,0:T(8,128)(2,1)S(1)}, bf16[512,512]{1,0:T(8,128)(2,1)}, u32[]{:S(2)}) copy-start(bf16[512,512]{1,0:T(8,128)(2,1)} %copy-done.15) | copy-start | bytes 1572868
  36.5 8.3 %copy-start.18 = (f32[512,1]{1,0:T(8,128)S(1)}, f32[512,1]{1,0:T(8,128)}, u32[]{:S(2)}) copy-start(f32[512,1]{1,0:T(8,128)} %copy-done.17) | copy-start | bytes 6148
  37.7 1.1 %copy-start.24 = (bf16[512,768]{1,0:T(8,128)(2,1)S(1)}, bf16[512,768]{1,0:T(8,128)(2,1)}, u32[]{:S(2)}) copy-start(bf16[512,768]{1,0:T(8,128)(2,1)} %copy-done.23) | copy-start | bytes 2359300
  38.8 6.0 %copy-start.2 = (bf16[768,768]{1,0:T(8,128)(2,1)S(1)}, bf16[768,768]{1,0:T(8,128)(2,1)}, u32[]{:S(2)}) copy-start(bf16[768,768]{1,0:T(8,128)(2,1)} %query_matrix_ref.3) | copy-start | bytes 3538948
  38.8 6.0 %copy-start.4 = (bf16[768,768]{1,0:T(8,128)(2,1)S(1)}, bf16[768,768]{1,0:T(8,128)(2,1)}, u32[]{:S(2)}) copy-start(bf16[768,768]{1,0:T(8,128)(2,1)} %output_matrix_ref.3) | copy-start | bytes 3538948
  38.8 6.0 %copy-start.6 = (bf16[512,768]{1,0:T(8,128)(2,1)S(1)}, bf16[512,768]{1,0:T(8,128)(2,1)}, u32[]{:S(2)}) copy-start(bf16[512,768]{1,0:T(8,128)(2,1)} %cotangent_ref.3) | copy-start | bytes 2359300
  38.8 6.0 %copy-start.8 = (bf16[512,768]{1,0:T(8,128)(2,1)S(1)}, bf16[512,768]{1,0:T(8,128)(2,1)}, u32[]{:S(2)}) copy-start(bf16[512,768]{1,0:T(8,128)(2,1)} %copy-done.7) | copy-start | bytes 2359300
  38.8 6.0 %copy-start.10 = (bf16[512,512]{1,0:T(8,128)(2,1)S(1)}, bf16[512,512]{1,0:T(8,128)(2,1)}, u32[]{:S(2)}) copy-start(bf16[512,512]{1,0:T(8,128)(2,1)} %copy-done.9) | copy-start | bytes 1572868
